TPU v7x, 256 devices: a whole 4x4x8 slice. The times are simulated.
256 devices in a mesh: ctx: 32 (over z, y), head: 8 (over x, core).
Axes of the slice: x: 4, y: 4, z: 8, core: 2. Of those that a mesh axis runs over, the one named last changes fastest.
Arguments:
- inputs: bfloat16 [6144, 4096], P('ctx', 'head'), may hold values from -6 to 6
- key_weight: bfloat16 [4096, 8192], P(None, 'head'), may hold values from -0.09375 to 0.09375
- beta_weight: bfloat16 [4096, 64], P(None, 'head'), may hold values from -0.09375 to 0.09375
- beta_bias: float32 [64], P('head'), may hold values from -3.6 to 2
- queries: bfloat16 [6144, 4096], P('ctx', 'head'), may hold values from -0.5390625 to 0.5390625
- values: bfloat16 [6144, 8192], P('ctx', 'head'), may hold values from -6 to 6
- out_grad: bfloat16 [6144, 4096], P('ctx', 'head'), may hold values from -6 to 6
Outputs:
- mixed: bfloat16 [6144, 4096], P('ctx', 'head')
- query_grad: bfloat16 [6144, 4096], P('ctx', 'head')
- value_grad: bfloat16 [6144, 8192], P('ctx', 'head')
- input_grad: bfloat16 [6144, 4096], P('ctx', 'head')
All inputs are finite; a program needn't handle non-finite values.
Results may differ from a plain program's by a relative error of at most 0.005.
Values may be sent and summed in bfloat16 or wider, within the bound.
No kernel may reach another device: no remote copies, remote signals or barrier semaphores. Data moves between devices by JAX's collectives and lax.ppermute only.
A program may use at most 192 MiB of HBM per device.

v0:
```python
import jax
import jax.numpy as jnp
from jax import lax
from jax.sharding import PartitionSpec as P

maximal_precision = lax.Precision.HIGHEST
block_limit = 128


def passed_along(shard, axis, by):
    count = lax.axis_size(axis)
    pairs = [(i, i + by) for i in range(count) if 0 <= i + by < count]
    return lax.ppermute(shard, axis, pairs)


def batched(left, right):
    return jnp.einsum("hij,hjk->hik", left, right, precision=maximal_precision)


def block_parts(segment_key_rows, block_values, block_rates, segment_query_rows):
    span_len = segment_key_rows.shape[1]
    feature_len = segment_key_rows.shape[2]
    scaled_keys = segment_key_rows * block_rates[..., None]
    segment_crossings = jnp.einsum(
        "hid,hjd->hij", scaled_keys, segment_key_rows, precision=maximal_precision
    )
    triangle = jnp.tril(segment_crossings, -1) + jnp.eye(span_len, dtype=segment_crossings.dtype)
    targets = jnp.concatenate([scaled_keys, block_values * block_rates[..., None]], axis=2)
    solved = jax.scipy.linalg.solve_triangular(triangle, targets, lower=True, unit_diagonal=True)
    key_mix = solved[..., :feature_len]
    value_mix = solved[..., feature_len:]
    attention_scores = jnp.einsum(
        "pfe,pge->pfg", segment_query_rows, segment_key_rows, precision=maximal_precision
    )
    visible = jnp.arange(span_len)[None, :] <= 2 * jnp.arange(span_len // 2)[:, None] + 1
    attention_scores = jnp.where(visible[None], attention_scores, 0.0)
    return (key_mix, value_mix, attention_scores)


def arrange(query_data, key_proj, value_data, logits):
    row_count = query_data.shape[0]
    head_count = logits.shape[1] // 2
    feature_len = query_data.shape[1] // head_count
    shaped = key_proj.reshape(row_count, head_count, 2, feature_len)
    unit_keys = shaped / jnp.sqrt(jnp.sum(shaped * shaped, axis=3, keepdims=True) + 1e-06)
    span_len = min(block_limit, 2 * row_count)
    block_total = 2 * row_count // span_len
    key_seq = jnp.transpose(unit_keys, (1, 0, 2, 3)).reshape(
        head_count, block_total, span_len, feature_len
    )
    value_seq = jnp.transpose(
        value_data.reshape(row_count, head_count, 2, feature_len), (1, 0, 2, 3)
    )
    value_seq = value_seq.reshape(head_count, block_total, span_len, feature_len)
    rate_seq = jnp.transpose(
        (2.0 * jax.nn.sigmoid(logits)).reshape(row_count, head_count, 2), (1, 0, 2)
    )
    rate_seq = rate_seq.reshape(head_count, block_total, span_len)
    query_seq = jnp.transpose(query_data.reshape(row_count, head_count, feature_len), (1, 0, 2))
    query_seq = query_seq.reshape(head_count, block_total, span_len // 2, feature_len)
    return tuple(
        (jnp.moveaxis(member, 1, 0) for member in (key_seq, value_seq, rate_seq, query_seq))
    )


def split_heads(stacked):
    block_total, head_count, half_span, feature_len = stacked.shape
    return jnp.transpose(stacked, (1, 0, 2, 3)).reshape(
        head_count, block_total * half_span, feature_len
    )


def local_span(query_data, key_proj, value_data, logits):
    sequences = arrange(query_data, key_proj, value_data, logits)
    head_count = logits.shape[1] // 2
    feature_len = query_data.shape[1] // head_count

    def advance(carry, block):
        trans_acc, state_running_total = carry
        segment_key_rows, block_values, block_rates, segment_query_rows = block
        key_mix, value_mix, attention_scores = block_parts(
            segment_key_rows, block_values, block_rates, segment_query_rows
        )
        residue = value_mix - batched(key_mix, state_running_total)
        reach = batched(segment_query_rows - batched(attention_scores, key_mix), trans_acc)
        emitted = batched(segment_query_rows, state_running_total) + batched(
            attention_scores, residue
        )
        trans_acc = trans_acc - jnp.einsum(
            "hcd,hce->hde",
            segment_key_rows,
            batched(key_mix, trans_acc),
            precision=maximal_precision,
        )
        state_running_total = state_running_total + jnp.einsum(
            "hcd,hce->hde", segment_key_rows, residue, precision=maximal_precision
        )
        return ((trans_acc, state_running_total), (reach, emitted))

    identity = jnp.broadcast_to(
        jnp.eye(feature_len, dtype=jnp.float32), (head_count, feature_len, feature_len)
    )
    empty_state = jnp.zeros((head_count, feature_len, feature_len), jnp.float32)
    (transition, offset), (reach, emitted) = lax.scan(advance, (identity, empty_state), sequences)
    return (transition, offset, split_heads(reach), split_heads(emitted))


def per_device(inputs, key_weight, beta_weight, beta_bias, queries, values, out_grad):
    row_count = inputs.shape[0]
    piece = lax.all_gather(inputs, "head", axis=1, tiled=True)
    key_proj = jnp.dot(piece, key_weight, preferred_element_type=jnp.float32)
    logits = jnp.dot(piece, beta_weight, preferred_element_type=jnp.float32)
    logits = logits + beta_bias
    (transition, offset, reach, emitted), pullback = jax.vjp(
        local_span, queries.astype(jnp.float32), key_proj, values.astype(jnp.float32), logits
    )
    head_count, feature_len = (transition.shape[0], transition.shape[1])
    cotangent = jnp.transpose(
        out_grad.astype(jnp.float32).reshape(row_count, head_count, feature_len), (1, 0, 2)
    )
    local_grad = jnp.einsum("hld,hle->hde", reach, cotangent, precision=maximal_precision)
    flipped = jnp.swapaxes(transition, 1, 2)
    empty_state = jnp.zeros((head_count, feature_len, feature_len), jnp.float32)

    def turn(turn_index, carried):
        incoming, returning = carried
        incoming = passed_along(batched(transition, incoming) + offset, "ctx", 1)
        returning = passed_along(local_grad + batched(flipped, returning), "ctx", -1)
        return (incoming, returning)

    incoming, returning = lax.fori_loop(
        0, lax.axis_size("ctx") - 1, turn, (empty_state, empty_state)
    )
    mixed_full = emitted + batched(reach, incoming)
    reach_gradient = jnp.einsum("hle,hde->hld", cotangent, incoming, precision=maximal_precision)
    transition_cot = jnp.einsum("hde,hfe->hdf", returning, incoming, precision=maximal_precision)
    query_cot, key_cot, value_cot, logit_cot = pullback(
        (transition_cot, returning, reach_gradient, cotangent)
    )
    contract = (((1,), (1,)), ((), ()))
    partial_grad = lax.dot_general(
        key_cot.astype(jnp.bfloat16), key_weight, contract, preferred_element_type=jnp.float32
    )
    partial_grad = partial_grad + lax.dot_general(
        logit_cot.astype(jnp.bfloat16), beta_weight, contract, preferred_element_type=jnp.float32
    )
    input_grad = lax.psum_scatter(partial_grad, "head", scatter_dimension=1, tiled=True).astype(
        jnp.bfloat16
    )
    mixed = jnp.transpose(mixed_full, (1, 0, 2)).reshape(row_count, head_count * feature_len)
    return (
        mixed.astype(jnp.bfloat16),
        query_cot.astype(jnp.bfloat16),
        value_cot.astype(jnp.bfloat16),
        input_grad,
    )


def solution(mesh):
    placed = (
        P("ctx", "head"),
        P(None, "head"),
        P(None, "head"),
        P("head"),
        P("ctx", "head"),
        P("ctx", "head"),
        P("ctx", "head"),
    )
    return jax.shard_map(
        per_device,
        mesh=mesh,
        in_specs=placed,
        out_specs=(P("ctx", "head"), P("ctx", "head"), P("ctx", "head"), P("ctx", "head")),
        check_vma=False,
    )
```

profile of v0, /device:TPU:1, one launch (start us, length us, event | category | flops | bytes accessed | tf_op | source)
XLA Modules:
  0.0 986.5 jit_solution(9836314191757356723)
XLA Ops:
  13.1 27.8 %all-gather.2.cloned.1.call-done = bf16[192,4096]{1,0:T(8,128)(2,1)} async-done(((bf16[192,512]{1,0:T(8,128)(2,1)}), bf16[192,4096]{1,0:T(8,128)(2,1)}) %all-gather.2.cloned.1.call-update) | async-done | bytes 1572880 | tf_op jit(solution)/shard_map/all_gather | solution.py:110
  41.0 5.7 fusion.177
  51.3 164.8 %while.87 = (s32[]{:T(128)}, f32[4,128,128]{2,1,0:T(8,128)S(1)}, f32[4,128,128]{2,1,0:T(8,128)S(1)}, f32[3,4,64,128]{3,2,0,1:T(8,128)}, f32[3,4,64,128]{3,2,1,0:...) while((s32[]{:T(128)}, f32[4,128,128]{2,1,0:T(8,128)S(1)}, ...), condition=%wide.region_2.3_spmd.clone.clone, body=%wide.region_1.2_spmd.clone.sunk.clone | while | flops 957530240 | bytes 14495466 | solution.py:104
  54.2 39.9 %custom-call.44 = f32[4,1,128,128]{2,3,1,0:T(8,128)} custom-call(f32[4,1,128,128]{3,2,1,0:T(8,128)S(1)} %add_bitcast_fusion.7), custom_call_target="InvertDiagBlocksLowerTriangular" | custom-call | tf_op jit(solution)/shard_map/jvp()/while/body/eval_jaxpr/jit(_solve_triangular)/vmap()/triangular_solve | solution.py:29
  109.1 39.9 %custom-call.44 = f32[4,1,128,128]{2,3,1,0:T(8,128)} custom-call(f32[4,1,128,128]{3,2,1,0:T(8,128)S(1)} %add_bitcast_fusion.7), custom_call_target="InvertDiagBlocksLowerTriangular" | custom-call | tf_op jit(solution)/shard_map/jvp()/while/body/eval_jaxpr/jit(_solve_triangular)/vmap()/triangular_solve | solution.py:29
  163.9 39.9 %custom-call.44 = f32[4,1,128,128]{2,3,1,0:T(8,128)} custom-call(f32[4,1,128,128]{3,2,1,0:T(8,128)S(1)} %add_bitcast_fusion.7), custom_call_target="InvertDiagBlocksLowerTriangular" | custom-call | tf_op jit(solution)/shard_map/jvp()/while/body/eval_jaxpr/jit(_solve_triangular)/vmap()/triangular_solve | solution.py:29
  218.0 460.0 %while.85 = (s32[]{:T(128)}, f32[4,128,128]{2,1,0:T(8,128)S(1)}, f32[4,128,128]{2,1,0:T(8,128)S(1)}, f32[4,128,128]{2,1,0:T(8,128)S(1)}, f32[4,128,128]{2,1,0:T(...) while((s32[]{:T(128)}, f32[4,128,128]{2,1,0:T(8,128)S(1)}, ...), condition=%wide.region_4.5_spmd.clone, body=%wide.region_3.4_spmd.sunk.clone | while | flops 201457664 | bytes 4194461 | solution.py:131
  379.3 5.4 collective-permute-done.1
  395.5 5.4 collective-permute-done.1
  448.8 5.7 collective-permute-start
  493.5 5.5 collective-permute-start
  508.7 5.8 collective-permute-start
  524.0 5.5 collective-permute-start
  552.8 5.5 collective-permute-start
  567.8 5.5 collective-permute-start
  582.8 5.5 collective-permute-start
  598.0 5.4 collective-permute-start
  608.6 5.4 collective-permute-done.1
  680.0 196.8 %while.86 = (s32[]{:T(128)}, f32[4,128,128]{2,1,0:T(8,128)S(1)}, f32[4,128,128]{2,1,0:T(8,128)S(1)}, f32[3,4,128,128]{3,2,0,1:T(8,128)}, bf16[3,4,128,128]{3,2,0...) while((s32[]{:T(128)}, f32[4,128,128]{2,1,0:T(8,128)S(1)}, ...), condition=%wide.region_8.9_spmd.clone.clone.clone, body=%wide.region_5.8_spmd.clone.clone.sunk.clone | while | flops 2015542912 | bytes 40981088 | solution.py:104
  690.4 40.1 %custom-call.43 = f32[4,1,128,128]{2,3,1,0:T(8,128)S(1)} custom-call(f32[4,1,128,128]{3,2,1,0:T(8,128)} %add_bitcast_fusion.6), custom_call_target="InvertDiagBlocksLowerTriangular" | custom-call | tf_op jit(solution)/shard_map/transpose(jvp())/while/body/eval_jaxpr/jit(_solve_triangular)/vmap()/triangular_solve | solution.py:29
  755.9 40.1 %custom-call.43 = f32[4,1,128,128]{2,3,1,0:T(8,128)S(1)} custom-call(f32[4,1,128,128]{3,2,1,0:T(8,128)} %add_bitcast_fusion.6), custom_call_target="InvertDiagBlocksLowerTriangular" | custom-call | tf_op jit(solution)/shard_map/transpose(jvp())/while/body/eval_jaxpr/jit(_solve_triangular)/vmap()/triangular_solve | solution.py:29
  821.5 40.1 %custom-call.43 = f32[4,1,128,128]{2,3,1,0:T(8,128)S(1)} custom-call(f32[4,1,128,128]{3,2,1,0:T(8,128)} %add_bitcast_fusion.6), custom_call_target="InvertDiagBlocksLowerTriangular" | custom-call | tf_op jit(solution)/shard_map/transpose(jvp())/while/body/eval_jaxpr/jit(_solve_triangular)/vmap()/triangular_solve | solution.py:29
  881.4 6.4 fusion.179
  894.9 83.0 %reduce-scatter.2.cloned.1.call-done = f32[192,512]{1,0:T(8,128)} async-done(((f32[192,4096]{1,0:T(8,128)}), f32[192,512]{1,0:T(8,128)}) %reduce-scatter.2.cloned.1.call-update) | async-done | bytes 393232 | tf_op jit(solution)/shard_map/reduce_scatter | solution.py:147
  (499 shorter events, 546.1 us)
Async XLA Ops:
  7.2 33.8 %all-gather.2.cloned.1.call-start = ((), (), s32[]{:S(2)}) async-start(), calls=%async_computation.1 | async-start | bytes 1769472 | tf_op jit(solution)/shard_map/all_gather | solution.py:110
  7.9 970.0 %reduce-scatter.2.cloned.1.call-start = ((), (), s32[]{:S(2)}) async-start(), calls=%async_computation.2 | async-start | bytes 3538944 | tf_op jit(solution)/shard_map/reduce_scatter | solution.py:147
  219.1 9.0 collective-permute-start
  223.5 9.4 collective-permute-start.1
  375.6 9.1 collective-permute-start.1
  385.7 9.7 collective-permute-start
  390.7 10.1 %collective-permute-start.1 = (f32[4,128,128]{2,1,0:T(8,128)}, f32[4,128,128]{2,1,0:T(8,128)S(1)}, u32[]{:S(2)}, u32[]{:S(2)}) collective-permute-start(f32[4,128,128]{2,1,0:T(8,128)} %convolution_add_fusion.48), channel_id=1, source_target_pairs={{8,0},{16,8},{24,16},{32,24},{40,32},{48,40},{56,48},{64,56},{72,6... | collective-permute-start | bytes 786440 | tf_op jit(solution)/shard_map/while/body/eval_jaxpr/ppermute | solution.py:13
  401.9 10.6 %collective-permute-start = (f32[4,128,128]{2,1,0:T(8,128)}, f32[4,128,128]{2,1,0:T(8,128)S(1)}, u32[]{:S(2)}, u32[]{:S(2)}) collective-permute-start(f32[4,128,128]{2,1,0:T(8,128)} %convolution_add_fusion.47), channel_id=1, source_target_pairs={{0,8},{8,16},{16,24},{24,32},{32,40},{40,48},{48,56},{56,64},{64,7... | collective-permute-start | bytes 786440 | tf_op jit(solution)/shard_map/while/body/eval_jaxpr/ppermute | solution.py:13
  407.8 9.9 collective-permute-start.1
  418.7 9.8 collective-permute-start
  448.8 9.3 collective-permute-start
  493.5 9.1 collective-permute-start
  508.7 9.4 collective-permute-start
  524.0 9.1 collective-permute-start
  552.8 9.1 collective-permute-start
  567.8 9.1 collective-permute-start
  582.8 9.1 collective-permute-start
  598.0 10.5 %collective-permute-start = (f32[4,128,128]{2,1,0:T(8,128)}, f32[4,128,128]{2,1,0:T(8,128)S(1)}, u32[]{:S(2)}, u32[]{:S(2)}) collective-permute-start(f32[4,128,128]{2,1,0:T(8,128)} %convolution_add_fusion.47), channel_id=1, source_target_pairs={{0,8},{8,16},{16,24},{24,32},{32,40},{40,48},{48,56},{56,64},{64,7... | collective-permute-start | bytes 786440 | tf_op jit(solution)/shard_map/while/body/eval_jaxpr/ppermute | solution.py:13
  604.6 9.4 collective-permute-start.1
  615.0 11.3 %collective-permute-start = (f32[4,128,128]{2,1,0:T(8,128)}, f32[4,128,128]{2,1,0:T(8,128)S(1)}, u32[]{:S(2)}, u32[]{:S(2)}) collective-permute-start(f32[4,128,128]{2,1,0:T(8,128)} %convolution_add_fusion.47), channel_id=1, source_target_pairs={{0,8},{8,16},{16,24},{24,32},{32,40},{40,48},{48,56},{56,64},{64,7... | collective-permute-start | bytes 786440 | tf_op jit(solution)/shard_map/while/body/eval_jaxpr/ppermute | solution.py:13
  621.1 10.5 %collective-permute-start.1 = (f32[4,128,128]{2,1,0:T(8,128)}, f32[4,128,128]{2,1,0:T(8,128)S(1)}, u32[]{:S(2)}, u32[]{:S(2)}) collective-permute-start(f32[4,128,128]{2,1,0:T(8,128)} %convolution_add_fusion.48), channel_id=1, source_target_pairs={{8,0},{16,8},{24,16},{32,24},{40,32},{48,40},{56,48},{64,56},{72,6... | collective-permute-start | bytes 786440 | tf_op jit(solution)/shard_map/while/body/eval_jaxpr/ppermute | solution.py:13
  632.8 10.1 %collective-permute-start = (f32[4,128,128]{2,1,0:T(8,128)}, f32[4,128,128]{2,1,0:T(8,128)S(1)}, u32[]{:S(2)}, u32[]{:S(2)}) collective-permute-start(f32[4,128,128]{2,1,0:T(8,128)} %convolution_add_fusion.47), channel_id=1, source_target_pairs={{0,8},{8,16},{16,24},{24,32},{32,40},{40,48},{48,56},{56,64},{64,7... | collective-permute-start | bytes 786440 | tf_op jit(solution)/shard_map/while/body/eval_jaxpr/ppermute | solution.py:13
  638.4 9.6 collective-permute-start.1
  649.1 9.7 collective-permute-start
  (89 other events, 438.9 us)
Sparse Core Ops, SparseCore 0:
  9.9 31.0 all-gather.1
  891.4 86.5 reduce-scatter.1
where the time goes:
time: 991 us; the launch traced here: 986 us
  waiting for transfers between devices  319 us (32%)
  other arithmetic  263 us (27%)
  matrix products  188 us (19%)
  starting transfers between devices  183 us (18%)
  local copies, waits for them, and re-layouts  15.7 us (2%)
  between operations  14.6 us (1%)
    another operation x27, other arithmetic, block_parts(): jax.scipy.linalg.solve_triangular(triangle, targets, lower=True, unit_dia...  246 us
    ppermute x62, waiting for transfers between devices, passed_along(): return lax.ppermute(shard, axis, pairs)  208 us
    ppermute x62, starting transfers between devices, passed_along(): return lax.ppermute(shard, axis, pairs)  183 us
    dot_general x117, matrix products, batched(): return jnp.einsum('hij,hjk->hik', left, right, precision=maximal_precision)  122 us
    reduce_scatter x1, waiting for transfers between devices, per_device(): lax.psum_scatter(partial_grad, 'head', scatter_dimension=1, tiled=True)  83 us
    all_gather x1, waiting for transfers between devices, per_device(): piece = lax.all_gather(inputs, 'head', axis=1, tiled=True)  27.8 us
  transfers between devices with their start and end apart: 64, of which 64 were waited for; matrix products, arithmetic and copies ran while one was open for 4% of the time, Pallas kernels for 0%

commit v1 on v0

v1 whole, which is shorter than its diff:
```python
import functools

import jax
import jax.numpy as jnp
from jax import lax
from jax.experimental import pallas as pl
from jax.experimental.pallas import tpu as pltpu
from jax.sharding import PartitionSpec as P

F32 = jnp.float32
BF16 = jnp.bfloat16
SPAN = 64
CTX_INNER = 4
VMEM_BYTES = 48 * 1024 * 1024


def product(left, right, over_left=1, over_right=0):
    return lax.dot_general(
        left,
        right,
        (((over_left,), (over_right,)), ((), ())),
        preferred_element_type=F32,
    )


def halves(value):
    if isinstance(value, tuple):
        return value
    if value.dtype == BF16:
        return (value, None)
    high = value.astype(BF16)
    return (high, (value - high.astype(F32)).astype(BF16))


def fine(left, right, over_left=1, over_right=0):
    left_high, left_low = halves(left)
    right_high, right_low = halves(right)
    total = product(left_high, right_high, over_left, over_right)
    if left_low is not None:
        total = total + product(left_low, right_high, over_left, over_right)
    if right_low is not None:
        total = total + product(left_high, right_low, over_left, over_right)
    return total


def block_times(axis, shape):
    index = lax.broadcasted_iota(jnp.int32, shape, axis)
    return 2 * lax.rem(index, SPAN) + lax.div(index, SPAN)


def key_masks():
    shape = (2 * SPAN, 2 * SPAN)
    later, earlier = block_times(0, shape), block_times(1, shape)
    levels = []
    for level in range((2 * SPAN).bit_length() - 1):
        later_half, earlier_half = later >> level, earlier >> level
        levels.append(
            ((later_half >> 1) == (earlier_half >> 1)) & (later_half > earlier_half)
        )
    return later > earlier, levels


def query_mask():
    shape = (SPAN, 2 * SPAN)
    return block_times(1, shape) <= 2 * lax.broadcasted_iota(jnp.int32, shape, 0) + 1


def unit_rows(rows):
    inverse = lax.rsqrt(jnp.sum(rows * rows, axis=1, keepdims=True) + 1e-06)
    return rows * inverse, inverse


def local_blocks(key_rows, rates, values, queries, cotangents):
    count = len(key_rows)
    each = range(count)
    _, levels = key_masks()
    visible = query_mask()
    keys = [unit_rows(key_rows[i])[0] for i in each]
    key_halves = [halves(keys[i]) for i in each]
    crossings = [rates[i] * fine(key_halves[i], key_halves[i], 1, 1) for i in each]
    row, column = block_times(0, crossings[0].shape), block_times(1, crossings[0].shape)
    one = jnp.where(row == column, 1.0, 0.0)
    solver = [one - jnp.where(levels[0], crossings[i], 0.0) for i in each]
    for level in levels[1:]:
        parts = [halves(solver[i]) for i in each]
        step = [fine(jnp.where(level, crossings[i], 0.0), parts[i]) for i in each]
        solver = [solver[i] - fine(parts[i], step[i]) for i in each]
    parts = [halves(solver[i]) for i in each]
    targets = [
        jnp.concatenate([rates[i] * keys[i], rates[i] * values[i].astype(F32)], axis=1)
        for i in each
    ]
    mixes = [fine(parts[i], targets[i]) for i in each]
    scores = [jnp.where(visible, fine(queries[i], key_halves[i], 1, 1), 0.0) for i in each]
    moves = [fine(key_halves[i], mixes[i], 0, 0) for i in each]
    width = keys[0].shape[1]
    diagonal = lax.broadcasted_iota(jnp.int32, (width, width), 0) == lax.broadcasted_iota(
        jnp.int32, (width, width), 1
    )
    transitions = [jnp.where(diagonal, 1.0, 0.0) - moves[i][:, :width] for i in each]
    offsets = [moves[i][:, width:] for i in each]
    early = [fine(scores[i], cotangents[i], 0, 0) for i in each]
    pulls = [
        fine(queries[i], cotangents[i], 0, 0) - fine(mixes[i][:, :width], early[i], 0, 0)
        for i in each
    ]
    return solver, mixes, scores, early, transitions, offsets, pulls


def chained(transitions, offsets, pulls):
    transition, offset = transitions[0], offsets[0]
    pull = pulls[-1]
    for later in range(1, len(transitions)):
        parts = halves(transitions[later])
        transition, offset = (
            fine(parts, transition),
            fine(parts, offset) + offsets[later],
        )
        earlier = len(transitions) - 1 - later
        pull = pulls[earlier] + fine(transitions[earlier], pull, 0, 0)
    return transition, offset, pull


def entered(transitions, offsets, pulls, state, returning):
    count = len(transitions)
    states, returned = [state], [returning]
    for i in range(count - 1):
        states.append(fine(transitions[i], states[-1]) + offsets[i])
        back = count - 1 - i
        returned.append(fine(transitions[back], returned[-1], 0, 0) + pulls[back])
    return states, returned[::-1]


def full_blocks(
    key_rows, rates, values, queries, cotangents, solver, mixes, scores, early, states, returning
):
    each = range(len(key_rows))
    causal, _ = key_masks()
    visible = query_mask()
    width = key_rows[0].shape[1]
    normal = [unit_rows(key_rows[i]) for i in each]
    keys = [normal[i][0] for i in each]
    key_halves = [halves(keys[i]) for i in each]
    state_halves = [halves(states[i]) for i in each]
    returning_halves = [halves(returning[i]) for i in each]
    residues = [mixes[i][:, width:] - fine(mixes[i][:, :width], state_halves[i]) for i in each]
    residue_halves = [halves(residues[i]) for i in each]
    residue_cots = [early[i] + fine(key_halves[i], returning_halves[i]) for i in each]
    mixed = [
        fine(queries[i], state_halves[i]) + fine(scores[i], residue_halves[i]) for i in each
    ]
    pushes = [fine(solver[i], residue_cots[i], 0, 0) for i in each]
    score_cots = [
        halves(jnp.where(visible, fine(cotangents[i], residue_halves[i], 1, 1), 0.0))
        for i in each
    ]
    query_cots = [
        fine(cotangents[i], state_halves[i], 1, 1) + fine(score_cots[i], key_halves[i])
        for i in each
    ]
    ratings = [rates[i] * pushes[i] for i in each]
    rating_halves = [halves(ratings[i]) for i in each]
    links = [
        halves(jnp.where(causal, fine(rating_halves[i], residue_halves[i], 1, 1), 0.0))
        for i in each
    ]
    key_cots = [
        fine(score_cots[i], queries[i], 0, 0)
        + fine(residue_halves[i], returning_halves[i], 1, 1)
        - fine(rating_halves[i], state_halves[i], 1, 1)
        - fine(links[i], key_halves[i])
        - fine(links[i], key_halves[i], 0, 0)
        for i in each
    ]
    logit_cots = [
        jnp.sum(pushes[i] * residues[i], axis=1, keepdims=True) * (1.0 - 0.5 * rates[i])
        for i in each
    ]
    key_row_cots = [
        normal[i][1]
        * (key_cots[i] - keys[i] * jnp.sum(keys[i] * key_cots[i], axis=1, keepdims=True))
        for i in each
    ]
    return mixed, query_cots, ratings, key_row_cots, logit_cots


def block_rows(ref, count):
    return [ref[i * SPAN : (i + 1) * SPAN, :] for i in range(count)]


def paired(rows, width):
    return jnp.concatenate([rows[:, :width], rows[:, width:]], axis=0)


def unpaired(rows):
    return jnp.concatenate([rows[:SPAN], rows[SPAN:]], axis=1)


def head_rates(logits, head):
    lane = lax.broadcasted_iota(jnp.int32, logits.shape, 1)
    rates = [
        2.0
        * jax.nn.sigmoid(
            jnp.sum(jnp.where(lane == 2 * head + key, logits, 0.0), axis=1, keepdims=True)
        )
        for key in range(2)
    ]
    blocks = logits.shape[0] // SPAN
    return [
        jnp.concatenate([rate[i * SPAN : (i + 1) * SPAN] for rate in rates], axis=0)
        for i in range(blocks)
    ]


def project_kernel(shifts, *refs):
    pieces = refs[: len(shifts)]
    (key_weight, beta_weight, beta_bias, queries, values, out_grad) = refs[
        len(shifts) : len(shifts) + 6
    ]
    (key_proj, logits, solver, mixes, scores, early, moves, whole) = refs[len(shifts) + 6 :]
    head = pl.program_id(0)
    depth = pieces[0].shape[1]
    width = queries.shape[1]
    blocks = queries.shape[0] // SPAN
    owners = [owner_of(lax.axis_index("head"), shift) for shift in shifts]
    starts = [pl.multiple_of(owner * depth, depth) for owner in owners]

    @pl.when(head == 0)
    def _():
        total = beta_bias[...]
        for piece, start in zip(pieces, starts):
            total = total + product(piece[...], beta_weight[:, pl.ds(start, depth)], 1, 1)
        logits[...] = total

    total = product(pieces[0][...], key_weight[pl.ds(starts[0], depth), :])
    for piece, start in zip(pieces[1:], starts[1:]):
        total = total + product(piece[...], key_weight[pl.ds(start, depth), :])
    key_proj[...] = total

    found = local_blocks(
        [paired(rows, width) for rows in block_rows(key_proj, blocks)],
        head_rates(logits[...], head),
        [paired(rows, width) for rows in block_rows(values, blocks)],
        block_rows(queries, blocks),
        block_rows(out_grad, blocks),
    )
    for ref, arrays in zip((solver, mixes, scores, early), found[:4]):
        for i in range(blocks):
            ref[0, i] = arrays[i]
    for position, arrays in enumerate(found[4:]):
        for i in range(blocks):
            moves[0, position, i] = arrays[i]
    for position, array in enumerate(chained(*found[4:])):
        whole[0, position] = array


def group_kernel(spans, whole):
    count = spans.shape[0]
    found = chained(*[[spans[i, part] for i in range(count)] for part in range(3)])
    for part in range(3):
        whole[part] = found[part]


def scan_kernel(group_count, inner, *refs):
    spans, groups, entering = refs[0], refs[1:-1], refs[-1]
    position = lax.div(lax.axis_index("ctx"), inner)
    width = spans.shape[2]
    state = jnp.zeros((width, width), F32)
    returning = jnp.zeros((width, width), F32)
    for step in range(1, group_count):
        before = groups[group_count - step - 1]
        there = group_count - step <= position
        moved = fine(before[0], state) + before[1]
        state = jnp.where(there, moved, state)
        after = groups[step - 1]
        there = position - step < 0
        moved = fine(after[0], returning, 0, 0) + after[2]
        returning = jnp.where(there, moved, returning)
    count = spans.shape[0]
    states, returned = entered(
        *[[spans[i, part] for i in range(count)] for part in range(3)], state, returning
    )
    for i in range(count):
        entering[i, 0] = states[i]
        entering[i, 1] = returned[i]


def outputs_kernel(*refs):
    (key_proj, logits, queries, values, out_grad, solver, mixes, scores, early, moves) = refs[:10]
    (entering, mixed, query_grad, value_grad, key_cot, logit_cot, logit_total) = refs[10:]
    head = pl.program_id(0)
    width = queries.shape[1]
    blocks = queries.shape[0] // SPAN
    each = range(blocks)
    rates = head_rates(logits[...], head)
    states, returning = entered(
        *[[moves[0, part, i] for i in each] for part in range(3)], entering[0, 0], entering[0, 1]
    )
    found = full_blocks(
        [paired(rows, width) for rows in block_rows(key_proj, blocks)],
        rates,
        [paired(rows, width) for rows in block_rows(values, blocks)],
        block_rows(queries, blocks),
        block_rows(out_grad, blocks),
        [solver[0, i] for i in each],
        [mixes[0, i] for i in each],
        [scores[0, i] for i in each],
        [early[0, i] for i in each],
        states,
        returning,
    )
    lane = lax.broadcasted_iota(jnp.int32, (SPAN, logits.shape[1]), 1)

    @pl.when(head == 0)
    def _():
        logit_total[...] = jnp.zeros_like(logit_total)

    for i in each:
        rows = slice(i * SPAN, (i + 1) * SPAN)
        mixed[rows, :] = found[0][i].astype(BF16)
        query_grad[rows, :] = found[1][i].astype(BF16)
        value_grad[rows, :] = unpaired(found[2][i]).astype(BF16)
        key_cot[rows, :] = unpaired(found[3][i]).astype(BF16)
        logit_total[rows, :] += jnp.where(
            lane == 2 * head, found[4][i][:SPAN], 0.0
        ) + jnp.where(lane == 2 * head + 1, found[4][i][SPAN:], 0.0)
    logit_cot[...] = logit_total[...].astype(BF16)


def share_kernel(key_cot, logit_cot, key_weight, beta_weight, *refs):
    total = product(key_cot[...], key_weight[...], 1, 1)
    total = total + product(logit_cot[...], beta_weight[...])
    output = refs[-1]
    if len(refs) > 1:
        total = total + refs[0][0].astype(F32)
    output[0] = total.astype(output.dtype)


def owner_of(index, shift):
    chips = lax.axis_size("head") // 2
    chip, core = lax.div(index, 2), lax.rem(index, 2)
    return 2 * lax.rem(chip + shift[0], chips) + lax.rem(core + shift[1], 2)


def head_permute(value, chip_shift, core_shift):
    count = lax.axis_size("head")
    chips = count // 2
    pairs = []
    for target in range(count):
        source = 2 * ((target // 2 + chip_shift) % chips) + (target % 2 + core_shift) % 2
        pairs.append((source, target))
    return lax.ppermute(value, "head", pairs)


def ctx_permute(value, outer_shift, inner_shift):
    count = lax.axis_size("ctx")
    outer = count // CTX_INNER
    pairs = []
    for target in range(count):
        source = (target // CTX_INNER + outer_shift) % outer * CTX_INNER
        source += (target % CTX_INNER + inner_shift) % CTX_INNER
        pairs.append((source, target))
    return lax.ppermute(value, "ctx", pairs)


def params(*semantics):
    return pltpu.CompilerParams(vmem_limit_bytes=VMEM_BYTES, dimension_semantics=semantics)


def shape_of(*shape, dtype=F32):
    return jax.ShapeDtypeStruct(shape, dtype)


def per_device(inputs, key_weight, beta_weight, beta_bias, queries, values, out_grad):
    rows, depth = inputs.shape
    heads = beta_bias.shape[0] // 2
    width = queries.shape[1] // heads
    blocks = rows // SPAN
    keys = 2 * SPAN
    chips = lax.axis_size("head") // 2
    inner = CTX_INNER
    outer = lax.axis_size("ctx") // inner

    shifts = [(0, 0), (0, 1)]
    pieces = [inputs, head_permute(inputs, 0, 1)]
    for chip in range(1, chips):
        piece = head_permute(inputs, chip, 0)
        shifts += [(chip, 0), (chip, 1)]
        pieces += [piece, head_permute(piece, 0, 1)]
    beta_across = jnp.swapaxes(beta_weight, 0, 1)

    whole_spec = lambda *shape: pl.BlockSpec(shape, lambda h: (0,) * len(shape))
    column_spec = lambda n: pl.BlockSpec((rows, n), lambda h: (0, h))
    head_spec = lambda *shape: pl.BlockSpec((1, *shape), lambda h: (h,) + (0,) * len(shape))
    found = pl.pallas_call(
        functools.partial(project_kernel, shifts),
        grid=(heads,),
        in_specs=[whole_spec(rows, depth)] * len(pieces)
        + [
            pl.BlockSpec((key_weight.shape[0], 2 * width), lambda h: (0, h)),
            whole_spec(*beta_across.shape),
            whole_spec(1, 2 * heads),
            column_spec(width),
            column_spec(2 * width),
            column_spec(width),
        ],
        out_specs=[
            column_spec(2 * width),
            whole_spec(rows, 2 * heads),
            head_spec(blocks, keys, keys),
            head_spec(blocks, keys, 2 * width),
            head_spec(blocks, SPAN, keys),
            head_spec(blocks, keys, width),
            head_spec(3, blocks, width, width),
            head_spec(3, width, width),
        ],
        out_shape=[
            shape_of(rows, 2 * heads * width),
            shape_of(rows, 2 * heads),
            shape_of(heads, blocks, keys, keys),
            shape_of(heads, blocks, keys, 2 * width),
            shape_of(heads, blocks, SPAN, keys),
            shape_of(heads, blocks, keys, width),
            shape_of(heads, 3, blocks, width, width),
            shape_of(heads, 3, width, width),
        ],
        compiler_params=params("arbitrary"),
        name="project",
    )(*pieces, key_weight, beta_across, beta_bias[None], queries, values, out_grad)
    key_proj, logits, solver, mixes, scores, early, moves, whole = found

    place = lax.rem(lax.axis_index("ctx"), inner)

    def swap_inner(stacked):
        arrived = [lax.dynamic_index_in_dim(stacked, place, 0, keepdims=False)]
        for shift in range(1, inner):
            wanted = lax.rem(place + inner - shift, inner)
            sent = lax.dynamic_index_in_dim(stacked, wanted, 0, keepdims=False)
            arrived.append(ctx_permute(sent, 0, shift))
        return jnp.stack(
            [
                lax.select_n(
                    lax.rem(slot - place + inner, inner),
                    *arrived,
                )
                for slot in range(inner)
            ]
        )

    spans = swap_inner(whole)
    group = pl.pallas_call(
        group_kernel,
        out_shape=shape_of(3, width, width),
        compiler_params=params(),
        name="group",
    )(spans)
    others = [ctx_permute(group, outer - shift, 0) for shift in range(1, outer)]
    entering = pl.pallas_call(
        functools.partial(scan_kernel, outer, inner),
        out_shape=shape_of(inner, 2, width, width),
        compiler_params=params(),
        name="scan",
    )(spans, *others)
    entering = swap_inner(entering)

    mixed, query_grad, value_grad, key_cot, logit_cot = pl.pallas_call(
        outputs_kernel,
        grid=(heads,),
        in_specs=[
            column_spec(2 * width),
            whole_spec(rows, 2 * heads),
            column_spec(width),
            column_spec(2 * width),
            column_spec(width),
            head_spec(blocks, keys, keys),
            head_spec(blocks, keys, 2 * width),
            head_spec(blocks, SPAN, keys),
            head_spec(blocks, keys, width),
            head_spec(3, blocks, width, width),
            head_spec(2, width, width),
        ],
        out_specs=[
            column_spec(width),
            column_spec(width),
            column_spec(2 * width),
            column_spec(2 * width),
            whole_spec(rows, 2 * heads),
        ],
        out_shape=[
            shape_of(rows, heads * width, dtype=BF16),
            shape_of(rows, heads * width, dtype=BF16),
            shape_of(rows, 2 * heads * width, dtype=BF16),
            shape_of(rows, 2 * heads * width, dtype=BF16),
            shape_of(rows, 2 * heads, dtype=BF16),
        ],
        scratch_shapes=[pltpu.VMEM((rows, 2 * heads), F32)],
        compiler_params=params("arbitrary"),
        name="outputs",
    )(key_proj, logits, queries, values, out_grad, solver, mixes, scores, early, moves, entering)

    me = lax.axis_index("head")

    def shares(core_shift, dtype, *more):
        order = jnp.stack([owner_of(me, (chip, core_shift)) for chip in range(chips)])
        slot = pl.BlockSpec((1, rows, depth), lambda d, order: (d, 0, 0))
        return pl.pallas_call(
            lambda order, *refs: share_kernel(*refs),
            grid_spec=pltpu.PrefetchScalarGridSpec(
                num_scalar_prefetch=1,
                grid=(chips,),
                in_specs=[
                    pl.BlockSpec(key_cot.shape, lambda d, order: (0, 0)),
                    pl.BlockSpec(logit_cot.shape, lambda d, order: (0, 0)),
                    pl.BlockSpec((depth, key_weight.shape[1]), lambda d, order: (order[d], 0)),
                    pl.BlockSpec((2 * heads, depth), lambda d, order: (0, order[d])),
                ]
                + [slot] * len(more),
                out_specs=slot,
            ),
            out_shape=shape_of(chips, rows, depth, dtype=dtype),
            compiler_params=params("arbitrary"),
            name="shares",
        )(order, key_cot, logit_cot, key_weight, beta_across, *more)

    away = head_permute(shares(1, BF16), 0, 1)
    own = shares(0, F32, away)
    total = own[0]
    for chip in range(1, chips):
        total = total + head_permute(own[chip].astype(BF16), chips - chip, 0).astype(F32)
    return mixed, query_grad, value_grad, total.astype(BF16)


def solution(mesh):
    placed = (
        P("ctx", "head"),
        P(None, "head"),
        P(None, "head"),
        P("head"),
        P("ctx", "head"),
        P("ctx", "head"),
        P("ctx", "head"),
    )
    return jax.shard_map(
        per_device,
        mesh=mesh,
        in_specs=placed,
        out_specs=(P("ctx", "head"), P("ctx", "head"), P("ctx", "head"), P("ctx", "head")),
        check_vma=False,
    )
```

time: 991 us -> 165 us (0.17)
  other arithmetic: 263 us -> 2.32 us
  waiting for transfers between devices: 319 us -> 61.6 us
  matrix products: 188 us -> 0 us
  starting transfers between devices: 183 us -> 41.1 us
  Pallas kernels: 0 us -> 43.5 us
  between operations: 14.6 us -> 0.83 us
    another operation x39 -> x7, other arithmetic: 246 us -> 1.54 us  [the longest x4 1.29 us: swap_inner(): jnp.stack([lax.select_n(lax.rem(slot - place + inner, inner), *arrived) f...]
    dot_general x163 -> x0, matrix products: 178 us -> none  [the longest x117 122 us: batched(): return jnp.einsum('hij,hjk->hik', left, right, precision=maximal_precision)]
    ppermute x62 -> x24, waiting for transfers between devices: 208 us -> 61.6 us  [the longest x13 41.7 us: ctx_permute(): return lax.ppermute(value, 'ctx', pairs)]
    ppermute x62 -> x24, starting transfers between devices: 183 us -> 41.1 us  [the longest x13 26.3 us: ctx_permute(): return lax.ppermute(value, 'ctx', pairs)]
    reduce_scatter x1 -> x0, waiting for transfers between devices: 83 us -> none  [per_device(): lax.psum_scatter(partial_grad, 'head', scatter_dimension=1, tiled=True)]
    pallas_call x0 -> x6, Pallas kernels: none -> 43.5 us  [the longest x1 21.6 us: per_device(): pl.pallas_call(functools.partial(project_kernel, shifts), grid=(heads,),...]
    all_gather x1 -> x0, waiting for transfers between devices: 27.8 us -> none  [per_device(): piece = lax.all_gather(inputs, 'head', axis=1, tiled=True)]
    another operation x9 -> x0, matrix products: 10.1 us -> none  [block_parts(): jax.scipy.linalg.solve_triangular(triangle, targets, lower=True, unit_dia...]
  transfers between devices with their start and end apart: 64 -> 24, of which waited for: 64 -> 17; matrix products, arithmetic and copies ran while one was open for 4% -> 0% of each run, Pallas kernels for 0% -> 0%
where the time goes in v1:
time: 165 us; the launch traced here: 163 us
  waiting for transfers between devices  61.6 us (37%)
  Pallas kernels  43.5 us (26%)
  starting transfers between devices  41.1 us (25%)
  local copies, waits for them, and re-layouts  13.3 us (8%)
  other arithmetic  2.32 us (1%)
    ppermute x13, waiting for transfers between devices, ctx_permute(): return lax.ppermute(value, 'ctx', pairs)  41.7 us
    ppermute x13, starting transfers between devices, ctx_permute(): return lax.ppermute(value, 'ctx', pairs)  26.3 us
    pallas_call x1, Pallas kernels, per_device(): pl.pallas_call(functools.partial(project_kernel, shifts), grid=(heads,),...  21.6 us
    ppermute x11, waiting for transfers between devices, head_permute(): return lax.ppermute(value, 'head', pairs)  20 us
    ppermute x11, starting transfers between devices, head_permute(): return lax.ppermute(value, 'head', pairs)  14.9 us
    unnamed x42, local copies, waits for them, and re-layouts  12.5 us
    pallas_call x1, Pallas kernels, per_device(): pl.pallas_call(outputs_kernel, grid=(heads,), in_specs=[column_spec(2 * w...  10.1 us
    pallas_call x2, Pallas kernels, shares(): pl.pallas_call(lambda order, *refs: share_kernel(*refs), grid_spec=pltpu....  9.37 us
  transfers between devices with their start and end apart: 24, of which 17 were waited for; matrix products, arithmetic and copies ran while one was open for 0% of the time, Pallas kernels for 0%

profile of v1, /device:TPU:1, one launch (start us, length us, event | category | flops | bytes accessed | tf_op | source)
XLA Modules:
  0.0 162.7 jit_solution(8049861856903025107)
XLA Ops:
  0.6 3.4 %collective-permute-start.1 = (bf16[192,512]{1,0:T(8,128)(2,1)}, bf16[192,512]{1,0:T(8,128)(2,1)S(1)}, u32[]{:S(2)}, u32[]{:S(2)}) collective-permute-start(bf16[192,512]{1,0:T(8,128)(2,1)} %refs_0_.1), channel_id=1, source_target_pairs={{2,0},{3,1},{4,2},{5,3},{6,4},{7,5},{0,6},{1,7},{10,8},{11,9},{12,... | collective-permute-start | bytes 589832 | tf_op jit(solution)/shard_map/ppermute | solution.py:352
  6.7 3.4 %collective-permute-done.1.refs_2_ = bf16[192,512]{1,0:T(8,128)(2,1)S(1)} collective-permute-done((bf16[192,512]{1,0:T(8,128)(2,1)}, bf16[192,512]{1,0:T(8,128)(2,1)S(1)}, u32[]{:S(2)}, u32[]{:S(2)}) %collective-permute-start.1) | collective-permute-done | bytes 196640 | tf_op jit(solution)/shard_map/ppermute | solution.py:352
  10.1 3.6 %collective-permute-start.2 = (bf16[192,512]{1,0:T(8,128)(2,1)S(1)}, bf16[192,512]{1,0:T(8,128)(2,1)S(1)}, u32[]{:S(2)}, u32[]{:S(2)}) collective-permute-start(bf16[192,512]{1,0:T(8,128)(2,1)S(1)} %collective-permute-done.1.refs_2_), channel_id=1, source_target_pairs={{1,0},{0,1},{3,2},{2,3},{5,4},{4,5},{7,6},{6,7},{9,8},{8,9},{11,10... | collective-permute-start | bytes 589832 | tf_op jit(solution)/shard_map/ppermute | solution.py:352
  14.6 2.2 %collective-permute-done.5.refs_6_ = bf16[192,512]{1,0:T(8,128)(2,1)S(1)} collective-permute-done((bf16[192,512]{1,0:T(8,128)(2,1)}, bf16[192,512]{1,0:T(8,128)(2,1)S(1)}, u32[]{:S(2)}, u32[]{:S(2)}) %collective-permute-start.5) | collective-permute-done | bytes 196640 | tf_op jit(solution)/shard_map/ppermute | solution.py:352
  23.6 21.6 %project.1 = (f32[192,1024]{1,0:T(8,128)S(1)}, f32[192,8]{1,0:T(8,128)S(1)}, f32[4,3,128,128]{3,2,1,0:T(8,128)S(1)}, f32[4,3,128,256]{3,2,1,0:T(8,128)}, f32[4,3...) custom-call(bf16[192,512]{1,0:T(8,128)(2,1)S(1)} %copy-done.17, ...), custom_call_target="tpu_custom_call" | custom-call | tf_op jit(solution)/shard_map/project/pallas_call | solution.py:395
  47.7 2.8 %collective-permute-start.7 = (f32[3,128,128]{2,1,0:T(8,128)S(1)}, f32[3,128,128]{2,1,0:T(8,128)S(1)}, u32[]{:S(2)}, u32[]{:S(2)}) collective-permute-start(f32[3,128,128]{2,1,0:T(8,128)S(1)} %get-tuple-element.43), channel_id=1, source_target_pairs={{8,0},{16,8},{24,16},{0,24},{40,32},{48,40},{56,48},{32,56},{72,64... | collective-permute-start | bytes 589832 | tf_op jit(solution)/shard_map/ppermute | solution.py:363
  51.5 6.9 %collective-permute-done.7 = f32[3,128,128]{2,1,0:T(8,128)S(1)} collective-permute-done((f32[3,128,128]{2,1,0:T(8,128)S(1)}, f32[3,128,128]{2,1,0:T(8,128)S(1)}, u32[]{:S(2)}, u32[]{:S(2)}) %collective-permute-start.7) | collective-permute-done | bytes 196640 | tf_op jit(solution)/shard_map/ppermute | solution.py:363
  58.5 4.6 %collective-permute-done.9 = f32[3,128,128]{2,1,0:T(8,128)S(1)} collective-permute-done((f32[3,128,128]{2,1,0:T(8,128)S(1)}, f32[3,128,128]{2,1,0:T(8,128)S(1)}, u32[]{:S(2)}, u32[]{:S(2)}) %collective-permute-start.9) | collective-permute-done | bytes 196640 | tf_op jit(solution)/shard_map/ppermute | solution.py:363
  65.5 3.0 %collective-permute-start.11 = (f32[3,128,128]{2,1,0:T(8,128)S(1)}, f32[3,128,128]{2,1,0:T(8,128)S(1)}, u32[]{:S(2)}, u32[]{:S(2)}) collective-permute-start(f32[3,128,128]{2,1,0:T(8,128)S(1)} %group.1), channel_id=1, source_target_pairs={{192,0},{200,8},{208,16},{216,24},{224,32},{232,40},{240,48},{248,... | collective-permute-start | bytes 589832 | tf_op jit(solution)/shard_map/ppermute | solution.py:363
  68.5 3.8 %collective-permute-start.12 = (f32[3,128,128]{2,1,0:T(8,128)S(1)}, f32[3,128,128]{2,1,0:T(8,128)S(1)}, u32[]{:S(2)}, u32[]{:S(2)}) collective-permute-start(f32[3,128,128]{2,1,0:T(8,128)S(1)} %group.1), channel_id=1, source_target_pairs={{160,0},{168,8},{176,16},{184,24},{192,32},{200,40},{208,48},{216,... | collective-permute-start | bytes 589832 | tf_op jit(solution)/shard_map/ppermute | solution.py:363
  72.8 4.4 %collective-permute-start.14 = (f32[3,128,128]{2,1,0:T(8,128)S(1)}, f32[3,128,128]{2,1,0:T(8,128)S(1)}, u32[]{:S(2)}, u32[]{:S(2)}) collective-permute-start(f32[3,128,128]{2,1,0:T(8,128)S(1)} %group.1), channel_id=1, source_target_pairs={{96,0},{104,8},{112,16},{120,24},{128,32},{136,40},{144,48},{152,5... | collective-permute-start | bytes 589832 | tf_op jit(solution)/shard_map/ppermute | solution.py:363
  77.2 2.4 %collective-permute-start.15 = (f32[3,128,128]{2,1,0:T(8,128)S(1)}, f32[3,128,128]{2,1,0:T(8,128)S(1)}, u32[]{:S(2)}, u32[]{:S(2)}) collective-permute-start(f32[3,128,128]{2,1,0:T(8,128)S(1)} %group.1), channel_id=1, source_target_pairs={{64,0},{72,8},{80,16},{88,24},{96,32},{104,40},{112,48},{120,56},{... | collective-permute-start | bytes 589832 | tf_op jit(solution)/shard_map/ppermute | solution.py:363
  80.1 5.2 %collective-permute-start.16 = (f32[3,128,128]{2,1,0:T(8,128)S(1)}, f32[3,128,128]{2,1,0:T(8,128)S(1)}, u32[]{:S(2)}, u32[]{:S(2)}) collective-permute-start(f32[3,128,128]{2,1,0:T(8,128)S(1)} %group.1), channel_id=1, source_target_pairs={{32,0},{40,8},{48,16},{56,24},{64,32},{72,40},{80,48},{88,56},{96,... | collective-permute-start | bytes 589832 | tf_op jit(solution)/shard_map/ppermute | solution.py:363
  85.3 9.4 %collective-permute-done.12.refs_3_ = f32[3,128,128]{2,1,0:T(8,128)S(1)} collective-permute-done((f32[3,128,128]{2,1,0:T(8,128)S(1)}, f32[3,128,128]{2,1,0:T(8,128)S(1)}, u32[]{:S(2)}, u32[]{:S(2)}) %collective-permute-start.12) | collective-permute-done | bytes 196640 | tf_op jit(solution)/shard_map/ppermute | solution.py:363
  94.7 4.6 %collective-permute-done.13.refs_4_ = f32[3,128,128]{2,1,0:T(8,128)S(1)} collective-permute-done((f32[3,128,128]{2,1,0:T(8,128)S(1)}, f32[3,128,128]{2,1,0:T(8,128)S(1)}, u32[]{:S(2)}, u32[]{:S(2)}) %collective-permute-start.13) | collective-permute-done | bytes 196640 | tf_op jit(solution)/shard_map/ppermute | solution.py:363
  99.3 7.8 %collective-permute-done.15.refs_6_ = f32[3,128,128]{2,1,0:T(8,128)S(1)} collective-permute-done((f32[3,128,128]{2,1,0:T(8,128)S(1)}, f32[3,128,128]{2,1,0:T(8,128)S(1)}, u32[]{:S(2)}, u32[]{:S(2)}) %collective-permute-start.15) | collective-permute-done | bytes 196640 | tf_op jit(solution)/shard_map/ppermute | solution.py:363
  112.3 2.6 %collective-permute-done.17 = f32[2,128,128]{2,1,0:T(8,128)} collective-permute-done((f32[2,128,128]{2,1,0:T(8,128)}, f32[2,128,128]{2,1,0:T(8,128)}, u32[]{:S(2)}, u32[]{:S(2)}) %collective-permute-start.17) | collective-permute-done | bytes 131104 | tf_op jit(solution)/shard_map/ppermute | solution.py:363
  116.4 2.6 %collective-permute-done.19 = f32[2,128,128]{2,1,0:T(8,128)} collective-permute-done((f32[2,128,128]{2,1,0:T(8,128)}, f32[2,128,128]{2,1,0:T(8,128)}, u32[]{:S(2)}, u32[]{:S(2)}) %collective-permute-start.19) | collective-permute-done | bytes 131104 | tf_op jit(solution)/shard_map/ppermute | solution.py:363
  124.2 10.1 %outputs.1 = (bf16[192,512]{1,0:T(8,128)(2,1)}, bf16[192,512]{1,0:T(8,128)(2,1)}, bf16[192,1024]{1,0:T(8,128)(2,1)}, bf16[192,1024]{1,0:T(8,128)(2,1)S(1)}, bf16[192,8]{1,0:T(8,128)(2,1)S(1)}) custom-call(f32[192,1024]{1,0:T(8,128)S(1)} %get-tuple-element.17.refs_0_, f32[192,8]{1,0:T(8,128)S(1)} %copy-done.19, bf16[192,512]{1,0:T(8,128)(2,1)S(1)} %copy-done.8, ...), custom_call_target="tpu_custom_call" | custom-call | tf_op jit(solution)/shard_map/outputs/pallas_call | solution.py:466
  134.3 4.7 %shares.2 = bf16[4,192,512]{2,1,0:T(8,128)(2,1)S(1)} custom-call(s32[4]{0:T(128)S(1)} %pad_add_fusion.1.order, bf16[192,1024]{1,0:T(8,128)(2,1)S(1)} %get-tuple-element.28.refs_0_, bf16[192,8]{1,0:T(8,128)(2,1)S(1)} %get-tuple-element.29.refs_1_, bf16[4096,1024]{1,0:T(8,128)(2,1)} %refs_2_.5, bf16[8,4096]{1,0:T(8,128)(2,1)S(1)} %bitcast.97), custom_call_target="tpu_custom_call" | custom-call | tf_op jit(solution)/shard_map/shares/pallas_call | solution.py:506
  139.0 2.3 %collective-permute-start.20 = (bf16[4,192,512]{2,1,0:T(8,128)(2,1)S(1)}, bf16[4,192,512]{2,1,0:T(8,128)(2,1)S(1)}, u32[]{:S(2)}, u32[]{:S(2)}) collective-permute-start(bf16[4,192,512]{2,1,0:T(8,128)(2,1)S(1)} %shares.2), channel_id=1, source_target_pairs={{1,0},{0,1},{3,2},{2,3},{5,4},{4,5},{7,6},{6,7},{9,8},{8,9},{11,10... | collective-permute-start | bytes 2359304 | tf_op jit(solution)/shard_map/ppermute | solution.py:352
  144.0 4.7 %shares.3 = f32[4,192,512]{2,1,0:T(8,128)S(1)} custom-call(s32[4]{0:T(128)S(1)} %pad_add_fusion.order, bf16[192,1024]{1,0:T(8,128)(2,1)S(1)} %get-tuple-element.28.refs_0_, bf16[192,8]{1,0:T(8,128)(2,1)S(1)} %copy-done.16, bf16[4096,1024]{1,0:T(8,128)(2,1)} %refs_2_.5, bf16[8,4096]{1,0:T(8,128)(2,1)S(1)} %bitcast.98, ...), custom_call_target="tpu_custom_call" | custom-call | tf_op jit(solution)/shard_map/shares/pallas_call | solution.py:506
  150.4 4.6 %collective-permute-done.23 = bf16[192,512]{1,0:T(8,128)(2,1)S(1)} collective-permute-done((bf16[192,512]{1,0:T(8,128)(2,1)S(1)}, bf16[192,512]{1,0:T(8,128)(2,1)S(1)}, u32[]{:S(2)}, u32[]{:S(2)}) %collective-permute-start.23) | collective-permute-done | bytes 196640 | tf_op jit(solution)/shard_map/ppermute | solution.py:352
  156.7 5.2 %collective-permute-done.21 = bf16[192,512]{1,0:T(8,128)(2,1)S(1)} collective-permute-done((bf16[192,512]{1,0:T(8,128)(2,1)S(1)}, bf16[192,512]{1,0:T(8,128)(2,1)S(1)}, u32[]{:S(2)}, u32[]{:S(2)}) %collective-permute-start.21) | collective-permute-done | bytes 196640 | tf_op jit(solution)/shard_map/ppermute | solution.py:352
  (83 shorter events, 36.0 us)
Async XLA Ops:
  0.6 9.4 %collective-permute-start.1 = (bf16[192,512]{1,0:T(8,128)(2,1)}, bf16[192,512]{1,0:T(8,128)(2,1)S(1)}, u32[]{:S(2)}, u32[]{:S(2)}) collective-permute-start(bf16[192,512]{1,0:T(8,128)(2,1)} %refs_0_.1), channel_id=1, source_target_pairs={{2,0},{3,1},{4,2},{5,3},{6,4},{7,5},{0,6},{1,7},{10,8},{11,9},{12,... | collective-permute-start | bytes 589832 | tf_op jit(solution)/shard_map/ppermute | solution.py:352
  4.0 9.7 %collective-permute-start.3 = (bf16[192,512]{1,0:T(8,128)(2,1)}, bf16[192,512]{1,0:T(8,128)(2,1)S(1)}, u32[]{:S(2)}, u32[]{:S(2)}) collective-permute-start(bf16[192,512]{1,0:T(8,128)(2,1)} %refs_0_.1), channel_id=1, source_target_pairs={{4,0},{5,1},{6,2},{7,3},{0,4},{1,5},{2,6},{3,7},{12,8},{13,9},{14,... | collective-permute-start | bytes 589832 | tf_op jit(solution)/shard_map/ppermute | solution.py:352
  4.5 12.2 %collective-permute-start.5 = (bf16[192,512]{1,0:T(8,128)(2,1)}, bf16[192,512]{1,0:T(8,128)(2,1)S(1)}, u32[]{:S(2)}, u32[]{:S(2)}) collective-permute-start(bf16[192,512]{1,0:T(8,128)(2,1)} %refs_0_.1), channel_id=1, source_target_pairs={{6,0},{7,1},{0,2},{1,3},{2,4},{3,5},{4,6},{5,7},{14,8},{15,9},{8,1... | collective-permute-start | bytes 589832 | tf_op jit(solution)/shard_map/ppermute | solution.py:352
  5.1 12.1 %collective-permute-start = (bf16[192,512]{1,0:T(8,128)(2,1)}, bf16[192,512]{1,0:T(8,128)(2,1)S(1)}, u32[]{:S(2)}, u32[]{:S(2)}) collective-permute-start(bf16[192,512]{1,0:T(8,128)(2,1)} %refs_0_.1), channel_id=1, source_target_pairs={{1,0},{0,1},{3,2},{2,3},{5,4},{4,5},{7,6},{6,7},{9,8},{8,9},{11,10... | collective-permute-start | bytes 589832 | tf_op jit(solution)/shard_map/ppermute | solution.py:352
  10.1 7.2 %collective-permute-start.2 = (bf16[192,512]{1,0:T(8,128)(2,1)S(1)}, bf16[192,512]{1,0:T(8,128)(2,1)S(1)}, u32[]{:S(2)}, u32[]{:S(2)}) collective-permute-start(bf16[192,512]{1,0:T(8,128)(2,1)S(1)} %collective-permute-done.1.refs_2_), channel_id=1, source_target_pairs={{1,0},{0,1},{3,2},{2,3},{5,4},{4,5},{7,6},{6,7},{9,8},{8,9},{11,10... | collective-permute-start | bytes 589832 | tf_op jit(solution)/shard_map/ppermute | solution.py:352
  13.7 3.6 %collective-permute-start.4 = (bf16[192,512]{1,0:T(8,128)(2,1)S(1)}, bf16[192,512]{1,0:T(8,128)(2,1)S(1)}, u32[]{:S(2)}, u32[]{:S(2)}) collective-permute-start(bf16[192,512]{1,0:T(8,128)(2,1)S(1)} %collective-permute-done.3.refs_4_), channel_id=1, source_target_pairs={{1,0},{0,1},{3,2},{2,3},{5,4},{4,5},{7,6},{6,7},{9,8},{8,9},{11,10... | collective-permute-start | bytes 589832 | tf_op jit(solution)/shard_map/ppermute | solution.py:352
  16.8 1.6 collective-permute-start.6
  47.7 10.8 %collective-permute-start.7 = (f32[3,128,128]{2,1,0:T(8,128)S(1)}, f32[3,128,128]{2,1,0:T(8,128)S(1)}, u32[]{:S(2)}, u32[]{:S(2)}) collective-permute-start(f32[3,128,128]{2,1,0:T(8,128)S(1)} %get-tuple-element.43), channel_id=1, source_target_pairs={{8,0},{16,8},{24,16},{0,24},{40,32},{48,40},{56,48},{32,56},{72,64... | collective-permute-start | bytes 589832 | tf_op jit(solution)/shard_map/ppermute | solution.py:363
  50.5 8.0 %collective-permute-start.8 = (f32[3,128,128]{2,1,0:T(8,128)S(1)}, f32[3,128,128]{2,1,0:T(8,128)S(1)}, u32[]{:S(2)}, u32[]{:S(2)}) collective-permute-start(f32[3,128,128]{2,1,0:T(8,128)S(1)} %get-tuple-element.42), channel_id=1, source_target_pairs={{16,0},{24,8},{0,16},{8,24},{48,32},{56,40},{32,48},{40,56},{80,64... | collective-permute-start | bytes 589832 | tf_op jit(solution)/shard_map/ppermute | solution.py:363
  50.8 12.2 %collective-permute-start.9 = (f32[3,128,128]{2,1,0:T(8,128)S(1)}, f32[3,128,128]{2,1,0:T(8,128)S(1)}, u32[]{:S(2)}, u32[]{:S(2)}) collective-permute-start(f32[3,128,128]{2,1,0:T(8,128)S(1)} %get-tuple-element.41), channel_id=1, source_target_pairs={{24,0},{0,8},{8,16},{16,24},{56,32},{32,40},{40,48},{48,56},{88,64... | collective-permute-start | bytes 589832 | tf_op jit(solution)/shard_map/ppermute | solution.py:363
  63.8 13.4 %collective-permute-start.10 = (f32[3,128,128]{2,1,0:T(8,128)S(1)}, f32[3,128,128]{2,1,0:T(8,128)S(1)}, u32[]{:S(2)}, u32[]{:S(2)}) collective-permute-start(f32[3,128,128]{2,1,0:T(8,128)S(1)} %group.1), channel_id=1, source_target_pairs={{224,0},{232,8},{240,16},{248,24},{0,32},{8,40},{16,48},{24,56},{3... | collective-permute-start | bytes 589832 | tf_op jit(solution)/shard_map/ppermute | solution.py:363
  65.5 14.6 %collective-permute-start.11 = (f32[3,128,128]{2,1,0:T(8,128)S(1)}, f32[3,128,128]{2,1,0:T(8,128)S(1)}, u32[]{:S(2)}, u32[]{:S(2)}) collective-permute-start(f32[3,128,128]{2,1,0:T(8,128)S(1)} %group.1), channel_id=1, source_target_pairs={{192,0},{200,8},{208,16},{216,24},{224,32},{232,40},{240,48},{248,... | collective-permute-start | bytes 589832 | tf_op jit(solution)/shard_map/ppermute | solution.py:363
  68.5 26.2 %collective-permute-start.12 = (f32[3,128,128]{2,1,0:T(8,128)S(1)}, f32[3,128,128]{2,1,0:T(8,128)S(1)}, u32[]{:S(2)}, u32[]{:S(2)}) collective-permute-start(f32[3,128,128]{2,1,0:T(8,128)S(1)} %group.1), channel_id=1, source_target_pairs={{160,0},{168,8},{176,16},{184,24},{192,32},{200,40},{208,48},{216,... | collective-permute-start | bytes 589832 | tf_op jit(solution)/shard_map/ppermute | solution.py:363
  72.3 27.0 %collective-permute-start.13 = (f32[3,128,128]{2,1,0:T(8,128)S(1)}, f32[3,128,128]{2,1,0:T(8,128)S(1)}, u32[]{:S(2)}, u32[]{:S(2)}) collective-permute-start(f32[3,128,128]{2,1,0:T(8,128)S(1)} %group.1), channel_id=1, source_target_pairs={{128,0},{136,8},{144,16},{152,24},{160,32},{168,40},{176,48},{184,... | collective-permute-start | bytes 589832 | tf_op jit(solution)/shard_map/ppermute | solution.py:363
  72.8 26.4 %collective-permute-start.14 = (f32[3,128,128]{2,1,0:T(8,128)S(1)}, f32[3,128,128]{2,1,0:T(8,128)S(1)}, u32[]{:S(2)}, u32[]{:S(2)}) collective-permute-start(f32[3,128,128]{2,1,0:T(8,128)S(1)} %group.1), channel_id=1, source_target_pairs={{96,0},{104,8},{112,16},{120,24},{128,32},{136,40},{144,48},{152,5... | collective-permute-start | bytes 589832 | tf_op jit(solution)/shard_map/ppermute | solution.py:363
  77.2 29.9 %collective-permute-start.15 = (f32[3,128,128]{2,1,0:T(8,128)S(1)}, f32[3,128,128]{2,1,0:T(8,128)S(1)}, u32[]{:S(2)}, u32[]{:S(2)}) collective-permute-start(f32[3,128,128]{2,1,0:T(8,128)S(1)} %group.1), channel_id=1, source_target_pairs={{64,0},{72,8},{80,16},{88,24},{96,32},{104,40},{112,48},{120,56},{... | collective-permute-start | bytes 589832 | tf_op jit(solution)/shard_map/ppermute | solution.py:363
  80.1 28.1 %collective-permute-start.16 = (f32[3,128,128]{2,1,0:T(8,128)S(1)}, f32[3,128,128]{2,1,0:T(8,128)S(1)}, u32[]{:S(2)}, u32[]{:S(2)}) collective-permute-start(f32[3,128,128]{2,1,0:T(8,128)S(1)} %group.1), channel_id=1, source_target_pairs={{32,0},{40,8},{48,16},{56,24},{64,32},{72,40},{80,48},{88,56},{96,... | collective-permute-start | bytes 589832 | tf_op jit(solution)/shard_map/ppermute | solution.py:363
  110.7 4.1 %collective-permute-start.17 = (f32[2,128,128]{2,1,0:T(8,128)}, f32[2,128,128]{2,1,0:T(8,128)}, u32[]{:S(2)}, u32[]{:S(2)}) collective-permute-start(f32[2,128,128]{2,1,0:T(8,128)} %get-tuple-element.46), channel_id=1, source_target_pairs={{8,0},{16,8},{24,16},{0,24},{40,32},{48,40},{56,48},{32,56},{72,64... | collective-permute-start | bytes 393224 | tf_op jit(solution)/shard_map/ppermute | solution.py:363
  110.7 5.7 %collective-permute-start.18 = (f32[2,128,128]{2,1,0:T(8,128)}, f32[2,128,128]{2,1,0:T(8,128)}, u32[]{:S(2)}, u32[]{:S(2)}) collective-permute-start(f32[2,128,128]{2,1,0:T(8,128)} %get-tuple-element.45), channel_id=1, source_target_pairs={{16,0},{24,8},{0,16},{8,24},{48,32},{56,40},{32,48},{40,56},{80,64... | collective-permute-start | bytes 393224 | tf_op jit(solution)/shard_map/ppermute | solution.py:363
  111.1 7.9 %collective-permute-start.19 = (f32[2,128,128]{2,1,0:T(8,128)}, f32[2,128,128]{2,1,0:T(8,128)}, u32[]{:S(2)}, u32[]{:S(2)}) collective-permute-start(f32[2,128,128]{2,1,0:T(8,128)} %get-tuple-element.44), channel_id=1, source_target_pairs={{24,0},{0,8},{8,16},{16,24},{56,32},{32,40},{40,48},{48,56},{88,64... | collective-permute-start | bytes 393224 | tf_op jit(solution)/shard_map/ppermute | solution.py:363
  139.0 4.2 %collective-permute-start.20 = (bf16[4,192,512]{2,1,0:T(8,128)(2,1)S(1)}, bf16[4,192,512]{2,1,0:T(8,128)(2,1)S(1)}, u32[]{:S(2)}, u32[]{:S(2)}) collective-permute-start(bf16[4,192,512]{2,1,0:T(8,128)(2,1)S(1)} %shares.2), channel_id=1, source_target_pairs={{1,0},{0,1},{3,2},{2,3},{5,4},{4,5},{7,6},{6,7},{9,8},{8,9},{11,10... | collective-permute-start | bytes 2359304 | tf_op jit(solution)/shard_map/ppermute | solution.py:352
  148.9 6.2 %collective-permute-start.23 = (bf16[192,512]{1,0:T(8,128)(2,1)S(1)}, bf16[192,512]{1,0:T(8,128)(2,1)S(1)}, u32[]{:S(2)}, u32[]{:S(2)}) collective-permute-start(bf16[192,512]{1,0:T(8,128)(2,1)S(1)} %get-tuple-element.39), channel_id=1, source_target_pairs={{2,0},{3,1},{4,2},{5,3},{6,4},{7,5},{0,6},{1,7},{10,8},{11,9},{12,... | collective-permute-start | bytes 589832 | tf_op jit(solution)/shard_map/ppermute | solution.py:352
  149.4 7.3 %collective-permute-start.22 = (bf16[192,512]{1,0:T(8,128)(2,1)S(1)}, bf16[192,512]{1,0:T(8,128)(2,1)S(1)}, u32[]{:S(2)}, u32[]{:S(2)}) collective-permute-start(bf16[192,512]{1,0:T(8,128)(2,1)S(1)} %get-tuple-element.40), channel_id=1, source_target_pairs={{4,0},{5,1},{6,2},{7,3},{0,4},{1,5},{2,6},{3,7},{12,8},{13,9},{14,... | collective-permute-start | bytes 589832 | tf_op jit(solution)/shard_map/ppermute | solution.py:352
  149.8 12.1 %collective-permute-start.21 = (bf16[192,512]{1,0:T(8,128)(2,1)S(1)}, bf16[192,512]{1,0:T(8,128)(2,1)S(1)}, u32[]{:S(2)}, u32[]{:S(2)}) collective-permute-start(bf16[192,512]{1,0:T(8,128)(2,1)S(1)} %get-tuple-element.38), channel_id=1, source_target_pairs={{6,0},{7,1},{0,2},{1,3},{2,4},{3,5},{4,6},{5,7},{14,8},{15,9},{8,1... | collective-permute-start | bytes 589832 | tf_op jit(solution)/shard_map/ppermute | solution.py:352
  (21 other events, 81.5 us)

commit v2 on v0

v2 whole, which is shorter than its diff:
```python
import functools

import jax
import jax.numpy as jnp
from jax import lax
from jax.experimental import pallas as pl
from jax.experimental.pallas import tpu as pltpu
from jax.sharding import PartitionSpec as P

F32 = jnp.float32
BF16 = jnp.bfloat16
SPAN = 64
INNER = 4
VMEM_BYTES = 24 * 1024 * 1024
FETCH_BYTES = 16 * 1024 * 1024


def product(left, right, over_left=1, over_right=0):
    return lax.dot_general(
        left,
        right,
        (((over_left,), (over_right,)), ((), ())),
        preferred_element_type=F32,
    )


def halves(value):
    if isinstance(value, tuple):
        return value
    if value.dtype == BF16:
        return (value, None)
    high = value.astype(BF16)
    return (high, (value - high.astype(F32)).astype(BF16))


def fine(left, right, over_left=1, over_right=0):
    left_high, left_low = halves(left)
    right_high, right_low = halves(right)
    lefts, rights = [left_high], [right_high]
    if left_low is not None:
        lefts.append(left_low)
        rights.append(right_high)
    if right_low is not None:
        lefts.append(left_high)
        rights.append(right_low)
    return product(
        jnp.concatenate(lefts, axis=over_left),
        jnp.concatenate(rights, axis=over_right),
        over_left,
        over_right,
    )


def block_times(axis, shape):
    index = lax.broadcasted_iota(jnp.int32, shape, axis)
    return 2 * lax.rem(index, SPAN) + lax.div(index, SPAN)


def key_order():
    shape = (2 * SPAN, 2 * SPAN)
    return block_times(0, shape), block_times(1, shape)


def solver_levels():
    later, earlier = key_order()
    levels = []
    for level in range((2 * SPAN).bit_length() - 1):
        later_half, earlier_half = later >> level, earlier >> level
        levels.append(
            ((later_half >> 1) == (earlier_half >> 1)) & (later_half > earlier_half)
        )
    return levels


def seen(axis):
    shape = (SPAN, 2 * SPAN) if axis == 0 else (2 * SPAN, SPAN)
    return block_times(1 - axis, shape) <= 2 * lax.broadcasted_iota(jnp.int32, shape, axis) + 1


def unit_rows(rows):
    inverse = lax.rsqrt(jnp.sum(rows * rows, axis=1, keepdims=True) + 1e-06)
    return rows * inverse, inverse


def local_blocks(key_rows, rates, values, queries, cotangents):
    each = range(len(key_rows))
    levels = solver_levels()
    sees = seen(1)
    later, earlier = key_order()
    keys = [unit_rows(key_rows[i])[0] for i in each]
    key_halves = [halves(keys[i]) for i in each]
    crossings = [
        jnp.where(later > earlier, rates[i] * fine(key_halves[i], key_halves[i], 1, 1), 0.0)
        for i in each
    ]
    lower = [halves(crossings[i]) for i in each]
    one = jnp.where(later == earlier, 1.0, 0.0)
    solver = [one - jnp.where(levels[0], crossings[i], 0.0) for i in each]
    for level in levels[1:]:
        parts = [halves(solver[i]) for i in each]
        step = [fine(lower[i], parts[i]) for i in each]
        solver = [solver[i] - jnp.where(level, fine(parts[i], step[i]), 0.0) for i in each]
    turned = [halves(jnp.swapaxes(solver[i], 0, 1)) for i in each]
    targets = [
        jnp.concatenate([rates[i] * keys[i], rates[i] * values[i].astype(F32)], axis=1)
        for i in each
    ]
    mixes = [fine(solver[i], targets[i]) for i in each]
    early = [
        fine(jnp.where(sees, fine(key_halves[i], queries[i], 1, 1), 0.0), cotangents[i])
        for i in each
    ]
    pushes = [
        fine(turned[i], jnp.concatenate([keys[i], early[i]], axis=1)) for i in each
    ]
    width = keys[0].shape[1]
    moves = [fine(jnp.swapaxes(keys[i], 0, 1), mixes[i]) for i in each]
    diagonal = lax.broadcasted_iota(jnp.int32, (width, width), 0) == lax.broadcasted_iota(
        jnp.int32, (width, width), 1
    )
    transitions = [jnp.where(diagonal, 1.0, 0.0) - moves[i][:, :width] for i in each]
    offsets = [moves[i][:, width:] for i in each]
    ratings = [jnp.swapaxes(rates[i] * pushes[i][:, width:], 0, 1) for i in each]
    pulls = [
        fine(jnp.swapaxes(cotangents[i].astype(F32), 0, 1).astype(BF16), queries[i])
        - fine(ratings[i], key_halves[i])
        for i in each
    ]
    return mixes, pushes, transitions, offsets, pulls


def chained(transitions, offsets, pulls):
    transition, offset, pull = transitions[0], offsets[0], pulls[0]
    for later in range(1, len(transitions)):
        parts = halves(transition)
        after = halves(transitions[later])
        pull = pull + fine(pulls[later], parts)
        offset = fine(after, offset) + offsets[later]
        transition = fine(after, parts)
    return transition, offset, pull


def entered(transitions, offsets, pulls, state, returning):
    count = len(transitions)
    states, returned = [state], [returning]
    for i in range(count - 1):
        states.append(fine(transitions[i], states[-1]) + offsets[i])
        back = count - 1 - i
        returned.append(fine(returned[-1], transitions[back]) + pulls[back])
    return states, returned[::-1]


def full_blocks(key_rows, rates, queries, cotangents, mixes, pushes, states, returning):
    each = range(len(key_rows))
    later, earlier = key_order()
    sees, seen_by = seen(0), seen(1)
    width = key_rows[0].shape[1]
    normal = [unit_rows(key_rows[i]) for i in each]
    keys = [normal[i][0] for i in each]
    key_halves = [halves(keys[i]) for i in each]
    state_halves = [halves(states[i]) for i in each]
    returning_halves = [halves(returning[i]) for i in each]
    residues = [mixes[i][:, width:] - fine(mixes[i][:, :width], state_halves[i]) for i in each]
    pushed = [
        pushes[i][:, width:] + fine(pushes[i][:, :width], returning_halves[i], 1, 1) for i in each
    ]
    residue_halves = [halves(residues[i]) for i in each]
    ratings = [rates[i] * pushed[i] for i in each]
    rating_halves = [halves(ratings[i]) for i in each]
    scores = [jnp.where(sees, fine(queries[i], key_halves[i], 1, 1), 0.0) for i in each]
    mixed = [
        fine(queries[i], state_halves[i]) + fine(scores[i], residue_halves[i]) for i in each
    ]
    score_cots = [
        jnp.where(sees, fine(cotangents[i], residue_halves[i], 1, 1), 0.0) for i in each
    ]
    turned_cots = [
        jnp.where(seen_by, fine(residue_halves[i], cotangents[i], 1, 1), 0.0) for i in each
    ]
    query_cots = [
        fine(cotangents[i], state_halves[i], 1, 1) + fine(score_cots[i], key_halves[i])
        for i in each
    ]
    links = [
        jnp.where(later > earlier, fine(rating_halves[i], residue_halves[i], 1, 1), 0.0)
        for i in each
    ]
    links = [links[i] + jnp.swapaxes(links[i], 0, 1) for i in each]
    key_cots = [
        fine(turned_cots[i], queries[i])
        + fine(residue_halves[i], returning_halves[i])
        - fine(rating_halves[i], state_halves[i], 1, 1)
        - fine(links[i], key_halves[i])
        for i in each
    ]
    logit_cots = [
        jnp.sum(pushed[i] * residues[i], axis=1, keepdims=True) * (1.0 - 0.5 * rates[i])
        for i in each
    ]
    key_row_cots = [
        normal[i][1]
        * (key_cots[i] - keys[i] * jnp.sum(keys[i] * key_cots[i], axis=1, keepdims=True))
        for i in each
    ]
    return mixed, query_cots, ratings, key_row_cots, logit_cots


def head_rows(ref, head, width):
    lanes = slice(head * width, (head + 1) * width)
    return [ref[i : i + SPAN, lanes] for i in range(0, ref.shape[0], SPAN)]


def head_pairs(ref, head, width):
    return [
        jnp.concatenate([rows[:, :width], rows[:, width:]], axis=0)
        for rows in head_rows(ref, head, 2 * width)
    ]


def unpaired(rows):
    return jnp.concatenate([rows[:SPAN], rows[SPAN:]], axis=1)


def head_rates(logits, head):
    rates = 2.0 * jax.nn.sigmoid(logits[:, 2 * head : 2 * head + 2])
    return [
        jnp.concatenate([rates[i : i + SPAN, :1], rates[i : i + SPAN, 1:]], axis=0)
        for i in range(0, logits.shape[0], SPAN)
    ]


def each_head(heads, of):
    return [part for head in range(heads) for part in of(head)]


def fetch_kernel(*refs):
    count = len(refs) // 2
    arrays, places, sems = refs[:count], refs[count : 2 * count], refs[2 * count]
    copies = [
        pltpu.make_async_copy(array, place, sems.at[i])
        for i, (array, place) in enumerate(zip(arrays, places))
    ]
    for copy in copies:
        copy.start()
    for copy in copies:
        copy.wait()


def project_kernel(masks, *refs):
    pieces = refs[: len(masks)]
    (key_weight, beta_weight, beta_bias, queries, values, out_grad) = refs[
        len(masks) : len(masks) + 6
    ]
    (key_proj, logits, mixes, pushes, moves) = refs[len(masks) + 6 : len(masks) + 11]
    wholes, totals = refs[len(masks) + 11 : -1], refs[-1]
    heads = len(wholes)
    depth = pieces[0].shape[1]
    width = queries.shape[1] // heads
    blocks = queries.shape[0] // SPAN
    me = lax.axis_index("head")
    place = lax.rem(lax.axis_index("ctx"), INNER)
    starts = [pl.multiple_of((me ^ mask) * depth, depth) for mask in masks]

    total = beta_bias[...]
    for piece, start in zip(pieces, starts):
        total = total + product(piece[...], beta_weight[:, pl.ds(start, depth)], 1, 1)
    logits[...] = total
    for head in range(heads):
        wide = slice(2 * head * width, 2 * (head + 1) * width)
        total = product(pieces[0][...], key_weight[pl.ds(starts[0], depth), wide])
        for piece, start in zip(pieces[1:], starts[1:]):
            total = total + product(piece[...], key_weight[pl.ds(start, depth), wide])
        key_proj[:, wide] = total
    found = local_blocks(
        each_head(heads, lambda head: head_pairs(key_proj, head, width)),
        each_head(heads, lambda head: head_rates(logits, head)),
        each_head(heads, lambda head: head_pairs(values, head, width)),
        each_head(heads, lambda head: head_rows(queries, head, width)),
        each_head(heads, lambda head: head_rows(out_grad, head, width)),
    )
    for head in range(heads):
        mine = [arrays[head * blocks : (head + 1) * blocks] for arrays in found]
        for i in range(blocks):
            mixes[head, i] = mine[0][i]
            pushes[head, i] = mine[1][i]
            for part in range(3):
                moves[head, part, i] = mine[2 + part][i]
        for part, array in enumerate(chained(*mine[2:])):
            totals[head, part] = array
    for mask, whole in enumerate(wholes):
        whole[...] = totals[place ^ mask]


def parts_of(ref):
    return [ref[part] for part in range(3)]


def join_kernel(*refs):
    arrived, (spans, total) = refs[:-2], refs[-2:]
    place = lax.rem(lax.axis_index("ctx"), INNER)
    for mask, ref in enumerate(arrived):
        spans[place ^ mask] = ref[...]
    found = chained(*[[spans[i, part] for i in range(len(arrived))] for part in range(3)])
    for part in range(3):
        total[part] = found[part]


def wider(mine, other, upper):
    first = [jnp.where(upper, theirs, own) for own, theirs in zip(mine, other)]
    second = [jnp.where(upper, own, theirs) for own, theirs in zip(mine, other)]
    return chained(*[list(pair) for pair in zip(first, second)])


def pair_kernel(mine, other, total):
    upper = lax.rem(lax.div(lax.axis_index("ctx"), INNER), 2) == 1
    found = wider(parts_of(mine), parts_of(other), upper)
    for part in range(3):
        total[part] = found[part]


def quad_kernel(pair, other, total):
    group = lax.div(lax.axis_index("ctx"), INNER)
    found = wider(parts_of(pair), parts_of(other), lax.rem(lax.div(group, 2), 2) == 1)
    total[...] = jnp.where(group < 4, found[1], found[2])


def scan_kernel(spans, near_group, near_pair, far_half, *refs):
    outputs, entering = refs[:-1], refs[-1]
    position = lax.axis_index("ctx")
    group, place = lax.div(position, INNER), lax.rem(position, INNER)
    nothing = jnp.zeros(far_half.shape, F32)
    state = jnp.where(group >= 4, far_half[...], nothing)
    returning = jnp.where(group < 4, far_half[...], nothing)
    for ref, above in ((near_pair, lax.rem(lax.div(group, 2), 2)), (near_group, lax.rem(group, 2))):
        transition = halves(ref[0])
        state = jnp.where(above == 1, fine(transition, state) + ref[1], state)
        returning = jnp.where(above == 0, fine(returning, transition) + ref[2], returning)
    count = spans.shape[0]
    states, returned = entered(
        *[[spans[i, part] for i in range(count)] for part in range(3)], state, returning
    )
    for i in range(count):
        entering[i, 0] = states[i]
        entering[i, 1] = returned[i]
    for mask, output in enumerate(outputs):
        output[...] = entering[place ^ mask]


def outputs_kernel(*refs):
    (key_proj, logits, queries, out_grad, mixes, pushes, moves) = refs[:7]
    arrived = refs[7 : 7 + INNER]
    (mixed, query_grad, value_grad, key_cot, logit_cot, entering) = refs[7 + INNER :]
    heads = moves.shape[0]
    place = lax.rem(lax.axis_index("ctx"), INNER)
    width = queries.shape[1] // heads
    blocks = queries.shape[0] // SPAN
    each = range(blocks)
    for mask, ref in enumerate(arrived):
        entering[place ^ mask] = ref[...]
    around = [
        entered(
            *[[moves[head, part, i] for i in each] for part in range(3)],
            entering[head, 0],
            entering[head, 1],
        )
        for head in range(heads)
    ]
    found = full_blocks(
        each_head(heads, lambda head: head_pairs(key_proj, head, width)),
        each_head(heads, lambda head: head_rates(logits, head)),
        each_head(heads, lambda head: head_rows(queries, head, width)),
        each_head(heads, lambda head: head_rows(out_grad, head, width)),
        each_head(heads, lambda head: [mixes[head, i] for i in each]),
        each_head(heads, lambda head: [pushes[head, i] for i in each]),
        each_head(heads, lambda head: around[head][0]),
        each_head(heads, lambda head: around[head][1]),
    )
    for head in range(heads):
        lanes = slice(head * width, (head + 1) * width)
        wide = slice(2 * head * width, 2 * (head + 1) * width)
        for i in each:
            rows = slice(i * SPAN, (i + 1) * SPAN)
            block = head * blocks + i
            mixed[rows, lanes] = found[0][block].astype(BF16)
            query_grad[rows, lanes] = found[1][block].astype(BF16)
            value_grad[rows, wide] = unpaired(found[2][block]).astype(BF16)
            key_cot[rows, wide] = unpaired(found[3][block]).astype(BF16)
    for i in each:
        columns = [unpaired(found[4][head * blocks + i]) for head in range(heads)]
        logit_cot[i * SPAN : (i + 1) * SPAN, :] = jnp.concatenate(columns, axis=1).astype(BF16)


def shares_kernel(core, key_cot, logit_cot, key_weight, beta_weight, *refs):
    output = refs[-1]
    depth = output.shape[2]
    me = lax.axis_index("head")
    for chip in range(output.shape[0]):
        start = pl.multiple_of((me ^ (2 * chip + core)) * depth, depth)
        total = product(key_cot[...], key_weight[pl.ds(start, depth), :], 1, 1)
        total = total + product(logit_cot[...], beta_weight[:, pl.ds(start, depth)])
        if len(refs) > 1:
            total = total + refs[0][chip].astype(F32)
        output[chip] = total.astype(output.dtype)


VMEM = pl.BlockSpec(memory_space=pltpu.VMEM)


def shape_of(*shape, dtype=F32):
    return jax.ShapeDtypeStruct(shape, dtype)


def call(kernel, name, out_shape, *operands, scratch=(), specs=None, limit=VMEM_BYTES, cost=None):
    single = isinstance(out_shape, jax.ShapeDtypeStruct)
    return pl.pallas_call(
        kernel,
        in_specs=specs or [VMEM] * len(operands),
        out_specs=VMEM if single else [VMEM] * len(out_shape),
        out_shape=out_shape,
        scratch_shapes=list(scratch),
        compiler_params=pltpu.CompilerParams(vmem_limit_bytes=limit),
        cost_estimate=cost,
        name=name,
    )(*operands)


def fetch(*arrays):
    return call(
        fetch_kernel,
        "fetch",
        [shape_of(*array.shape, dtype=array.dtype) for array in arrays],
        *arrays,
        scratch=[pltpu.SemaphoreType.DMA((len(arrays),))],
        specs=[pl.BlockSpec(memory_space=pltpu.HBM)] * len(arrays),
        limit=FETCH_BYTES,
        cost=pl.CostEstimate(
            flops=0, bytes_accessed=2 * sum(array.nbytes for array in arrays), transcendentals=0
        ),
    )


def project(masks, pieces, key_weight, beta_across, beta_bias, queries, values, out_grad):
    rows = pieces[0].shape[0]
    heads = beta_bias.shape[1] // 2
    width = queries.shape[1] // heads
    blocks, keys = rows // SPAN, 2 * SPAN
    return call(
        functools.partial(project_kernel, masks),
        "project",
        [
            shape_of(rows, 2 * heads * width),
            shape_of(rows, 2 * heads),
            shape_of(heads, blocks, keys, 2 * width),
            shape_of(heads, blocks, keys, 2 * width),
            shape_of(heads, 3, blocks, width, width),
        ]
        + [shape_of(3, width, width)] * heads,
        *pieces,
        key_weight,
        beta_across,
        beta_bias,
        queries,
        values,
        out_grad,
        scratch=[pltpu.VMEM((heads, 3, width, width), F32)],
    )


def finish(key_proj, logits, queries, out_grad, mixes, pushes, moves, arrived):
    rows = queries.shape[0]
    heads = logits.shape[1] // 2
    width = queries.shape[1] // heads
    return call(
        outputs_kernel,
        "outputs",
        [
            shape_of(rows, heads * width, dtype=BF16),
            shape_of(rows, heads * width, dtype=BF16),
            shape_of(rows, 2 * heads * width, dtype=BF16),
            shape_of(rows, 2 * heads * width, dtype=BF16),
            shape_of(rows, 2 * heads, dtype=BF16),
        ],
        key_proj,
        logits,
        queries,
        out_grad,
        mixes,
        pushes,
        moves,
        *arrived,
        scratch=[pltpu.VMEM((heads, 2, width, width), F32)],
    )


def shares(core, chips, key_cot, logit_cot, key_weight, beta_across, dtype, *more):
    depth = key_weight.shape[0] // (2 * chips)
    return call(
        functools.partial(shares_kernel, core),
        "shares",
        shape_of(chips, key_cot.shape[0], depth, dtype=dtype),
        key_cot,
        logit_cot,
        key_weight,
        beta_across,
        *more,
    )


def swapped(value, axis, mask):
    return lax.ppermute(value, axis, [(i, i ^ mask) for i in range(lax.axis_size(axis))])


def per_device(inputs, key_weight, beta_weight, beta_bias, queries, values, out_grad):
    heads = beta_bias.shape[0] // 2
    width = queries.shape[1] // heads
    chips = lax.axis_size("head") // 2
    beta_across = jnp.swapaxes(beta_weight, 0, 1)

    key_weight, beta_across, queries, values, out_grad = fetch(
        key_weight, beta_across, queries, values, out_grad
    )
    masks, pieces = [0, 1], [inputs, swapped(inputs, "head", 1)]
    for chip in (2, 1, 3):
        piece = swapped(inputs, "head", 2 * chip)
        masks += [2 * chip, 2 * chip + 1]
        pieces += [piece, swapped(piece, "head", 1)]
    key_proj, logits, mixes, pushes, moves, *wholes = project(
        masks, pieces, key_weight, beta_across, beta_bias[None], queries, values, out_grad
    )

    arrived = [wholes[0]] + [swapped(wholes[mask], "ctx", mask) for mask in range(1, INNER)]
    square = (width, width)
    spans, group = call(
        join_kernel,
        "join", [shape_of(INNER, 3, *square), shape_of(3, *square)], *arrived
    )
    near_group = swapped(group, "ctx", INNER)
    pair = call(pair_kernel, "pair", shape_of(3, *square), group, near_group)
    near_pair = swapped(pair, "ctx", 2 * INNER)
    quad = call(quad_kernel, "quad", shape_of(*square), pair, near_pair)
    far_half = swapped(quad, "ctx", 4 * INNER)
    entering = call(
        scan_kernel,
        "scan",
        [shape_of(2, *square)] * INNER,
        spans,
        near_group,
        near_pair,
        far_half,
        scratch=[pltpu.VMEM((INNER, 2, *square), F32)],
    )
    arrived = [entering[0]] + [swapped(entering[mask], "ctx", mask) for mask in range(1, INNER)]

    mixed, query_grad, value_grad, key_cot, logit_cot = finish(
        key_proj, logits, queries, out_grad, mixes, pushes, moves, arrived
    )

    operands = (chips, key_cot, logit_cot, key_weight, beta_across)
    away = swapped(shares(1, *operands, BF16), "head", 1)
    own = shares(0, *operands, F32, away)
    total = own[0]
    for chip in (2, 1, 3):
        total = total + swapped(own[chip].astype(BF16), "head", 2 * chip).astype(F32)
    return mixed, query_grad, value_grad, total.astype(BF16)


def solution(mesh):
    placed = (
        P("ctx", "head"),
        P(None, "head"),
        P(None, "head"),
        P("head"),
        P("ctx", "head"),
        P("ctx", "head"),
        P("ctx", "head"),
    )
    return jax.shard_map(
        per_device,
        mesh=mesh,
        in_specs=placed,
        out_specs=(P("ctx", "head"), P("ctx", "head"), P("ctx", "head"), P("ctx", "head")),
        check_vma=False,
    )
```

time: 991 us -> 117 us (0.12)
  waiting for transfers between devices: 319 us -> 45.1 us
  other arithmetic: 263 us -> 0.89 us
  matrix products: 188 us -> 0 us
  starting transfers between devices: 183 us -> 37.6 us
  Pallas kernels: 0 us -> 25.4 us
  between operations: 14.6 us -> 0.79 us
    another operation x39 -> x1, other arithmetic: 246 us -> 0.1 us  [the longest x27 246 us: block_parts(): jax.scipy.linalg.solve_triangular(triangle, targets, lower=True, unit_dia...]
    dot_general x163 -> x0, matrix products: 178 us -> none  [the longest x117 122 us: batched(): return jnp.einsum('hij,hjk->hik', left, right, precision=maximal_precision)]
    ppermute x62 -> x20, waiting for transfers between devices: 208 us -> 45.1 us  [swapped(): lax.ppermute(value, axis, [(i, i ^ mask) for i in range(lax.axis_size(axi...]
    ppermute x62 -> x20, starting transfers between devices: 183 us -> 37.6 us  [swapped(): lax.ppermute(value, axis, [(i, i ^ mask) for i in range(lax.axis_size(axi...]
    reduce_scatter x1 -> x0, waiting for transfers between devices: 83 us -> none  [per_device(): lax.psum_scatter(partial_grad, 'head', scatter_dimension=1, tiled=True)]
    all_gather x1 -> x0, waiting for transfers between devices: 27.8 us -> none  [per_device(): piece = lax.all_gather(inputs, 'head', axis=1, tiled=True)]
    pallas_call x0 -> x9, Pallas kernels: none -> 25.4 us  [call(): pl.pallas_call(kernel, in_specs=specs or [VMEM] * len(operands), out_spec...]
    another operation x9 -> x0, matrix products: 10.1 us -> none  [block_parts(): jax.scipy.linalg.solve_triangular(triangle, targets, lower=True, unit_dia...]
  transfers between devices with their start and end apart: 64 -> 20, of which waited for: 64 -> 13; matrix products, arithmetic and copies ran while one was open for 4% -> 0% of each run, Pallas kernels for 0% -> 1%
where the time goes in v2:
time: 117 us
  waiting for transfers between devices  45.1 us (39%)
  starting transfers between devices  37.6 us (32%)
  Pallas kernels  25.4 us (22%)
  local copies, waits for them, and re-layouts  7.12 us (6%)
    ppermute x20, waiting for transfers between devices, swapped(): lax.ppermute(value, axis, [(i, i ^ mask) for i in range(lax.axis_size(axi...  45.1 us
    ppermute x20, starting transfers between devices, swapped(): lax.ppermute(value, axis, [(i, i ^ mask) for i in range(lax.axis_size(axi...  37.6 us
    pallas_call x9, Pallas kernels, call(): pl.pallas_call(kernel, in_specs=specs or [VMEM] * len(operands), out_spec...  25.4 us
    unnamed x14, local copies, waits for them, and re-layouts  7.08 us
  transfers between devices with their start and end apart: 20, of which 13 were waited for; matrix products, arithmetic and copies ran while one was open for 0% of the time, Pallas kernels for 1%

profile of v2, /device:TPU:1, one launch (start us, length us, event | category | flops | bytes accessed | tf_op | source)
XLA Modules:
  0.0 117.0 jit_solution(8079265513262728255)
XLA Ops:
  0.6 2.1 %collective-permute-start.3 = (bf16[192,512]{1,0:T(8,128)(2,1)}, bf16[192,512]{1,0:T(8,128)(2,1)S(1)}, u32[]{:S(2)}, u32[]{:S(2)}) collective-permute-start(bf16[192,512]{1,0:T(8,128)(2,1)} %refs_0_.3), channel_id=1, source_target_pairs={{0,2},{1,3},{2,0},{3,1},{4,6},{5,7},{6,4},{7,5},{8,10},{9,11},{10,... | collective-permute-start | bytes 589832 | tf_op jit(solution)/shard_map/ppermute | solution.py:510
  2.8 2.5 %collective-permute-start.1 = (bf16[192,512]{1,0:T(8,128)(2,1)}, bf16[192,512]{1,0:T(8,128)(2,1)S(1)}, u32[]{:S(2)}, u32[]{:S(2)}) collective-permute-start(bf16[192,512]{1,0:T(8,128)(2,1)} %refs_0_.3), channel_id=1, source_target_pairs={{0,4},{1,5},{2,6},{3,7},{4,0},{5,1},{6,2},{7,3},{8,12},{9,13},{10,... | collective-permute-start | bytes 589832 | tf_op jit(solution)/shard_map/ppermute | solution.py:510
  5.3 3.4 %collective-permute-start = (bf16[192,512]{1,0:T(8,128)(2,1)}, bf16[192,512]{1,0:T(8,128)(2,1)S(1)}, u32[]{:S(2)}, u32[]{:S(2)}) collective-permute-start(bf16[192,512]{1,0:T(8,128)(2,1)} %refs_0_.3), channel_id=1, source_target_pairs={{0,1},{1,0},{2,3},{3,2},{4,5},{5,4},{6,7},{7,6},{8,9},{9,8},{10,11... | collective-permute-start | bytes 589832 | tf_op jit(solution)/shard_map/ppermute | solution.py:510
  8.7 2.6 %collective-permute-start.4 = (bf16[192,512]{1,0:T(8,128)(2,1)S(1)}, bf16[192,512]{1,0:T(8,128)(2,1)S(1)}, u32[]{:S(2)}, u32[]{:S(2)}) collective-permute-start(bf16[192,512]{1,0:T(8,128)(2,1)S(1)} %collective-permute-done.3.refs_4_), channel_id=1, source_target_pairs={{0,1},{1,0},{2,3},{3,2},{4,5},{5,4},{6,7},{7,6},{8,9},{9,8},{10,11... | collective-permute-start | bytes 589832 | tf_op jit(solution)/shard_map/ppermute | solution.py:510
  11.2 2.8 %collective-permute-done.1.refs_2_ = bf16[192,512]{1,0:T(8,128)(2,1)S(1)} collective-permute-done((bf16[192,512]{1,0:T(8,128)(2,1)}, bf16[192,512]{1,0:T(8,128)(2,1)S(1)}, u32[]{:S(2)}, u32[]{:S(2)}) %collective-permute-start.1) | collective-permute-done | bytes 196640 | tf_op jit(solution)/shard_map/ppermute | solution.py:510
  18.2 3.4 %copy-done = bf16[4096,1024]{1,0:T(8,128)(2,1)S(1)} copy-done((bf16[4096,1024]{1,0:T(8,128)(2,1)S(1)}, bf16[4096,1024]{1,0:T(8,128)(2,1)}, u32[]{:S(2)}) %copy-start) | copy-done | bytes 8388632
  26.7 12.6 %project.1 = (f32[192,1024]{1,0:T(8,128)S(1)}, f32[192,8]{1,0:T(8,128)S(1)}, f32[4,3,128,256]{3,2,1,0:T(8,128)S(1)}, f32[4,3,128,256]{3,2,1,0:T(8,128)S(1)}, f32...) custom-call(bf16[192,512]{1,0:T(8,128)(2,1)S(1)} %copy-done.4, ...), custom_call_target="tpu_custom_call" | custom-call | tf_op jit(solution)/shard_map/project/pallas_call | solution.py:415
  40.6 2.7 %collective-permute-start.8 = (f32[3,128,128]{2,1,0:T(8,128)S(1)}, f32[3,128,128]{2,1,0:T(8,128)S(1)}, u32[]{:S(2)}, u32[]{:S(2)}) collective-permute-start(f32[3,128,128]{2,1,0:T(8,128)S(1)} %get-tuple-element.41), channel_id=1, source_target_pairs={{0,16},{8,24},{16,0},{24,8},{32,48},{40,56},{48,32},{56,40},{64,80... | collective-permute-start | bytes 589832 | tf_op jit(solution)/shard_map/ppermute | solution.py:510
  43.3 2.6 %collective-permute-done.7.refs_1_ = f32[3,128,128]{2,1,0:T(8,128)S(1)} collective-permute-done((f32[3,128,128]{2,1,0:T(8,128)S(1)}, f32[3,128,128]{2,1,0:T(8,128)S(1)}, u32[]{:S(2)}, u32[]{:S(2)}) %collective-permute-start.7) | collective-permute-done | bytes 196640 | tf_op jit(solution)/shard_map/ppermute | solution.py:510
  45.9 6.7 %collective-permute-done.8.refs_2_ = f32[3,128,128]{2,1,0:T(8,128)S(1)} collective-permute-done((f32[3,128,128]{2,1,0:T(8,128)S(1)}, f32[3,128,128]{2,1,0:T(8,128)S(1)}, u32[]{:S(2)}, u32[]{:S(2)}) %collective-permute-start.8) | collective-permute-done | bytes 196640 | tf_op jit(solution)/shard_map/ppermute | solution.py:510
  52.6 2.0 %collective-permute-done.9.refs_3_ = f32[3,128,128]{2,1,0:T(8,128)S(1)} collective-permute-done((f32[3,128,128]{2,1,0:T(8,128)S(1)}, f32[3,128,128]{2,1,0:T(8,128)S(1)}, u32[]{:S(2)}, u32[]{:S(2)}) %collective-permute-start.9) | collective-permute-done | bytes 196640 | tf_op jit(solution)/shard_map/ppermute | solution.py:510
  55.4 1.7 %collective-permute-start.10 = (f32[3,128,128]{2,1,0:T(8,128)S(1)}, f32[3,128,128]{2,1,0:T(8,128)S(1)}, u32[]{:S(2)}, u32[]{:S(2)}) collective-permute-start(f32[3,128,128]{2,1,0:T(8,128)S(1)} %get-tuple-element.44.mine), channel_id=1, source_target_pairs={{0,32},{8,40},{16,48},{24,56},{32,0},{40,8},{48,16},{56,24},{64,96... | collective-permute-start | bytes 589832 | tf_op jit(solution)/shard_map/ppermute | solution.py:510
  57.1 3.7 %collective-permute-done.10.other.near_group = f32[3,128,128]{2,1,0:T(8,128)S(1)} collective-permute-done((f32[3,128,128]{2,1,0:T(8,128)S(1)}, f32[3,128,128]{2,1,0:T(8,128)S(1)}, u32[]{:S(2)}, u32[]{:S(2)}) %collective-permute-start.10) | collective-permute-done | bytes 196640 | tf_op jit(solution)/shard_map/ppermute | solution.py:510
  61.0 3.1 %collective-permute-start.11 = (f32[3,128,128]{2,1,0:T(8,128)S(1)}, f32[3,128,128]{2,1,0:T(8,128)S(1)}, u32[]{:S(2)}, u32[]{:S(2)}) collective-permute-start(f32[3,128,128]{2,1,0:T(8,128)S(1)} %pair.1), channel_id=1, source_target_pairs={{0,64},{8,72},{16,80},{24,88},{32,96},{40,104},{48,112},{56,120},{... | collective-permute-start | bytes 589832 | tf_op jit(solution)/shard_map/ppermute | solution.py:510
  64.1 8.5 %collective-permute-done.11.other.near_pair = f32[3,128,128]{2,1,0:T(8,128)S(1)} collective-permute-done((f32[3,128,128]{2,1,0:T(8,128)S(1)}, f32[3,128,128]{2,1,0:T(8,128)S(1)}, u32[]{:S(2)}, u32[]{:S(2)}) %collective-permute-start.11) | collective-permute-done | bytes 196640 | tf_op jit(solution)/shard_map/ppermute | solution.py:510
  72.8 6.4 %collective-permute-start.12 = (f32[128,128]{1,0:T(8,128)S(1)}, f32[128,128]{1,0:T(8,128)S(1)}, u32[]{:S(2)}, u32[]{:S(2)}) collective-permute-start(f32[128,128]{1,0:T(8,128)S(1)} %quad.1), channel_id=1, source_target_pairs={{0,128},{8,136},{16,144},{24,152},{32,160},{40,168},{48,176},{56,1... | collective-permute-start | bytes 196616 | tf_op jit(solution)/shard_map/ppermute | solution.py:510
  83.4 2.4 %collective-permute-start.15 = (f32[2,128,128]{2,1,0:T(8,128)S(1)}, f32[2,128,128]{2,1,0:T(8,128)S(1)}, u32[]{:S(2)}, u32[]{:S(2)}) collective-permute-start(f32[2,128,128]{2,1,0:T(8,128)S(1)} %get-tuple-element.48), channel_id=1, source_target_pairs={{0,24},{8,16},{16,8},{24,0},{32,56},{40,48},{48,40},{56,32},{64,88... | collective-permute-start | bytes 393224 | tf_op jit(solution)/shard_map/ppermute | solution.py:510
  85.8 2.2 %collective-permute-done.14.refs_9_ = f32[2,128,128]{2,1,0:T(8,128)S(1)} collective-permute-done((f32[2,128,128]{2,1,0:T(8,128)S(1)}, f32[2,128,128]{2,1,0:T(8,128)S(1)}, u32[]{:S(2)}, u32[]{:S(2)}) %collective-permute-start.14) | collective-permute-done | bytes 131104 | tf_op jit(solution)/shard_map/ppermute | solution.py:510
  88.0 2.5 %collective-permute-done.15.refs_10_ = f32[2,128,128]{2,1,0:T(8,128)S(1)} collective-permute-done((f32[2,128,128]{2,1,0:T(8,128)S(1)}, f32[2,128,128]{2,1,0:T(8,128)S(1)}, u32[]{:S(2)}, u32[]{:S(2)}) %collective-permute-start.15) | collective-permute-done | bytes 131104 | tf_op jit(solution)/shard_map/ppermute | solution.py:510
  90.5 6.0 %outputs.1 = (bf16[192,512]{1,0:T(8,128)(2,1)}, bf16[192,512]{1,0:T(8,128)(2,1)}, bf16[192,1024]{1,0:T(8,128)(2,1)}, bf16[192,1024]{1,0:T(8,128)(2,1)S(1)}, bf16[192,8]{1,0:T(8,128)(2,1)S(1)}) custom-call(f32[192,1024]{1,0:T(8,128)S(1)} %get-tuple-element.34.refs_0_, f32[192,8]{1,0:T(8,128)S(1)} %get-tuple-element.35.refs_1_, ...), custom_call_target="tpu_custom_call" | custom-call | tf_op jit(solution)/shard_map/outputs/pallas_call | solution.py:415
  98.2 2.0 %collective-permute-start.16 = (bf16[4,192,512]{2,1,0:T(8,128)(2,1)S(1)}, bf16[4,192,512]{2,1,0:T(8,128)(2,1)S(1)}, u32[]{:S(2)}, u32[]{:S(2)}) collective-permute-start(bf16[4,192,512]{2,1,0:T(8,128)(2,1)S(1)} %shares.2), channel_id=1, source_target_pairs={{0,1},{1,0},{2,3},{3,2},{4,5},{5,4},{6,7},{7,6},{8,9},{9,8},{10,11... | collective-permute-start | bytes 2359304 | tf_op jit(solution)/shard_map/ppermute | solution.py:510
  100.2 1.9 %collective-permute-done.16.refs_0_ = bf16[4,192,512]{2,1,0:T(8,128)(2,1)S(1)} collective-permute-done((bf16[4,192,512]{2,1,0:T(8,128)(2,1)S(1)}, bf16[4,192,512]{2,1,0:T(8,128)(2,1)S(1)}, u32[]{:S(2)}, u32[]{:S(2)}) %collective-permute-start.16) | collective-permute-done | bytes 786464 | tf_op jit(solution)/shard_map/ppermute | solution.py:510
  106.7 5.0 %collective-permute-done.17 = bf16[192,512]{1,0:T(8,128)(2,1)S(1)} collective-permute-done((bf16[192,512]{1,0:T(8,128)(2,1)S(1)}, bf16[192,512]{1,0:T(8,128)(2,1)S(1)}, u32[]{:S(2)}, u32[]{:S(2)}) %collective-permute-start.17) | collective-permute-done | bytes 196640 | tf_op jit(solution)/shard_map/ppermute | solution.py:510
  111.7 4.5 %collective-permute-done.19 = bf16[192,512]{1,0:T(8,128)(2,1)S(1)} collective-permute-done((bf16[192,512]{1,0:T(8,128)(2,1)S(1)}, bf16[192,512]{1,0:T(8,128)(2,1)S(1)}, u32[]{:S(2)}, u32[]{:S(2)}) %collective-permute-start.19) | collective-permute-done | bytes 196640 | tf_op jit(solution)/shard_map/ppermute | solution.py:510
  (42 shorter events, 23.1 us)
Async XLA Ops:
  0.6 8.0 %collective-permute-start.3 = (bf16[192,512]{1,0:T(8,128)(2,1)}, bf16[192,512]{1,0:T(8,128)(2,1)S(1)}, u32[]{:S(2)}, u32[]{:S(2)}) collective-permute-start(bf16[192,512]{1,0:T(8,128)(2,1)} %refs_0_.3), channel_id=1, source_target_pairs={{0,2},{1,3},{2,0},{3,1},{4,6},{5,7},{6,4},{7,5},{8,10},{9,11},{10,... | collective-permute-start | bytes 589832 | tf_op jit(solution)/shard_map/ppermute | solution.py:510
  2.8 11.2 %collective-permute-start.1 = (bf16[192,512]{1,0:T(8,128)(2,1)}, bf16[192,512]{1,0:T(8,128)(2,1)S(1)}, u32[]{:S(2)}, u32[]{:S(2)}) collective-permute-start(bf16[192,512]{1,0:T(8,128)(2,1)} %refs_0_.3), channel_id=1, source_target_pairs={{0,4},{1,5},{2,6},{3,7},{4,0},{5,1},{6,2},{7,3},{8,12},{9,13},{10,... | collective-permute-start | bytes 589832 | tf_op jit(solution)/shard_map/ppermute | solution.py:510
  5.2 11.4 %collective-permute-start.5 = (bf16[192,512]{1,0:T(8,128)(2,1)}, bf16[192,512]{1,0:T(8,128)(2,1)S(1)}, u32[]{:S(2)}, u32[]{:S(2)}) collective-permute-start(bf16[192,512]{1,0:T(8,128)(2,1)} %refs_0_.3), channel_id=1, source_target_pairs={{0,6},{1,7},{2,4},{3,5},{4,2},{5,3},{6,0},{7,1},{8,14},{9,15},{10,... | collective-permute-start | bytes 589832 | tf_op jit(solution)/shard_map/ppermute | solution.py:510
  5.3 21.4 %collective-permute-start = (bf16[192,512]{1,0:T(8,128)(2,1)}, bf16[192,512]{1,0:T(8,128)(2,1)S(1)}, u32[]{:S(2)}, u32[]{:S(2)}) collective-permute-start(bf16[192,512]{1,0:T(8,128)(2,1)} %refs_0_.3), channel_id=1, source_target_pairs={{0,1},{1,0},{2,3},{3,2},{4,5},{5,4},{6,7},{7,6},{8,9},{9,8},{10,11... | collective-permute-start | bytes 589832 | tf_op jit(solution)/shard_map/ppermute | solution.py:510
  8.7 18.0 %collective-permute-start.4 = (bf16[192,512]{1,0:T(8,128)(2,1)S(1)}, bf16[192,512]{1,0:T(8,128)(2,1)S(1)}, u32[]{:S(2)}, u32[]{:S(2)}) collective-permute-start(bf16[192,512]{1,0:T(8,128)(2,1)S(1)} %collective-permute-done.3.refs_4_), channel_id=1, source_target_pairs={{0,1},{1,0},{2,3},{3,2},{4,5},{5,4},{6,7},{7,6},{8,9},{9,8},{10,11... | collective-permute-start | bytes 589832 | tf_op jit(solution)/shard_map/ppermute | solution.py:510
  14.0 12.7 %collective-permute-start.2 = (bf16[192,512]{1,0:T(8,128)(2,1)S(1)}, bf16[192,512]{1,0:T(8,128)(2,1)S(1)}, u32[]{:S(2)}, u32[]{:S(2)}) collective-permute-start(bf16[192,512]{1,0:T(8,128)(2,1)S(1)} %collective-permute-done.1.refs_2_), channel_id=1, source_target_pairs={{0,1},{1,0},{2,3},{3,2},{4,5},{5,4},{6,7},{7,6},{8,9},{9,8},{10,11... | collective-permute-start | bytes 589832 | tf_op jit(solution)/shard_map/ppermute | solution.py:510
  16.7 10.0 %collective-permute-start.6 = (bf16[192,512]{1,0:T(8,128)(2,1)S(1)}, bf16[192,512]{1,0:T(8,128)(2,1)S(1)}, u32[]{:S(2)}, u32[]{:S(2)}) collective-permute-start(bf16[192,512]{1,0:T(8,128)(2,1)S(1)} %collective-permute-done.5.refs_6_), channel_id=1, source_target_pairs={{0,1},{1,0},{2,3},{3,2},{4,5},{5,4},{6,7},{7,6},{8,9},{9,8},{10,11... | collective-permute-start | bytes 589832 | tf_op jit(solution)/shard_map/ppermute | solution.py:510
  18.2 3.4 %copy-start = (bf16[4096,1024]{1,0:T(8,128)(2,1)S(1)}, bf16[4096,1024]{1,0:T(8,128)(2,1)}, u32[]{:S(2)}) copy-start(bf16[4096,1024]{1,0:T(8,128)(2,1)} %refs_0_.2) | copy-start | bytes 25165828
  21.5 1.0 copy-start.1
  25.2 1.4 %copy-start.4 = (bf16[192,512]{1,0:T(8,128)(2,1)S(1)}, bf16[192,512]{1,0:T(8,128)(2,1)}, u32[]{:S(2)}) copy-start(bf16[192,512]{1,0:T(8,128)(2,1)} %refs_0_.3) | copy-start | bytes 589828
  25.2 1.4 %copy-start.6 = (f32[8]{0:T(128)S(1)}, f32[8]{0:T(128)}, u32[]{:S(2)}) copy-start(f32[8]{0:T(128)} %param.10) | copy-start | bytes 100
  39.3 6.6 %collective-permute-start.7 = (f32[3,128,128]{2,1,0:T(8,128)S(1)}, f32[3,128,128]{2,1,0:T(8,128)S(1)}, u32[]{:S(2)}, u32[]{:S(2)}) collective-permute-start(f32[3,128,128]{2,1,0:T(8,128)S(1)} %get-tuple-element.40), channel_id=1, source_target_pairs={{0,8},{8,0},{16,24},{24,16},{32,40},{40,32},{48,56},{56,48},{64,72... | collective-permute-start | bytes 589832 | tf_op jit(solution)/shard_map/ppermute | solution.py:510
  40.6 12.0 %collective-permute-start.8 = (f32[3,128,128]{2,1,0:T(8,128)S(1)}, f32[3,128,128]{2,1,0:T(8,128)S(1)}, u32[]{:S(2)}, u32[]{:S(2)}) collective-permute-start(f32[3,128,128]{2,1,0:T(8,128)S(1)} %get-tuple-element.41), channel_id=1, source_target_pairs={{0,16},{8,24},{16,0},{24,8},{32,48},{40,56},{48,32},{56,40},{64,80... | collective-permute-start | bytes 589832 | tf_op jit(solution)/shard_map/ppermute | solution.py:510
  43.3 11.3 %collective-permute-start.9 = (f32[3,128,128]{2,1,0:T(8,128)S(1)}, f32[3,128,128]{2,1,0:T(8,128)S(1)}, u32[]{:S(2)}, u32[]{:S(2)}) collective-permute-start(f32[3,128,128]{2,1,0:T(8,128)S(1)} %get-tuple-element.42), channel_id=1, source_target_pairs={{0,24},{8,16},{16,8},{24,0},{32,56},{40,48},{48,40},{56,32},{64,88... | collective-permute-start | bytes 589832 | tf_op jit(solution)/shard_map/ppermute | solution.py:510
  55.4 5.4 %collective-permute-start.10 = (f32[3,128,128]{2,1,0:T(8,128)S(1)}, f32[3,128,128]{2,1,0:T(8,128)S(1)}, u32[]{:S(2)}, u32[]{:S(2)}) collective-permute-start(f32[3,128,128]{2,1,0:T(8,128)S(1)} %get-tuple-element.44.mine), channel_id=1, source_target_pairs={{0,32},{8,40},{16,48},{24,56},{32,0},{40,8},{48,16},{56,24},{64,96... | collective-permute-start | bytes 589832 | tf_op jit(solution)/shard_map/ppermute | solution.py:510
  61.0 11.6 %collective-permute-start.11 = (f32[3,128,128]{2,1,0:T(8,128)S(1)}, f32[3,128,128]{2,1,0:T(8,128)S(1)}, u32[]{:S(2)}, u32[]{:S(2)}) collective-permute-start(f32[3,128,128]{2,1,0:T(8,128)S(1)} %pair.1), channel_id=1, source_target_pairs={{0,64},{8,72},{16,80},{24,88},{32,96},{40,104},{48,112},{56,120},{... | collective-permute-start | bytes 589832 | tf_op jit(solution)/shard_map/ppermute | solution.py:510
  72.8 8.1 %collective-permute-start.12 = (f32[128,128]{1,0:T(8,128)S(1)}, f32[128,128]{1,0:T(8,128)S(1)}, u32[]{:S(2)}, u32[]{:S(2)}) collective-permute-start(f32[128,128]{1,0:T(8,128)S(1)} %quad.1), channel_id=1, source_target_pairs={{0,128},{8,136},{16,144},{24,152},{32,160},{40,168},{48,176},{56,1... | collective-permute-start | bytes 196616 | tf_op jit(solution)/shard_map/ppermute | solution.py:510
  81.9 3.9 %collective-permute-start.13 = (f32[2,128,128]{2,1,0:T(8,128)S(1)}, f32[2,128,128]{2,1,0:T(8,128)S(1)}, u32[]{:S(2)}, u32[]{:S(2)}) collective-permute-start(f32[2,128,128]{2,1,0:T(8,128)S(1)} %get-tuple-element.46), channel_id=1, source_target_pairs={{0,8},{8,0},{16,24},{24,16},{32,40},{40,32},{48,56},{56,48},{64,72... | collective-permute-start | bytes 393224 | tf_op jit(solution)/shard_map/ppermute | solution.py:510
  82.0 6.1 %collective-permute-start.14 = (f32[2,128,128]{2,1,0:T(8,128)S(1)}, f32[2,128,128]{2,1,0:T(8,128)S(1)}, u32[]{:S(2)}, u32[]{:S(2)}) collective-permute-start(f32[2,128,128]{2,1,0:T(8,128)S(1)} %get-tuple-element.47), channel_id=1, source_target_pairs={{0,16},{8,24},{16,0},{24,8},{32,48},{40,56},{48,32},{56,40},{64,80... | collective-permute-start | bytes 393224 | tf_op jit(solution)/shard_map/ppermute | solution.py:510
  83.4 7.1 %collective-permute-start.15 = (f32[2,128,128]{2,1,0:T(8,128)S(1)}, f32[2,128,128]{2,1,0:T(8,128)S(1)}, u32[]{:S(2)}, u32[]{:S(2)}) collective-permute-start(f32[2,128,128]{2,1,0:T(8,128)S(1)} %get-tuple-element.48), channel_id=1, source_target_pairs={{0,24},{8,16},{16,8},{24,0},{32,56},{40,48},{48,40},{56,32},{64,88... | collective-permute-start | bytes 393224 | tf_op jit(solution)/shard_map/ppermute | solution.py:510
  98.2 3.9 %collective-permute-start.16 = (bf16[4,192,512]{2,1,0:T(8,128)(2,1)S(1)}, bf16[4,192,512]{2,1,0:T(8,128)(2,1)S(1)}, u32[]{:S(2)}, u32[]{:S(2)}) collective-permute-start(bf16[4,192,512]{2,1,0:T(8,128)(2,1)S(1)} %shares.2), channel_id=1, source_target_pairs={{0,1},{1,0},{2,3},{3,2},{4,5},{5,4},{6,7},{7,6},{8,9},{9,8},{10,11... | collective-permute-start | bytes 2359304 | tf_op jit(solution)/shard_map/ppermute | solution.py:510
  104.0 7.8 %collective-permute-start.17 = (bf16[192,512]{1,0:T(8,128)(2,1)S(1)}, bf16[192,512]{1,0:T(8,128)(2,1)S(1)}, u32[]{:S(2)}, u32[]{:S(2)}) collective-permute-start(bf16[192,512]{1,0:T(8,128)(2,1)S(1)} %get-tuple-element.54), channel_id=1, source_target_pairs={{0,4},{1,5},{2,6},{3,7},{4,0},{5,1},{6,2},{7,3},{8,12},{9,13},{10,... | collective-permute-start | bytes 589832 | tf_op jit(solution)/shard_map/ppermute | solution.py:510
  104.1 12.1 %collective-permute-start.19 = (bf16[192,512]{1,0:T(8,128)(2,1)S(1)}, bf16[192,512]{1,0:T(8,128)(2,1)S(1)}, u32[]{:S(2)}, u32[]{:S(2)}) collective-permute-start(bf16[192,512]{1,0:T(8,128)(2,1)S(1)} %get-tuple-element.55), channel_id=1, source_target_pairs={{0,6},{1,7},{2,4},{3,5},{4,2},{5,3},{6,0},{7,1},{8,14},{9,15},{10,... | collective-permute-start | bytes 589832 | tf_op jit(solution)/shard_map/ppermute | solution.py:510
  105.2 11.0 %collective-permute-start.18 = (bf16[192,512]{1,0:T(8,128)(2,1)S(1)}, bf16[192,512]{1,0:T(8,128)(2,1)S(1)}, u32[]{:S(2)}, u32[]{:S(2)}) collective-permute-start(bf16[192,512]{1,0:T(8,128)(2,1)S(1)} %get-tuple-element.56), channel_id=1, source_target_pairs={{0,2},{1,3},{2,0},{3,1},{4,6},{5,7},{6,4},{7,5},{8,10},{9,11},{10,... | collective-permute-start | bytes 589832 | tf_op jit(solution)/shard_map/ppermute | solution.py:510
  (3 other events, 2.7 us)

commit v3 on v2

--- a/solution.py
+++ b/solution.py
@@ -10,6 +10,8 @@
 F32 = jnp.float32
 BF16 = jnp.bfloat16
 SPAN = 64
+TAIL = 16
+PEAK = 14.0
 INNER = 4
 VMEM_BYTES = 24 * 1024 * 1024
 FETCH_BYTES = 16 * 1024 * 1024
@@ -285,24 +287,49 @@
             pushes[head, i] = mine[1][i]
             for part in range(3):
                 moves[head, part, i] = mine[2 + part][i]
-        for part, array in enumerate(chained(*mine[2:])):
-            totals[head, part] = array
+        pack(totals.at[head], 1, chained(*mine[2:]))
     for mask, whole in enumerate(wholes):
         whole[...] = totals[place ^ mask]
 
 
-def parts_of(ref):
-    return [ref[part] for part in range(3)]
+def pack(ref, bounded, matrices):
+    side = matrices[0].shape[0]
+    tail = side * len(matrices)
+    if len(matrices) > bounded:
+        ref[tail:, :] = jnp.zeros((ref.shape[0] - tail, ref.shape[1]), F32)
+    for part, matrix in enumerate(matrices):
+        exponent = jnp.zeros((1, 1), F32)
+        if part >= bounded:
+            peak = jnp.max(jnp.abs(matrix), axis=(0, 1), keepdims=True)
+            exponent = jnp.clip(jnp.ceil(jnp.log2(jnp.maximum(peak, 1e-30))), -99.0, 99.0)
+            row = tail + 8 * (part - bounded)
+            ref[row : row + 8, :] = jnp.broadcast_to(exponent, (8, ref.shape[1]))
+        ref[part * side : (part + 1) * side, :] = matrix * jnp.exp2(PEAK - exponent)
+
+
+def unpack(ref, bounded, count):
+    side = ref.shape[1]
+    matrices = []
+    for part in range(count):
+        exponent = 0.0
+        if part >= bounded:
+            row = side * count + 8 * (part - bounded)
+            exponent = ref[row : row + 1, :]
+        factor = jnp.exp2(jnp.zeros((1, side), F32) + exponent - PEAK)
+        matrices.append(ref[part * side : (part + 1) * side, :] * factor)
+    return matrices
 
 
 def join_kernel(*refs):
-    arrived, (spans, total) = refs[:-2], refs[-2:]
+    arrived, (spans, total, packed) = refs[:-3], refs[-3:]
     place = lax.rem(lax.axis_index("ctx"), INNER)
     for mask, ref in enumerate(arrived):
-        spans[place ^ mask] = ref[...]
+        for part, matrix in enumerate(unpack(ref, 1, 3)):
+            spans[place ^ mask, part] = matrix
     found = chained(*[[spans[i, part] for i in range(len(arrived))] for part in range(3)])
     for part in range(3):
         total[part] = found[part]
+    pack(packed, 1, found)
 
 
 def wider(mine, other, upper):
@@ -311,37 +338,40 @@
     return chained(*[list(pair) for pair in zip(first, second)])
 
 
-def pair_kernel(mine, other, total):
+def pair_kernel(mine, other, total, packed):
     upper = lax.rem(lax.div(lax.axis_index("ctx"), INNER), 2) == 1
-    found = wider(parts_of(mine), parts_of(other), upper)
+    found = wider([mine[part] for part in range(3)], unpack(other, 1, 3), upper)
     for part in range(3):
         total[part] = found[part]
-
-
-def quad_kernel(pair, other, total):
+    pack(packed, 1, found)
+
+
+def quad_kernel(pair, other, packed):
     group = lax.div(lax.axis_index("ctx"), INNER)
-    found = wider(parts_of(pair), parts_of(other), lax.rem(lax.div(group, 2), 2) == 1)
-    total[...] = jnp.where(group < 4, found[1], found[2])
+    upper = lax.rem(lax.div(group, 2), 2) == 1
+    found = wider([pair[part] for part in range(3)], unpack(other, 1, 3), upper)
+    pack(packed, 0, [jnp.where(group < 4, found[1], found[2])])
 
 
 def scan_kernel(spans, near_group, near_pair, far_half, *refs):
     outputs, entering = refs[:-1], refs[-1]
     position = lax.axis_index("ctx")
     group, place = lax.div(position, INNER), lax.rem(position, INNER)
-    nothing = jnp.zeros(far_half.shape, F32)
-    state = jnp.where(group >= 4, far_half[...], nothing)
-    returning = jnp.where(group < 4, far_half[...], nothing)
+    (far,) = unpack(far_half, 0, 1)
+    nothing = jnp.zeros_like(far)
+    state = jnp.where(group >= 4, far, nothing)
+    returning = jnp.where(group < 4, far, nothing)
     for ref, above in ((near_pair, lax.rem(lax.div(group, 2), 2)), (near_group, lax.rem(group, 2))):
-        transition = halves(ref[0])
-        state = jnp.where(above == 1, fine(transition, state) + ref[1], state)
-        returning = jnp.where(above == 0, fine(returning, transition) + ref[2], returning)
+        transition, offset, pull = unpack(ref, 1, 3)
+        transition = halves(transition)
+        state = jnp.where(above == 1, fine(transition, state) + offset, state)
+        returning = jnp.where(above == 0, fine(returning, transition) + pull, returning)
     count = spans.shape[0]
     states, returned = entered(
         *[[spans[i, part] for i in range(count)] for part in range(3)], state, returning
     )
     for i in range(count):
-        entering[i, 0] = states[i]
-        entering[i, 1] = returned[i]
+        pack(entering.at[i], 0, [states[i], returned[i]])
     for mask, output in enumerate(outputs):
         output[...] = entering[place ^ mask]
 
@@ -356,7 +386,8 @@
     blocks = queries.shape[0] // SPAN
     each = range(blocks)
     for mask, ref in enumerate(arrived):
-        entering[place ^ mask] = ref[...]
+        for part, matrix in enumerate(unpack(ref, 0, 2)):
+            entering[place ^ mask, part] = matrix
     around = [
         entered(
             *[[moves[head, part, i] for i in each] for part in range(3)],
@@ -408,6 +439,10 @@
 
 def shape_of(*shape, dtype=F32):
     return jax.ShapeDtypeStruct(shape, dtype)
+
+
+def packed_shape(count, width):
+    return shape_of(count * width + TAIL, width)
 
 
 def call(kernel, name, out_shape, *operands, scratch=(), specs=None, limit=VMEM_BYTES, cost=None):
@@ -454,7 +489,7 @@
             shape_of(heads, blocks, keys, 2 * width),
             shape_of(heads, 3, blocks, width, width),
         ]
-        + [shape_of(3, width, width)] * heads,
+        + [packed_shape(3, width)] * heads,
         *pieces,
         key_weight,
         beta_across,
@@ -462,7 +497,7 @@
         queries,
         values,
         out_grad,
-        scratch=[pltpu.VMEM((heads, 3, width, width), F32)],
+        scratch=[pltpu.VMEM((heads, 3 * width + TAIL, width), F32)],
     )
 
 
@@ -510,46 +545,51 @@
     return lax.ppermute(value, axis, [(i, i ^ mask) for i in range(lax.axis_size(axis))])
 
 
+def swapped16(packed, axis, mask):
+    return swapped(packed.astype(jnp.float16), axis, mask).astype(F32)
+
+
 def per_device(inputs, key_weight, beta_weight, beta_bias, queries, values, out_grad):
     heads = beta_bias.shape[0] // 2
     width = queries.shape[1] // heads
     chips = lax.axis_size("head") // 2
     beta_across = jnp.swapaxes(beta_weight, 0, 1)
 
-    key_weight, beta_across, queries, values, out_grad = fetch(
-        key_weight, beta_across, queries, values, out_grad
-    )
+    fetched = fetch(key_weight, beta_across, queries, values, out_grad)
     masks, pieces = [0, 1], [inputs, swapped(inputs, "head", 1)]
+    far = {chip: swapped(inputs, "head", 2 * chip) for chip in (2, 1, 3)}
     for chip in (2, 1, 3):
-        piece = swapped(inputs, "head", 2 * chip)
+        piece, fetched = lax.optimization_barrier((far[chip], fetched))
         masks += [2 * chip, 2 * chip + 1]
         pieces += [piece, swapped(piece, "head", 1)]
+    key_weight, beta_across, queries, values, out_grad = fetched
     key_proj, logits, mixes, pushes, moves, *wholes = project(
         masks, pieces, key_weight, beta_across, beta_bias[None], queries, values, out_grad
     )
 
-    arrived = [wholes[0]] + [swapped(wholes[mask], "ctx", mask) for mask in range(1, INNER)]
-    square = (width, width)
-    spans, group = call(
-        join_kernel,
-        "join", [shape_of(INNER, 3, *square), shape_of(3, *square)], *arrived
-    )
-    near_group = swapped(group, "ctx", INNER)
-    pair = call(pair_kernel, "pair", shape_of(3, *square), group, near_group)
-    near_pair = swapped(pair, "ctx", 2 * INNER)
-    quad = call(quad_kernel, "quad", shape_of(*square), pair, near_pair)
-    far_half = swapped(quad, "ctx", 4 * INNER)
+    arrived = [wholes[0]] + [swapped16(wholes[mask], "ctx", mask) for mask in (2, 1, 3)]
+    arrived = [arrived[i] for i in (0, 2, 1, 3)]
+    whole, packed = shape_of(3, width, width), packed_shape(3, width)
+    spans, group, sent = call(
+        join_kernel, "join", [shape_of(INNER, 3, width, width), whole, packed], *arrived
+    )
+    near_group = swapped16(sent, "ctx", INNER)
+    pair, sent = call(pair_kernel, "pair", [whole, packed], group, near_group)
+    near_pair = swapped16(sent, "ctx", 2 * INNER)
+    quad = call(quad_kernel, "quad", packed_shape(1, width), pair, near_pair)
+    far_half = swapped16(quad, "ctx", 4 * INNER)
     entering = call(
         scan_kernel,
         "scan",
-        [shape_of(2, *square)] * INNER,
+        [packed_shape(2, width)] * INNER,
         spans,
         near_group,
         near_pair,
         far_half,
-        scratch=[pltpu.VMEM((INNER, 2, *square), F32)],
-    )
-    arrived = [entering[0]] + [swapped(entering[mask], "ctx", mask) for mask in range(1, INNER)]
+        scratch=[pltpu.VMEM((INNER, 2 * width + TAIL, width), F32)],
+    )
+    arrived = [entering[0]] + [swapped16(entering[mask], "ctx", mask) for mask in (2, 1, 3)]
+    arrived = [arrived[i] for i in (0, 2, 1, 3)]
 
     mixed, query_grad, value_grad, key_cot, logit_cot = finish(
         key_proj, logits, queries, out_grad, mixes, pushes, moves, arrived

time: 117 us -> 97.1 us (0.83)
  waiting for transfers between devices: 45.1 us -> 28.5 us
  starting transfers between devices: 37.6 us -> 33.2 us
    ppermute x20, waiting for transfers between devices: 45.1 us -> 28.5 us  [swapped(): lax.ppermute(value, axis, [(i, i ^ mask) for i in range(lax.axis_size(axi...]
    ppermute x20, starting transfers between devices: 37.6 us -> 33.2 us  [swapped(): lax.ppermute(value, axis, [(i, i ^ mask) for i in range(lax.axis_size(axi...]
where the time goes in v3:
time: 97.1 us; the launch traced here: 96.8 us
  starting transfers between devices  33.2 us (34%)
  waiting for transfers between devices  28.5 us (29%)
  Pallas kernels  26.1 us (27%)
  local copies, waits for them, and re-layouts  7.12 us (7%)
  other arithmetic  1.14 us (1%)
    ppermute x20, starting transfers between devices, swapped(): lax.ppermute(value, axis, [(i, i ^ mask) for i in range(lax.axis_size(axi...  33.2 us
    ppermute x20, waiting for transfers between devices, swapped(): lax.ppermute(value, axis, [(i, i ^ mask) for i in range(lax.axis_size(axi...  28.5 us
    pallas_call x9, Pallas kernels, call(): pl.pallas_call(kernel, in_specs=specs or [VMEM] * len(operands), out_spec...  26.1 us
    unnamed x14, local copies, waits for them, and re-layouts  7.08 us
  transfers between devices with their start and end apart: 20, of which 13 were waited for; matrix products, arithmetic and copies ran while one was open for 0% of the time, Pallas kernels for 1%

profile of v3, /device:TPU:1, one launch (start us, length us, event | category | flops | bytes accessed | tf_op | source)
XLA Modules:
  0.0 96.8 jit_solution(2158094742339007300)
XLA Ops:
  0.6 3.7 %collective-permute-start.1 = (bf16[192,512]{1,0:T(8,128)(2,1)}, bf16[192,512]{1,0:T(8,128)(2,1)S(1)}, u32[]{:S(2)}, u32[]{:S(2)}) collective-permute-start(bf16[192,512]{1,0:T(8,128)(2,1)} %refs_0_.3), channel_id=1, source_target_pairs={{0,4},{1,5},{2,6},{3,7},{4,0},{5,1},{6,2},{7,3},{8,12},{9,13},{10,... | collective-permute-start | bytes 589832 | tf_op jit(solution)/shard_map/ppermute | solution.py:545
  5.2 2.9 %collective-permute-start = (bf16[192,512]{1,0:T(8,128)(2,1)}, bf16[192,512]{1,0:T(8,128)(2,1)S(1)}, u32[]{:S(2)}, u32[]{:S(2)}) collective-permute-start(bf16[192,512]{1,0:T(8,128)(2,1)} %refs_0_.3), channel_id=1, source_target_pairs={{0,1},{1,0},{2,3},{3,2},{4,5},{5,4},{6,7},{7,6},{8,9},{9,8},{10,11... | collective-permute-start | bytes 589832 | tf_op jit(solution)/shard_map/ppermute | solution.py:545
  8.1 3.4 %copy-done = bf16[4096,1024]{1,0:T(8,128)(2,1)S(1)} copy-done((bf16[4096,1024]{1,0:T(8,128)(2,1)S(1)}, bf16[4096,1024]{1,0:T(8,128)(2,1)}, u32[]{:S(2)}) %copy-start) | copy-done | bytes 8388632
  15.1 1.4 %fetch.1 = (bf16[4096,1024]{1,0:T(8,128)(2,1)S(1)}, bf16[8,4096]{1,0:T(8,128)(2,1)S(1)}, bf16[192,512]{1,0:T(8,128)(2,1)S(1)}, bf16[192,1024]{1,0:T(8,128)(2,1)S(1)}, bf16[192,512]{1,0:T(8,128)(2,1)S(1)}) custom-call(bf16[4096,1024]{1,0:T(8,128)(2,1)S(1)} %copy-done, bf16[8,4096]{1,0:T(8,128)(2,1)S(1)} %bitcast.18, bf16[192,512]{1,0:T(8,128)(2,1)S(1)} %copy-done.2, ...), custom_call_target="tpu_custom_call" | custom-call | bytes 18481152 | tf_op jit(solution)/shard_map/fetch/pallas_call | solution.py:450
  18.6 12.6 %project.1 = (f32[192,1024]{1,0:T(8,128)S(1)}, f32[192,8]{1,0:T(8,128)S(1)}, f32[4,3,128,256]{3,2,1,0:T(8,128)S(1)}, f32[4,3,128,256]{3,2,1,0:T(8,128)S(1)}, f32...) custom-call(bf16[192,512]{1,0:T(8,128)(2,1)S(1)} %copy-done.4, ...), custom_call_target="tpu_custom_call" | custom-call | tf_op jit(solution)/shard_map/project/pallas_call | solution.py:450
  31.3 1.2 %collective-permute-start.9 = (f16[400,128]{1,0:T(8,128)(2,1)S(1)}, f16[400,128]{1,0:T(8,128)(2,1)S(1)}, u32[]{:S(2)}, u32[]{:S(2)}) collective-permute-start(f16[400,128]{1,0:T(8,128)(2,1)S(1)} %convert_element_type.82), channel_id=1, source_target_pairs={{0,24},{8,16},{16,8},{24,0},{32,56},{40,48},{48,40},{56,32},{64,88... | collective-permute-start | bytes 307208 | tf_op jit(solution)/shard_map/ppermute | solution.py:545
  32.9 2.1 %collective-permute-start.7 = (f16[400,128]{1,0:T(8,128)(2,1)S(1)}, f16[400,128]{1,0:T(8,128)(2,1)S(1)}, u32[]{:S(2)}, u32[]{:S(2)}) collective-permute-start(f16[400,128]{1,0:T(8,128)(2,1)S(1)} %convert_element_type.78), channel_id=1, source_target_pairs={{0,8},{8,0},{16,24},{24,16},{32,40},{40,32},{48,56},{56,48},{64,72... | collective-permute-start | bytes 307208 | tf_op jit(solution)/shard_map/ppermute | solution.py:545
  35.0 3.2 %collective-permute-done.9 = f16[400,128]{1,0:T(8,128)(2,1)S(1)} collective-permute-done((f16[400,128]{1,0:T(8,128)(2,1)S(1)}, f16[400,128]{1,0:T(8,128)(2,1)S(1)}, u32[]{:S(2)}, u32[]{:S(2)}) %collective-permute-start.9) | collective-permute-done | bytes 102432 | tf_op jit(solution)/shard_map/ppermute | solution.py:545
  40.7 3.2 %collective-permute-done.10 = f16[400,128]{1,0:T(8,128)(2,1)S(1)} collective-permute-done((f16[400,128]{1,0:T(8,128)(2,1)S(1)}, f16[400,128]{1,0:T(8,128)(2,1)S(1)}, u32[]{:S(2)}, u32[]{:S(2)}) %collective-permute-start.10) | collective-permute-done | bytes 102432 | tf_op jit(solution)/shard_map/ppermute | solution.py:545
  44.3 1.9 %collective-permute-start.11 = (f16[400,128]{1,0:T(8,128)(2,1)S(1)}, f16[400,128]{1,0:T(8,128)(2,1)S(1)}, u32[]{:S(2)}, u32[]{:S(2)}) collective-permute-start(f16[400,128]{1,0:T(8,128)(2,1)S(1)} %convert_element_type.86), channel_id=1, source_target_pairs={{0,64},{8,72},{16,80},{24,88},{32,96},{40,104},{48,112},{56,120},{... | collective-permute-start | bytes 307208 | tf_op jit(solution)/shard_map/ppermute | solution.py:545
  46.3 3.6 %collective-permute-done.11 = f16[400,128]{1,0:T(8,128)(2,1)S(1)} collective-permute-done((f16[400,128]{1,0:T(8,128)(2,1)S(1)}, f16[400,128]{1,0:T(8,128)(2,1)S(1)}, u32[]{:S(2)}, u32[]{:S(2)}) %collective-permute-start.11) | collective-permute-done | bytes 102432 | tf_op jit(solution)/shard_map/ppermute | solution.py:545
  50.3 5.7 %collective-permute-start.12 = (f16[144,128]{1,0:T(8,128)(2,1)S(1)}, f16[144,128]{1,0:T(8,128)(2,1)S(1)}, u32[]{:S(2)}, u32[]{:S(2)}) collective-permute-start(f16[144,128]{1,0:T(8,128)(2,1)S(1)} %convert_element_type.88), channel_id=1, source_target_pairs={{0,128},{8,136},{16,144},{24,152},{32,160},{40,168},{48,176},{56,1... | collective-permute-start | bytes 110600 | tf_op jit(solution)/shard_map/ppermute | solution.py:545
  56.0 1.6 %collective-permute-done.12 = f16[144,128]{1,0:T(8,128)(2,1)S(1)} collective-permute-done((f16[144,128]{1,0:T(8,128)(2,1)S(1)}, f16[144,128]{1,0:T(8,128)(2,1)S(1)}, u32[]{:S(2)}, u32[]{:S(2)}) %collective-permute-start.12) | collective-permute-done | bytes 36896 | tf_op jit(solution)/shard_map/ppermute | solution.py:545
  57.6 1.1 %scan.1 = (f32[272,128]{1,0:T(8,128)S(1)}, f32[272,128]{1,0:T(8,128)S(1)}, f32[272,128]{1,0:T(8,128)S(1)}, f32[272,128]{1,0:T(8,128)S(1)}) custom-call(f32[4,3,128,128]{3,2,1,0:T(8,128)S(1)} %get-tuple-element.82.spans, f32[400,128]{1,0:T(8,128)S(1)} %convert_element_type.85.other.near_group, f32[400,128]{1,0:T(8,128)S(1)} %convert_element_type.87.other.near_pair, ...), custom_call_target="tpu_custom_call" | custom-call | tf_op jit(solution)/shard_map/scan/pallas_call | solution.py:450
  58.7 2.2 %collective-permute-start.15 = (f16[272,128]{1,0:T(8,128)(2,1)S(1)}, f16[272,128]{1,0:T(8,128)(2,1)S(1)}, u32[]{:S(2)}, u32[]{:S(2)}) collective-permute-start(f16[272,128]{1,0:T(8,128)(2,1)S(1)} %convert_element_type.94), channel_id=1, source_target_pairs={{0,24},{8,16},{16,8},{24,0},{32,56},{40,48},{48,40},{56,32},{64,88... | collective-permute-start | bytes 208904 | tf_op jit(solution)/shard_map/ppermute | solution.py:545
  63.2 2.4 %collective-permute-done.14 = f16[272,128]{1,0:T(8,128)(2,1)S(1)} collective-permute-done((f16[272,128]{1,0:T(8,128)(2,1)S(1)}, f16[272,128]{1,0:T(8,128)(2,1)S(1)}, u32[]{:S(2)}, u32[]{:S(2)}) %collective-permute-start.14) | collective-permute-done | bytes 69664 | tf_op jit(solution)/shard_map/ppermute | solution.py:545
  65.6 6.0 %outputs.1 = (bf16[192,512]{1,0:T(8,128)(2,1)}, bf16[192,512]{1,0:T(8,128)(2,1)}, bf16[192,1024]{1,0:T(8,128)(2,1)}, bf16[192,1024]{1,0:T(8,128)(2,1)S(1)}, bf16[192,8]{1,0:T(8,128)(2,1)S(1)}) custom-call(f32[192,1024]{1,0:T(8,128)S(1)} %get-tuple-element.73.refs_0_, f32[192,8]{1,0:T(8,128)S(1)} %get-tuple-element.74.refs_1_, ...), custom_call_target="tpu_custom_call" | custom-call | tf_op jit(solution)/shard_map/outputs/pallas_call | solution.py:450
  71.7 1.7 %shares.2 = bf16[4,192,512]{2,1,0:T(8,128)(2,1)S(1)} custom-call(bf16[192,1024]{1,0:T(8,128)(2,1)S(1)} %get-tuple-element.94.key_cot, bf16[192,8]{1,0:T(8,128)(2,1)S(1)} %get-tuple-element.95.logit_cot, bf16[4096,1024]{1,0:T(8,128)(2,1)S(1)} %get-tuple-element.68.refs_8_.key_weight, bf16[8,4096]{1,0:T(8,128)(2,1)S(1)} %get-tuple-element.69.refs_9_.beta_weight), custom_call_target="tpu_custom_call" | custom-call | tf_op jit(solution)/shard_map/shares/pallas_call | solution.py:450
  73.4 6.3 %collective-permute-start.16 = (bf16[4,192,512]{2,1,0:T(8,128)(2,1)S(1)}, bf16[4,192,512]{2,1,0:T(8,128)(2,1)S(1)}, u32[]{:S(2)}, u32[]{:S(2)}) collective-permute-start(bf16[4,192,512]{2,1,0:T(8,128)(2,1)S(1)} %shares.2), channel_id=1, source_target_pairs={{0,1},{1,0},{2,3},{3,2},{4,5},{5,4},{6,7},{7,6},{8,9},{9,8},{10,11... | collective-permute-start | bytes 2359304 | tf_op jit(solution)/shard_map/ppermute | solution.py:545
  79.7 1.9 %collective-permute-done.16.refs_0_ = bf16[4,192,512]{2,1,0:T(8,128)(2,1)S(1)} collective-permute-done((bf16[4,192,512]{2,1,0:T(8,128)(2,1)S(1)}, bf16[4,192,512]{2,1,0:T(8,128)(2,1)S(1)}, u32[]{:S(2)}, u32[]{:S(2)}) %collective-permute-start.16) | collective-permute-done | bytes 786464 | tf_op jit(solution)/shard_map/ppermute | solution.py:545
  81.6 1.7 %shares.3 = f32[4,192,512]{2,1,0:T(8,128)S(1)} custom-call(bf16[192,1024]{1,0:T(8,128)(2,1)S(1)} %get-tuple-element.94.key_cot, bf16[192,8]{1,0:T(8,128)(2,1)S(1)} %get-tuple-element.95.logit_cot, bf16[4096,1024]{1,0:T(8,128)(2,1)S(1)} %get-tuple-element.68.refs_8_.key_weight, bf16[8,4096]{1,0:T(8,128)(2,1)S(1)} %get-tuple-element.69.refs_9_.beta_weight, ...), custom_call_target="tpu_custom_call" | custom-call | tf_op jit(solution)/shard_map/shares/pallas_call | solution.py:450
  83.4 2.8 %collective-permute-start.17 = (bf16[192,512]{1,0:T(8,128)(2,1)S(1)}, bf16[192,512]{1,0:T(8,128)(2,1)S(1)}, u32[]{:S(2)}, u32[]{:S(2)}) collective-permute-start(bf16[192,512]{1,0:T(8,128)(2,1)S(1)} %get-tuple-element.96), channel_id=1, source_target_pairs={{0,4},{1,5},{2,6},{3,7},{4,0},{5,1},{6,2},{7,3},{8,12},{9,13},{10,... | collective-permute-start | bytes 589832 | tf_op jit(solution)/shard_map/ppermute | solution.py:545
  87.0 4.1 %collective-permute-done.17 = bf16[192,512]{1,0:T(8,128)(2,1)S(1)} collective-permute-done((bf16[192,512]{1,0:T(8,128)(2,1)S(1)}, bf16[192,512]{1,0:T(8,128)(2,1)S(1)}, u32[]{:S(2)}, u32[]{:S(2)}) %collective-permute-start.17) | collective-permute-done | bytes 196640 | tf_op jit(solution)/shard_map/ppermute | solution.py:545
  91.1 4.9 %collective-permute-done.19 = bf16[192,512]{1,0:T(8,128)(2,1)S(1)} collective-permute-done((bf16[192,512]{1,0:T(8,128)(2,1)S(1)}, bf16[192,512]{1,0:T(8,128)(2,1)S(1)}, u32[]{:S(2)}, u32[]{:S(2)}) %collective-permute-start.19) | collective-permute-done | bytes 196640 | tf_op jit(solution)/shard_map/ppermute | solution.py:545
  (60 shorter events, 14.3 us)
Async XLA Ops:
  0.6 15.9 %collective-permute-start.1 = (bf16[192,512]{1,0:T(8,128)(2,1)}, bf16[192,512]{1,0:T(8,128)(2,1)S(1)}, u32[]{:S(2)}, u32[]{:S(2)}) collective-permute-start(bf16[192,512]{1,0:T(8,128)(2,1)} %refs_0_.3), channel_id=1, source_target_pairs={{0,4},{1,5},{2,6},{3,7},{4,0},{5,1},{6,2},{7,3},{8,12},{9,13},{10,... | collective-permute-start | bytes 589832 | tf_op jit(solution)/shard_map/ppermute | solution.py:545
  4.3 12.2 %collective-permute-start.3 = (bf16[192,512]{1,0:T(8,128)(2,1)}, bf16[192,512]{1,0:T(8,128)(2,1)S(1)}, u32[]{:S(2)}, u32[]{:S(2)}) collective-permute-start(bf16[192,512]{1,0:T(8,128)(2,1)} %refs_0_.3), channel_id=1, source_target_pairs={{0,2},{1,3},{2,0},{3,1},{4,6},{5,7},{6,4},{7,5},{8,10},{9,11},{10,... | collective-permute-start | bytes 589832 | tf_op jit(solution)/shard_map/ppermute | solution.py:545
  4.6 11.9 %collective-permute-start.5 = (bf16[192,512]{1,0:T(8,128)(2,1)}, bf16[192,512]{1,0:T(8,128)(2,1)S(1)}, u32[]{:S(2)}, u32[]{:S(2)}) collective-permute-start(bf16[192,512]{1,0:T(8,128)(2,1)} %refs_0_.3), channel_id=1, source_target_pairs={{0,6},{1,7},{2,4},{3,5},{4,2},{5,3},{6,0},{7,1},{8,14},{9,15},{10,... | collective-permute-start | bytes 589832 | tf_op jit(solution)/shard_map/ppermute | solution.py:545
  5.2 12.1 %collective-permute-start = (bf16[192,512]{1,0:T(8,128)(2,1)}, bf16[192,512]{1,0:T(8,128)(2,1)S(1)}, u32[]{:S(2)}, u32[]{:S(2)}) collective-permute-start(bf16[192,512]{1,0:T(8,128)(2,1)} %refs_0_.3), channel_id=1, source_target_pairs={{0,1},{1,0},{2,3},{3,2},{4,5},{5,4},{6,7},{7,6},{8,9},{9,8},{10,11... | collective-permute-start | bytes 589832 | tf_op jit(solution)/shard_map/ppermute | solution.py:545
  8.1 3.4 %copy-start = (bf16[4096,1024]{1,0:T(8,128)(2,1)S(1)}, bf16[4096,1024]{1,0:T(8,128)(2,1)}, u32[]{:S(2)}) copy-start(bf16[4096,1024]{1,0:T(8,128)(2,1)} %refs_0_.2) | copy-start | bytes 25165828
  11.4 1.0 %copy-start.1 = (bf16[192,1024]{1,0:T(8,128)(2,1)S(1)}, bf16[192,1024]{1,0:T(8,128)(2,1)}, u32[]{:S(2)}) copy-start(bf16[192,1024]{1,0:T(8,128)(2,1)} %refs_3_.1) | copy-start | bytes 1179652
  15.1 3.5 %copy-start.4 = (bf16[192,512]{1,0:T(8,128)(2,1)S(1)}, bf16[192,512]{1,0:T(8,128)(2,1)}, u32[]{:S(2)}) copy-start(bf16[192,512]{1,0:T(8,128)(2,1)} %refs_0_.3) | copy-start | bytes 589828
  15.1 3.5 %copy-start.6 = (f32[8]{0:T(128)S(1)}, f32[8]{0:T(128)}, u32[]{:S(2)}) copy-start(f32[8]{0:T(128)} %param.10) | copy-start | bytes 100
  16.6 1.5 %collective-permute-start.6 = (bf16[192,512]{1,0:T(8,128)(2,1)S(1)}, bf16[192,512]{1,0:T(8,128)(2,1)S(1)}, u32[]{:S(2)}, u32[]{:S(2)}) collective-permute-start(bf16[192,512]{1,0:T(8,128)(2,1)S(1)} %collective-permute-done.5.refs_6_), channel_id=1, source_target_pairs={{0,1},{1,0},{2,3},{3,2},{4,5},{5,4},{6,7},{7,6},{8,9},{9,8},{10,11... | collective-permute-start | bytes 589832 | tf_op jit(solution)/shard_map/ppermute | solution.py:545
  16.7 1.7 %collective-permute-start.4 = (bf16[192,512]{1,0:T(8,128)(2,1)S(1)}, bf16[192,512]{1,0:T(8,128)(2,1)S(1)}, u32[]{:S(2)}, u32[]{:S(2)}) collective-permute-start(bf16[192,512]{1,0:T(8,128)(2,1)S(1)} %collective-permute-done.3.refs_4_), channel_id=1, source_target_pairs={{0,1},{1,0},{2,3},{3,2},{4,5},{5,4},{6,7},{7,6},{8,9},{9,8},{10,11... | collective-permute-start | bytes 589832 | tf_op jit(solution)/shard_map/ppermute | solution.py:545
  17.1 1.5 %collective-permute-start.2 = (bf16[192,512]{1,0:T(8,128)(2,1)S(1)}, bf16[192,512]{1,0:T(8,128)(2,1)S(1)}, u32[]{:S(2)}, u32[]{:S(2)}) collective-permute-start(bf16[192,512]{1,0:T(8,128)(2,1)S(1)} %collective-permute-done.1.refs_2_), channel_id=1, source_target_pairs={{0,1},{1,0},{2,3},{3,2},{4,5},{5,4},{6,7},{7,6},{8,9},{9,8},{10,11... | collective-permute-start | bytes 589832 | tf_op jit(solution)/shard_map/ppermute | solution.py:545
  31.3 6.9 %collective-permute-start.9 = (f16[400,128]{1,0:T(8,128)(2,1)S(1)}, f16[400,128]{1,0:T(8,128)(2,1)S(1)}, u32[]{:S(2)}, u32[]{:S(2)}) collective-permute-start(f16[400,128]{1,0:T(8,128)(2,1)S(1)} %convert_element_type.82), channel_id=1, source_target_pairs={{0,24},{8,16},{16,8},{24,0},{32,56},{40,48},{48,40},{56,32},{64,88... | collective-permute-start | bytes 307208 | tf_op jit(solution)/shard_map/ppermute | solution.py:545
  32.5 5.8 %collective-permute-start.8 = (f16[400,128]{1,0:T(8,128)(2,1)S(1)}, f16[400,128]{1,0:T(8,128)(2,1)S(1)}, u32[]{:S(2)}, u32[]{:S(2)}) collective-permute-start(f16[400,128]{1,0:T(8,128)(2,1)S(1)} %convert_element_type.80), channel_id=1, source_target_pairs={{0,16},{8,24},{16,0},{24,8},{32,48},{40,56},{48,32},{56,40},{64,80... | collective-permute-start | bytes 307208 | tf_op jit(solution)/shard_map/ppermute | solution.py:545
  32.9 6.5 %collective-permute-start.7 = (f16[400,128]{1,0:T(8,128)(2,1)S(1)}, f16[400,128]{1,0:T(8,128)(2,1)S(1)}, u32[]{:S(2)}, u32[]{:S(2)}) collective-permute-start(f16[400,128]{1,0:T(8,128)(2,1)S(1)} %convert_element_type.78), channel_id=1, source_target_pairs={{0,8},{8,0},{16,24},{24,16},{32,40},{40,32},{48,56},{56,48},{64,72... | collective-permute-start | bytes 307208 | tf_op jit(solution)/shard_map/ppermute | solution.py:545
  40.3 3.6 %collective-permute-start.10 = (f16[400,128]{1,0:T(8,128)(2,1)S(1)}, f16[400,128]{1,0:T(8,128)(2,1)S(1)}, u32[]{:S(2)}, u32[]{:S(2)}) collective-permute-start(f16[400,128]{1,0:T(8,128)(2,1)S(1)} %convert_element_type.84), channel_id=1, source_target_pairs={{0,32},{8,40},{16,48},{24,56},{32,0},{40,8},{48,16},{56,24},{64,96... | collective-permute-start | bytes 307208 | tf_op jit(solution)/shard_map/ppermute | solution.py:545
  44.3 5.6 %collective-permute-start.11 = (f16[400,128]{1,0:T(8,128)(2,1)S(1)}, f16[400,128]{1,0:T(8,128)(2,1)S(1)}, u32[]{:S(2)}, u32[]{:S(2)}) collective-permute-start(f16[400,128]{1,0:T(8,128)(2,1)S(1)} %convert_element_type.86), channel_id=1, source_target_pairs={{0,64},{8,72},{16,80},{24,88},{32,96},{40,104},{48,112},{56,120},{... | collective-permute-start | bytes 307208 | tf_op jit(solution)/shard_map/ppermute | solution.py:545
  50.3 7.3 %collective-permute-start.12 = (f16[144,128]{1,0:T(8,128)(2,1)S(1)}, f16[144,128]{1,0:T(8,128)(2,1)S(1)}, u32[]{:S(2)}, u32[]{:S(2)}) collective-permute-start(f16[144,128]{1,0:T(8,128)(2,1)S(1)} %convert_element_type.88), channel_id=1, source_target_pairs={{0,128},{8,136},{16,144},{24,152},{32,160},{40,168},{48,176},{56,1... | collective-permute-start | bytes 110600 | tf_op jit(solution)/shard_map/ppermute | solution.py:545
  58.7 4.5 %collective-permute-start.15 = (f16[272,128]{1,0:T(8,128)(2,1)S(1)}, f16[272,128]{1,0:T(8,128)(2,1)S(1)}, u32[]{:S(2)}, u32[]{:S(2)}) collective-permute-start(f16[272,128]{1,0:T(8,128)(2,1)S(1)} %convert_element_type.94), channel_id=1, source_target_pairs={{0,24},{8,16},{16,8},{24,0},{32,56},{40,48},{48,40},{56,32},{64,88... | collective-permute-start | bytes 208904 | tf_op jit(solution)/shard_map/ppermute | solution.py:545
  60.9 4.7 %collective-permute-start.14 = (f16[272,128]{1,0:T(8,128)(2,1)S(1)}, f16[272,128]{1,0:T(8,128)(2,1)S(1)}, u32[]{:S(2)}, u32[]{:S(2)}) collective-permute-start(f16[272,128]{1,0:T(8,128)(2,1)S(1)} %convert_element_type.92), channel_id=1, source_target_pairs={{0,16},{8,24},{16,0},{24,8},{32,48},{40,56},{48,32},{56,40},{64,80... | collective-permute-start | bytes 208904 | tf_op jit(solution)/shard_map/ppermute | solution.py:545
  61.3 4.3 %collective-permute-start.13 = (f16[272,128]{1,0:T(8,128)(2,1)S(1)}, f16[272,128]{1,0:T(8,128)(2,1)S(1)}, u32[]{:S(2)}, u32[]{:S(2)}) collective-permute-start(f16[272,128]{1,0:T(8,128)(2,1)S(1)} %convert_element_type.90), channel_id=1, source_target_pairs={{0,8},{8,0},{16,24},{24,16},{32,40},{40,32},{48,56},{56,48},{64,72... | collective-permute-start | bytes 208904 | tf_op jit(solution)/shard_map/ppermute | solution.py:545
  73.4 8.2 %collective-permute-start.16 = (bf16[4,192,512]{2,1,0:T(8,128)(2,1)S(1)}, bf16[4,192,512]{2,1,0:T(8,128)(2,1)S(1)}, u32[]{:S(2)}, u32[]{:S(2)}) collective-permute-start(bf16[4,192,512]{2,1,0:T(8,128)(2,1)S(1)} %shares.2), channel_id=1, source_target_pairs={{0,1},{1,0},{2,3},{3,2},{4,5},{5,4},{6,7},{7,6},{8,9},{9,8},{10,11... | collective-permute-start | bytes 2359304 | tf_op jit(solution)/shard_map/ppermute | solution.py:545
  83.4 7.7 %collective-permute-start.17 = (bf16[192,512]{1,0:T(8,128)(2,1)S(1)}, bf16[192,512]{1,0:T(8,128)(2,1)S(1)}, u32[]{:S(2)}, u32[]{:S(2)}) collective-permute-start(bf16[192,512]{1,0:T(8,128)(2,1)S(1)} %get-tuple-element.96), channel_id=1, source_target_pairs={{0,4},{1,5},{2,6},{3,7},{4,0},{5,1},{6,2},{7,3},{8,12},{9,13},{10,... | collective-permute-start | bytes 589832 | tf_op jit(solution)/shard_map/ppermute | solution.py:545
  86.2 9.9 %collective-permute-start.19 = (bf16[192,512]{1,0:T(8,128)(2,1)S(1)}, bf16[192,512]{1,0:T(8,128)(2,1)S(1)}, u32[]{:S(2)}, u32[]{:S(2)}) collective-permute-start(bf16[192,512]{1,0:T(8,128)(2,1)S(1)} %get-tuple-element.97), channel_id=1, source_target_pairs={{0,6},{1,7},{2,4},{3,5},{4,2},{5,3},{6,0},{7,1},{8,14},{9,15},{10,... | collective-permute-start | bytes 589832 | tf_op jit(solution)/shard_map/ppermute | solution.py:545
  87.0 9.0 %collective-permute-start.18 = (bf16[192,512]{1,0:T(8,128)(2,1)S(1)}, bf16[192,512]{1,0:T(8,128)(2,1)S(1)}, u32[]{:S(2)}, u32[]{:S(2)}) collective-permute-start(bf16[192,512]{1,0:T(8,128)(2,1)S(1)} %get-tuple-element.98), channel_id=1, source_target_pairs={{0,2},{1,3},{2,0},{3,1},{4,6},{5,7},{6,4},{7,5},{8,10},{9,11},{10,... | collective-permute-start | bytes 589832 | tf_op jit(solution)/shard_map/ppermute | solution.py:545
  (3 other events, 2.7 us)

commit v4 on v3

--- a/solution.py
+++ b/solution.py
@@ -10,11 +10,12 @@
 F32 = jnp.float32
 BF16 = jnp.bfloat16
 SPAN = 64
+GROUPS = ((1, 2, 3), (0,))
 TAIL = 16
 PEAK = 14.0
 INNER = 4
 VMEM_BYTES = 24 * 1024 * 1024
-FETCH_BYTES = 16 * 1024 * 1024
+FETCH_BYTES = 44 * 1024 * 1024
 
 
 def product(left, right, over_left=1, over_right=0):
@@ -38,19 +39,33 @@
 def fine(left, right, over_left=1, over_right=0):
     left_high, left_low = halves(left)
     right_high, right_low = halves(right)
-    lefts, rights = [left_high], [right_high]
-    if left_low is not None:
-        lefts.append(left_low)
-        rights.append(right_high)
-    if right_low is not None:
-        lefts.append(left_high)
-        rights.append(right_low)
-    return product(
-        jnp.concatenate(lefts, axis=over_left),
-        jnp.concatenate(rights, axis=over_right),
-        over_left,
-        over_right,
-    )
+    def joined(lefts, rights):
+        return product(
+            jnp.concatenate(lefts, axis=over_left),
+            jnp.concatenate(rights, axis=over_right),
+            over_left,
+            over_right,
+        )
+
+    if left_low is None and right_low is None:
+        return product(left_high, right_high, over_left, over_right)
+    if right_low is None:
+        return joined([left_high, left_low], [right_high, right_high])
+    if left_low is None:
+        return joined([left_high, left_high], [right_high, right_low])
+    columns = right_high.shape[1 - over_right]
+    if columns > 128:
+        return joined([left_high, left_low, left_high], [right_high, right_high, right_low])
+    beside = [
+        jnp.concatenate([right_high, right_low], axis=1 - over_right),
+        jnp.concatenate([right_high, jnp.zeros_like(right_low)], axis=1 - over_right),
+    ]
+    total = joined([left_high, left_low], beside)
+    return total[:, :columns] + total[:, columns:]
+
+
+def plain(left, right, over_left=1, over_right=0):
+    return product(halves(left)[0], halves(right)[0], over_left, over_right)
 
 
 def block_times(axis, shape):
@@ -208,7 +223,7 @@
 
 
 def head_rows(ref, head, width):
-    lanes = slice(head * width, (head + 1) * width)
+    lanes = pl.ds(pl.multiple_of(head * width, width), width)
     return [ref[i : i + SPAN, lanes] for i in range(0, ref.shape[0], SPAN)]
 
 
@@ -224,15 +239,22 @@
 
 
 def head_rates(logits, head):
-    rates = 2.0 * jax.nn.sigmoid(logits[:, 2 * head : 2 * head + 2])
+    lane = lax.broadcasted_iota(jnp.int32, logits.shape, 1)
+    rates = [
+        2.0
+        * jax.nn.sigmoid(
+            jnp.sum(jnp.where(lane == 2 * head + key, logits, 0.0), axis=1, keepdims=True)
+        )
+        for key in range(2)
+    ]
     return [
-        jnp.concatenate([rates[i : i + SPAN, :1], rates[i : i + SPAN, 1:]], axis=0)
+        jnp.concatenate([rate[i : i + SPAN] for rate in rates], axis=0)
         for i in range(0, logits.shape[0], SPAN)
     ]
 
 
-def each_head(heads, of):
-    return [part for head in range(heads) for part in of(head)]
+def each_of(members, of):
+    return [part for member in members for part in of(member)]
 
 
 def fetch_kernel(*refs):
@@ -248,48 +270,46 @@
         copy.wait()
 
 
-def project_kernel(masks, *refs):
+def project_kernel(masks, slots, *refs):
     pieces = refs[: len(masks)]
     (key_weight, beta_weight, beta_bias, queries, values, out_grad) = refs[
         len(masks) : len(masks) + 6
     ]
-    (key_proj, logits, mixes, pushes, moves) = refs[len(masks) + 6 : len(masks) + 11]
-    wholes, totals = refs[len(masks) + 11 : -1], refs[-1]
-    heads = len(wholes)
+    (key_proj, logits, mixes, pushes, moves, *wholes) = refs[len(masks) + 6 :]
     depth = pieces[0].shape[1]
-    width = queries.shape[1] // heads
+    width = moves.shape[-1]
     blocks = queries.shape[0] // SPAN
     me = lax.axis_index("head")
     place = lax.rem(lax.axis_index("ctx"), INNER)
+    heads = [place ^ slot for slot in slots]
     starts = [pl.multiple_of((me ^ mask) * depth, depth) for mask in masks]
 
     total = beta_bias[...]
     for piece, start in zip(pieces, starts):
         total = total + product(piece[...], beta_weight[:, pl.ds(start, depth)], 1, 1)
     logits[...] = total
-    for head in range(heads):
-        wide = slice(2 * head * width, 2 * (head + 1) * width)
+    for near, head in enumerate(heads):
+        wide = pl.ds(pl.multiple_of(head * 2 * width, 2 * width), 2 * width)
         total = product(pieces[0][...], key_weight[pl.ds(starts[0], depth), wide])
         for piece, start in zip(pieces[1:], starts[1:]):
             total = total + product(piece[...], key_weight[pl.ds(start, depth), wide])
-        key_proj[:, wide] = total
+        key_proj[:, 2 * near * width : 2 * (near + 1) * width] = total
+    rates = logits[...]
     found = local_blocks(
-        each_head(heads, lambda head: head_pairs(key_proj, head, width)),
-        each_head(heads, lambda head: head_rates(logits, head)),
-        each_head(heads, lambda head: head_pairs(values, head, width)),
-        each_head(heads, lambda head: head_rows(queries, head, width)),
-        each_head(heads, lambda head: head_rows(out_grad, head, width)),
-    )
-    for head in range(heads):
-        mine = [arrays[head * blocks : (head + 1) * blocks] for arrays in found]
+        each_of(range(len(slots)), lambda near: head_pairs(key_proj, near, width)),
+        each_of(heads, lambda head: head_rates(rates, head)),
+        each_of(heads, lambda head: head_pairs(values, head, width)),
+        each_of(heads, lambda head: head_rows(queries, head, width)),
+        each_of(heads, lambda head: head_rows(out_grad, head, width)),
+    )
+    for near, whole in enumerate(wholes):
+        mine = [arrays[near * blocks : (near + 1) * blocks] for arrays in found]
         for i in range(blocks):
-            mixes[head, i] = mine[0][i]
-            pushes[head, i] = mine[1][i]
+            mixes[near, i] = mine[0][i]
+            pushes[near, i] = mine[1][i]
             for part in range(3):
-                moves[head, part, i] = mine[2 + part][i]
-        pack(totals.at[head], 1, chained(*mine[2:]))
-    for mask, whole in enumerate(wholes):
-        whole[...] = totals[place ^ mask]
+                moves[near, part, i] = mine[2 + part][i]
+        pack(whole, 1, chained(*mine[2:]))
 
 
 def pack(ref, bounded, matrices):
@@ -376,62 +396,73 @@
         output[...] = entering[place ^ mask]
 
 
-def outputs_kernel(*refs):
-    (key_proj, logits, queries, out_grad, mixes, pushes, moves) = refs[:7]
-    arrived = refs[7 : 7 + INNER]
-    (mixed, query_grad, value_grad, key_cot, logit_cot, entering) = refs[7 + INNER :]
-    heads = moves.shape[0]
+def outputs_kernel(groups, *refs):
+    logits, queries, out_grad = refs[:3]
+    (mixed, query_grad, value_grad, key_cot, logit_cot) = refs[-5:]
+    width = refs[-6].shape[1]
     place = lax.rem(lax.axis_index("ctx"), INNER)
-    width = queries.shape[1] // heads
     blocks = queries.shape[0] // SPAN
     each = range(blocks)
-    for mask, ref in enumerate(arrived):
-        for part, matrix in enumerate(unpack(ref, 0, 2)):
-            entering[place ^ mask, part] = matrix
-    around = [
-        entered(
-            *[[moves[head, part, i] for i in each] for part in range(3)],
-            entering[head, 0],
-            entering[head, 1],
-        )
-        for head in range(heads)
-    ]
+    heads, key_rows, mixes, pushes, states, returning = [], [], [], [], [], []
+    at = 3
+    for slots in groups:
+        key_proj, mix, push, moves = refs[at : at + 4]
+        arrived = refs[at + 4 : at + 4 + len(slots)]
+        at += 4 + len(slots)
+        heads += [place ^ slot for slot in slots]
+        for near in range(len(slots)):
+            key_rows += head_pairs(key_proj, near, width)
+            mixes += [mix[near, i] for i in each]
+            pushes += [push[near, i] for i in each]
+            around = entered(
+                *[[moves[near, part, i] for i in each] for part in range(3)],
+                *unpack(arrived[near], 0, 2),
+            )
+            states += around[0]
+            returning += around[1]
+    rates = logits[...]
     found = full_blocks(
-        each_head(heads, lambda head: head_pairs(key_proj, head, width)),
-        each_head(heads, lambda head: head_rates(logits, head)),
-        each_head(heads, lambda head: head_rows(queries, head, width)),
-        each_head(heads, lambda head: head_rows(out_grad, head, width)),
-        each_head(heads, lambda head: [mixes[head, i] for i in each]),
-        each_head(heads, lambda head: [pushes[head, i] for i in each]),
-        each_head(heads, lambda head: around[head][0]),
-        each_head(heads, lambda head: around[head][1]),
-    )
-    for head in range(heads):
-        lanes = slice(head * width, (head + 1) * width)
-        wide = slice(2 * head * width, 2 * (head + 1) * width)
+        key_rows,
+        each_of(heads, lambda head: head_rates(rates, head)),
+        each_of(heads, lambda head: head_rows(queries, head, width)),
+        each_of(heads, lambda head: head_rows(out_grad, head, width)),
+        mixes,
+        pushes,
+        states,
+        returning,
+    )
+    lane = lax.broadcasted_iota(jnp.int32, (SPAN, logits.shape[1]), 1)
+    columns = [jnp.zeros((SPAN, logits.shape[1]), F32) for _ in each]
+    for near, head in enumerate(heads):
+        lanes = pl.ds(pl.multiple_of(head * width, width), width)
+        wide = pl.ds(pl.multiple_of(head * 2 * width, 2 * width), 2 * width)
         for i in each:
             rows = slice(i * SPAN, (i + 1) * SPAN)
-            block = head * blocks + i
+            block = near * blocks + i
             mixed[rows, lanes] = found[0][block].astype(BF16)
             query_grad[rows, lanes] = found[1][block].astype(BF16)
             value_grad[rows, wide] = unpaired(found[2][block]).astype(BF16)
             key_cot[rows, wide] = unpaired(found[3][block]).astype(BF16)
+            cot = found[4][block]
+            columns[i] = jnp.where(lane == 2 * head, cot[:SPAN], columns[i])
+            columns[i] = jnp.where(lane == 2 * head + 1, cot[SPAN:], columns[i])
     for i in each:
-        columns = [unpaired(found[4][head * blocks + i]) for head in range(heads)]
-        logit_cot[i * SPAN : (i + 1) * SPAN, :] = jnp.concatenate(columns, axis=1).astype(BF16)
-
-
-def shares_kernel(core, key_cot, logit_cot, key_weight, beta_weight, *refs):
-    output = refs[-1]
+        logit_cot[i * SPAN : (i + 1) * SPAN, :] = columns[i].astype(BF16)
+
+
+def shares_kernel(core, key_cot, logit_cot, key_weight, beta_weight, output):
     depth = output.shape[2]
     me = lax.axis_index("head")
     for chip in range(output.shape[0]):
         start = pl.multiple_of((me ^ (2 * chip + core)) * depth, depth)
         total = product(key_cot[...], key_weight[pl.ds(start, depth), :], 1, 1)
         total = total + product(logit_cot[...], beta_weight[:, pl.ds(start, depth)])
-        if len(refs) > 1:
-            total = total + refs[0][chip].astype(F32)
         output[chip] = total.astype(output.dtype)
+
+
+def add_kernel(own, away, *outputs):
+    for chip, output in enumerate(outputs):
+        output[...] = (own[chip] + away[chip].astype(F32)).astype(output.dtype)
 
 
 VMEM = pl.BlockSpec(memory_space=pltpu.VMEM)
@@ -474,22 +505,22 @@
     )
 
 
-def project(masks, pieces, key_weight, beta_across, beta_bias, queries, values, out_grad):
+def project(masks, slots, pieces, key_weight, beta_across, beta_bias, queries, values, out_grad):
     rows = pieces[0].shape[0]
     heads = beta_bias.shape[1] // 2
     width = queries.shape[1] // heads
-    blocks, keys = rows // SPAN, 2 * SPAN
-    return call(
-        functools.partial(project_kernel, masks),
+    blocks, keys, count = rows // SPAN, 2 * SPAN, len(slots)
+    key_proj, logits, mixes, pushes, moves, *wholes = call(
+        functools.partial(project_kernel, masks, slots),
         "project",
         [
-            shape_of(rows, 2 * heads * width),
+            shape_of(rows, 2 * count * width),
             shape_of(rows, 2 * heads),
-            shape_of(heads, blocks, keys, 2 * width),
-            shape_of(heads, blocks, keys, 2 * width),
-            shape_of(heads, 3, blocks, width, width),
+            shape_of(count, blocks, keys, 2 * width),
+            shape_of(count, blocks, keys, 2 * width),
+            shape_of(count, 3, blocks, width, width),
         ]
-        + [packed_shape(3, width)] * heads,
+        + [packed_shape(3, width)] * count,
         *pieces,
         key_weight,
         beta_across,
@@ -497,16 +528,19 @@
         queries,
         values,
         out_grad,
-        scratch=[pltpu.VMEM((heads, 3 * width + TAIL, width), F32)],
-    )
-
-
-def finish(key_proj, logits, queries, out_grad, mixes, pushes, moves, arrived):
+    )
+    return logits, (key_proj, mixes, pushes, moves), wholes
+
+
+def finish(logits, queries, out_grad, groups, locals_of, arrived):
     rows = queries.shape[0]
     heads = logits.shape[1] // 2
     width = queries.shape[1] // heads
+    operands = []
+    for slots, local in zip(groups, locals_of):
+        operands += [*local, *[arrived[slot] for slot in slots]]
     return call(
-        outputs_kernel,
+        functools.partial(outputs_kernel, groups),
         "outputs",
         [
             shape_of(rows, heads * width, dtype=BF16),
@@ -515,19 +549,14 @@
             shape_of(rows, 2 * heads * width, dtype=BF16),
             shape_of(rows, 2 * heads, dtype=BF16),
         ],
-        key_proj,
         logits,
         queries,
         out_grad,
-        mixes,
-        pushes,
-        moves,
-        *arrived,
-        scratch=[pltpu.VMEM((heads, 2, width, width), F32)],
-    )
-
-
-def shares(core, chips, key_cot, logit_cot, key_weight, beta_across, dtype, *more):
+        *operands,
+    )
+
+
+def shares(core, chips, key_cot, logit_cot, key_weight, beta_across, dtype):
     depth = key_weight.shape[0] // (2 * chips)
     return call(
         functools.partial(shares_kernel, core),
@@ -537,7 +566,6 @@
         logit_cot,
         key_weight,
         beta_across,
-        *more,
     )
 
 
@@ -563,21 +591,23 @@
         masks += [2 * chip, 2 * chip + 1]
         pieces += [piece, swapped(piece, "head", 1)]
     key_weight, beta_across, queries, values, out_grad = fetched
-    key_proj, logits, mixes, pushes, moves, *wholes = project(
-        masks, pieces, key_weight, beta_across, beta_bias[None], queries, values, out_grad
-    )
-
-    arrived = [wholes[0]] + [swapped16(wholes[mask], "ctx", mask) for mask in (2, 1, 3)]
-    arrived = [arrived[i] for i in (0, 2, 1, 3)]
+    local, arrived = {}, {}
+    for slots in GROUPS:
+        logits, local[slots], wholes = project(
+            masks, slots, pieces, key_weight, beta_across, beta_bias[None], queries, values, out_grad
+        )
+        for slot, whole in zip(slots, wholes):
+            arrived[slot] = swapped16(whole, "ctx", slot) if slot else whole
+
     whole, packed = shape_of(3, width, width), packed_shape(3, width)
     spans, group, sent = call(
-        join_kernel, "join", [shape_of(INNER, 3, width, width), whole, packed], *arrived
+        join_kernel, "join", [shape_of(INNER, 3, width, width), whole, packed], *[arrived[i] for i in range(INNER)]
     )
     near_group = swapped16(sent, "ctx", INNER)
     pair, sent = call(pair_kernel, "pair", [whole, packed], group, near_group)
     near_pair = swapped16(sent, "ctx", 2 * INNER)
     quad = call(quad_kernel, "quad", packed_shape(1, width), pair, near_pair)
-    far_half = swapped16(quad, "ctx", 4 * INNER)
+    far_half = swapped16(quad, "ctx", 7 * INNER)
     entering = call(
         scan_kernel,
         "scan",
@@ -588,19 +618,26 @@
         far_half,
         scratch=[pltpu.VMEM((INNER, 2 * width + TAIL, width), F32)],
     )
-    arrived = [entering[0]] + [swapped16(entering[mask], "ctx", mask) for mask in (2, 1, 3)]
-    arrived = [arrived[i] for i in (0, 2, 1, 3)]
+    arrived = {0: entering[0]}
+    for slot in (2, 1, 3):
+        arrived[slot] = swapped16(entering[slot], "ctx", slot)
 
     mixed, query_grad, value_grad, key_cot, logit_cot = finish(
-        key_proj, logits, queries, out_grad, mixes, pushes, moves, arrived
+        logits, queries, out_grad, GROUPS, [local[slots] for slots in GROUPS], arrived
     )
 
     operands = (chips, key_cot, logit_cot, key_weight, beta_across)
     away = swapped(shares(1, *operands, BF16), "head", 1)
-    own = shares(0, *operands, F32, away)
-    total = own[0]
+    own = shares(0, *operands, F32)
+    total, *sent = call(
+        add_kernel,
+        "add",
+        [shape_of(*own.shape[1:])] + [shape_of(*own.shape[1:], dtype=BF16)] * (chips - 1),
+        own,
+        away,
+    )
     for chip in (2, 1, 3):
-        total = total + swapped(own[chip].astype(BF16), "head", 2 * chip).astype(F32)
+        total = total + swapped(sent[chip - 1], "head", 2 * chip).astype(F32)
     return mixed, query_grad, value_grad, total.astype(BF16)
 
 

time: 97.1 us -> 91.1 us (0.938)
  waiting for transfers between devices: 28.5 us -> 21.3 us
  local copies, waits for them, and re-layouts: 7.12 us -> 3.69 us
  Pallas kernels: 26.1 us -> 28.5 us
  starting transfers between devices: 33.2 us -> 35.5 us
    ppermute x20, waiting for transfers between devices: 28.5 us -> 21.3 us  [swapped(): lax.ppermute(value, axis, [(i, i ^ mask) for i in range(lax.axis_size(axi...]
    unnamed x14 -> x12, local copies, waits for them, and re-layouts: 7.08 us -> 3.69 us
    pallas_call x9 -> x11, Pallas kernels: 26.1 us -> 28.5 us  [call(): pl.pallas_call(kernel, in_specs=specs or [VMEM] * len(operands), out_spec...]
    ppermute x20, starting transfers between devices: 33.2 us -> 35.5 us  [swapped(): lax.ppermute(value, axis, [(i, i ^ mask) for i in range(lax.axis_size(axi...]
  transfers between devices with their start and end apart: 20 -> 20, of which waited for: 13 -> 13; matrix products, arithmetic and copies ran while one was open for 0% -> 0% of each run, Pallas kernels for 1% -> 11%
where the time goes in v4:
time: 91.1 us; the launch traced here: 90.9 us
  starting transfers between devices  35.5 us (39%)
  Pallas kernels  28.5 us (31%)
  waiting for transfers between devices  21.3 us (23%)
  local copies, waits for them, and re-layouts  3.69 us (4%)
  other arithmetic  1.03 us (1%)
    ppermute x20, starting transfers between devices, swapped(): lax.ppermute(value, axis, [(i, i ^ mask) for i in range(lax.axis_size(axi...  35.5 us
    pallas_call x11, Pallas kernels, call(): pl.pallas_call(kernel, in_specs=specs or [VMEM] * len(operands), out_spec...  28.5 us
    ppermute x20, waiting for transfers between devices, swapped(): lax.ppermute(value, axis, [(i, i ^ mask) for i in range(lax.axis_size(axi...  21.3 us
    unnamed x12, local copies, waits for them, and re-layouts  3.69 us
  transfers between devices with their start and end apart: 20, of which 13 were waited for; matrix products, arithmetic and copies ran while one was open for 0% of the time, Pallas kernels for 11%

profile of v4, /device:TPU:1, one launch (start us, length us, event | category | flops | bytes accessed | tf_op | source)
XLA Modules:
  0.0 90.9 jit_solution(4570086997753418940)
XLA Ops:
  0.6 3.7 %collective-permute-start.1 = (bf16[192,512]{1,0:T(8,128)(2,1)}, bf16[192,512]{1,0:T(8,128)(2,1)S(1)}, u32[]{:S(2)}, u32[]{:S(2)}) collective-permute-start(bf16[192,512]{1,0:T(8,128)(2,1)} %refs_0_.5), channel_id=1, source_target_pairs={{0,4},{1,5},{2,6},{3,7},{4,0},{5,1},{6,2},{7,3},{8,12},{9,13},{10,... | collective-permute-start | bytes 589832 | tf_op jit(solution)/shard_map/ppermute | solution.py:573
  5.2 2.9 %collective-permute-start = (bf16[192,512]{1,0:T(8,128)(2,1)}, bf16[192,512]{1,0:T(8,128)(2,1)S(1)}, u32[]{:S(2)}, u32[]{:S(2)}) collective-permute-start(bf16[192,512]{1,0:T(8,128)(2,1)} %refs_0_.5), channel_id=1, source_target_pairs={{0,1},{1,0},{2,3},{3,2},{4,5},{5,4},{6,7},{7,6},{8,9},{9,8},{10,11... | collective-permute-start | bytes 589832 | tf_op jit(solution)/shard_map/ppermute | solution.py:573
  8.1 1.0 %copy-done.1 = bf16[192,1024]{1,0:T(8,128)(2,1)S(1)} copy-done((bf16[192,1024]{1,0:T(8,128)(2,1)S(1)}, bf16[192,1024]{1,0:T(8,128)(2,1)}, u32[]{:S(2)}) %copy-start.1) | copy-done | bytes 393240
  11.8 3.5 %fetch.1 = (bf16[4096,1024]{1,0:T(8,128)(2,1)S(1)}, bf16[8,4096]{1,0:T(8,128)(2,1)S(1)}, bf16[192,512]{1,0:T(8,128)(2,1)S(1)}, bf16[192,1024]{1,0:T(8,128)(2,1)S(1)}, bf16[192,512]{1,0:T(8,128)(2,1)S(1)}) custom-call(bf16[4096,1024]{1,0:T(8,128)(2,1)} %refs_0_.3, bf16[8,4096]{1,0:T(8,128)(2,1)S(1)} %bitcast.2, bf16[192,512]{1,0:T(8,128)(2,1)S(1)} %copy-done.2, ...), custom_call_target="tpu_custom_call" | custom-call | bytes 18481152 | tf_op jit(solution)/shard_map/fetch/pallas_call | solution.py:481
  17.4 9.0 %project.3 = (f32[192,768]{1,0:T(8,128)S(1)}, f32[192,8]{1,0:T(8,128)}, f32[3,3,128,256]{3,2,1,0:T(8,128)S(1)}, f32[3,3,128,256]{3,2,1,0:T(8,128)S(1)}, f32[3,3,...) custom-call(bf16[192,512]{1,0:T(8,128)(2,1)S(1)} %copy-done, ...), custom_call_target="tpu_custom_call" | custom-call | tf_op jit(solution)/shard_map/project/pallas_call | solution.py:481
  27.1 2.9 %collective-permute-start.8 = (f16[400,128]{1,0:T(8,128)(2,1)S(1)}, f16[400,128]{1,0:T(8,128)(2,1)S(1)}, u32[]{:S(2)}, u32[]{:S(2)}) collective-permute-start(f16[400,128]{1,0:T(8,128)(2,1)S(1)} %convert_element_type.68), channel_id=1, source_target_pairs={{0,16},{8,24},{16,0},{24,8},{32,48},{40,56},{48,32},{56,40},{64,80... | collective-permute-start | bytes 307208 | tf_op jit(solution)/shard_map/ppermute | solution.py:573
  30.7 4.9 %project.2 = (f32[192,256]{1,0:T(8,128)S(1)}, f32[192,8]{1,0:T(8,128)S(1)}, f32[1,3,128,256]{3,2,1,0:T(8,128)S(1)}, f32[1,3,128,256]{3,2,1,0:T(8,128)S(1)}, f32[...) custom-call(bf16[192,512]{1,0:T(8,128)(2,1)S(1)} %copy-done, bf16[192,512]{1,0:T(8,128)(2,1)S(1)} %collective-permute-done.refs_1_, ...), custom_call_target="tpu_custom_call" | custom-call | tf_op jit(solution)/shard_map/project/pallas_call | solution.py:481
  35.7 1.7 %collective-permute-done.9 = f16[400,128]{1,0:T(8,128)(2,1)S(1)} collective-permute-done((f16[400,128]{1,0:T(8,128)(2,1)S(1)}, f16[400,128]{1,0:T(8,128)(2,1)S(1)}, u32[]{:S(2)}, u32[]{:S(2)}) %collective-permute-start.9) | collective-permute-done | bytes 102432 | tf_op jit(solution)/shard_map/ppermute | solution.py:573
  38.3 1.7 %collective-permute-start.10 = (f16[400,128]{1,0:T(8,128)(2,1)S(1)}, f16[400,128]{1,0:T(8,128)(2,1)S(1)}, u32[]{:S(2)}, u32[]{:S(2)}) collective-permute-start(f16[400,128]{1,0:T(8,128)(2,1)S(1)} %convert_element_type.72), channel_id=1, source_target_pairs={{0,32},{8,40},{16,48},{24,56},{32,0},{40,8},{48,16},{56,24},{64,96... | collective-permute-start | bytes 307208 | tf_op jit(solution)/shard_map/ppermute | solution.py:573
  40.0 2.7 %collective-permute-done.10 = f16[400,128]{1,0:T(8,128)(2,1)S(1)} collective-permute-done((f16[400,128]{1,0:T(8,128)(2,1)S(1)}, f16[400,128]{1,0:T(8,128)(2,1)S(1)}, u32[]{:S(2)}, u32[]{:S(2)}) %collective-permute-start.10) | collective-permute-done | bytes 102432 | tf_op jit(solution)/shard_map/ppermute | solution.py:573
  43.1 3.1 %collective-permute-start.11 = (f16[400,128]{1,0:T(8,128)(2,1)S(1)}, f16[400,128]{1,0:T(8,128)(2,1)S(1)}, u32[]{:S(2)}, u32[]{:S(2)}) collective-permute-start(f16[400,128]{1,0:T(8,128)(2,1)S(1)} %convert_element_type.74), channel_id=1, source_target_pairs={{0,64},{8,72},{16,80},{24,88},{32,96},{40,104},{48,112},{56,120},{... | collective-permute-start | bytes 307208 | tf_op jit(solution)/shard_map/ppermute | solution.py:573
  46.2 3.1 %collective-permute-done.11 = f16[400,128]{1,0:T(8,128)(2,1)S(1)} collective-permute-done((f16[400,128]{1,0:T(8,128)(2,1)S(1)}, f16[400,128]{1,0:T(8,128)(2,1)S(1)}, u32[]{:S(2)}, u32[]{:S(2)}) %collective-permute-start.11) | collective-permute-done | bytes 102432 | tf_op jit(solution)/shard_map/ppermute | solution.py:573
  49.7 6.4 %collective-permute-start.12 = (f16[144,128]{1,0:T(8,128)(2,1)S(1)}, f16[144,128]{1,0:T(8,128)(2,1)S(1)}, u32[]{:S(2)}, u32[]{:S(2)}) collective-permute-start(f16[144,128]{1,0:T(8,128)(2,1)S(1)} %convert_element_type.76), channel_id=1, source_target_pairs={{0,224},{8,232},{16,240},{24,248},{32,192},{40,200},{48,208},{56,2... | collective-permute-start | bytes 110600 | tf_op jit(solution)/shard_map/ppermute | solution.py:573
  56.1 1.3 %collective-permute-done.12 = f16[144,128]{1,0:T(8,128)(2,1)S(1)} collective-permute-done((f16[144,128]{1,0:T(8,128)(2,1)S(1)}, f16[144,128]{1,0:T(8,128)(2,1)S(1)}, u32[]{:S(2)}, u32[]{:S(2)}) %collective-permute-start.12) | collective-permute-done | bytes 36896 | tf_op jit(solution)/shard_map/ppermute | solution.py:573
  57.5 1.1 %scan.1 = (f32[272,128]{1,0:T(8,128)S(1)}, f32[272,128]{1,0:T(8,128)S(1)}, f32[272,128]{1,0:T(8,128)S(1)}, f32[272,128]{1,0:T(8,128)S(1)}) custom-call(f32[4,3,128,128]{3,2,1,0:T(8,128)S(1)} %get-tuple-element.90.spans, f32[400,128]{1,0:T(8,128)S(1)} %convert_element_type.73.other.near_group, f32[400,128]{1,0:T(8,128)S(1)} %convert_element_type.75.other.near_pair, ...), custom_call_target="tpu_custom_call" | custom-call | tf_op jit(solution)/shard_map/scan/pallas_call | solution.py:481
  58.8 4.1 %collective-permute-start.15 = (f16[272,128]{1,0:T(8,128)(2,1)S(1)}, f16[272,128]{1,0:T(8,128)(2,1)S(1)}, u32[]{:S(2)}, u32[]{:S(2)}) collective-permute-start(f16[272,128]{1,0:T(8,128)(2,1)S(1)} %convert_element_type.82), channel_id=1, source_target_pairs={{0,24},{8,16},{16,8},{24,0},{32,56},{40,48},{48,40},{56,32},{64,88... | collective-permute-start | bytes 208904 | tf_op jit(solution)/shard_map/ppermute | solution.py:573
  63.5 1.5 %collective-permute-done.15 = f16[272,128]{1,0:T(8,128)(2,1)S(1)} collective-permute-done((f16[272,128]{1,0:T(8,128)(2,1)S(1)}, f16[272,128]{1,0:T(8,128)(2,1)S(1)}, u32[]{:S(2)}, u32[]{:S(2)}) %collective-permute-start.15) | collective-permute-done | bytes 69664 | tf_op jit(solution)/shard_map/ppermute | solution.py:573
  65.0 5.0 %outputs.1 = (bf16[192,512]{1,0:T(8,128)(2,1)}, bf16[192,512]{1,0:T(8,128)(2,1)}, bf16[192,1024]{1,0:T(8,128)(2,1)}, bf16[192,1024]{1,0:T(8,128)(2,1)S(1)}, bf16[192,8]{1,0:T(8,128)(2,1)S(1)}) custom-call(f32[192,8]{1,0:T(8,128)S(1)} %get-tuple-element.81.refs_0_, bf16[192,512]{1,0:T(8,128)(2,1)S(1)} %get-tuple-element.78.refs_11_.refs_1_, ...), custom_call_target="tpu_custom_call" | custom-call | tf_op jit(solution)/shard_map/outputs/pallas_call | solution.py:481
  69.9 1.7 %shares.3 = bf16[4,192,512]{2,1,0:T(8,128)(2,1)S(1)} custom-call(bf16[192,1024]{1,0:T(8,128)(2,1)S(1)} %get-tuple-element.106.key_cot, bf16[192,8]{1,0:T(8,128)(2,1)S(1)} %get-tuple-element.107.logit_cot, bf16[4096,1024]{1,0:T(8,128)(2,1)S(1)} %get-tuple-element.76.refs_8_.key_weight, bf16[8,4096]{1,0:T(8,128)(2,1)S(1)} %get-tuple-element.77.refs_9_.beta_weight), custom_call_target="tpu_custom_call" | custom-call | tf_op jit(solution)/shard_map/shares/pallas_call | solution.py:481
  71.6 4.0 %collective-permute-start.16 = (bf16[4,192,512]{2,1,0:T(8,128)(2,1)S(1)}, bf16[4,192,512]{2,1,0:T(8,128)(2,1)S(1)}, u32[]{:S(2)}, u32[]{:S(2)}) collective-permute-start(bf16[4,192,512]{2,1,0:T(8,128)(2,1)S(1)} %shares.3), channel_id=1, source_target_pairs={{0,1},{1,0},{2,3},{3,2},{4,5},{5,4},{6,7},{7,6},{8,9},{9,8},{10,11... | collective-permute-start | bytes 2359304 | tf_op jit(solution)/shard_map/ppermute | solution.py:573
  75.6 1.7 %shares.2.own = f32[4,192,512]{2,1,0:T(8,128)S(1)} custom-call(bf16[192,1024]{1,0:T(8,128)(2,1)S(1)} %get-tuple-element.106.key_cot, bf16[192,8]{1,0:T(8,128)(2,1)S(1)} %get-tuple-element.107.logit_cot, bf16[4096,1024]{1,0:T(8,128)(2,1)S(1)} %get-tuple-element.76.refs_8_.key_weight, bf16[8,4096]{1,0:T(8,128)(2,1)S(1)} %get-tuple-element.77.refs_9_.beta_weight), custom_call_target="tpu_custom_call" | custom-call | tf_op jit(solution)/shard_map/shares/pallas_call | solution.py:481
  77.7 2.7 %collective-permute-start.17 = (bf16[192,512]{1,0:T(8,128)(2,1)S(1)}, bf16[192,512]{1,0:T(8,128)(2,1)S(1)}, u32[]{:S(2)}, u32[]{:S(2)}) collective-permute-start(bf16[192,512]{1,0:T(8,128)(2,1)S(1)} %get-tuple-element.109), channel_id=1, source_target_pairs={{0,4},{1,5},{2,6},{3,7},{4,0},{5,1},{6,2},{7,3},{8,12},{9,13},{10,... | collective-permute-start | bytes 589832 | tf_op jit(solution)/shard_map/ppermute | solution.py:573
  81.3 4.1 %collective-permute-done.17 = bf16[192,512]{1,0:T(8,128)(2,1)S(1)} collective-permute-done((bf16[192,512]{1,0:T(8,128)(2,1)S(1)}, bf16[192,512]{1,0:T(8,128)(2,1)S(1)}, u32[]{:S(2)}, u32[]{:S(2)}) %collective-permute-start.17) | collective-permute-done | bytes 196640 | tf_op jit(solution)/shard_map/ppermute | solution.py:573
  85.4 4.2 %collective-permute-done.18 = bf16[192,512]{1,0:T(8,128)(2,1)S(1)} collective-permute-done((bf16[192,512]{1,0:T(8,128)(2,1)S(1)}, bf16[192,512]{1,0:T(8,128)(2,1)S(1)}, u32[]{:S(2)}, u32[]{:S(2)}) %collective-permute-start.18) | collective-permute-done | bytes 196640 | tf_op jit(solution)/shard_map/ppermute | solution.py:573
  (58 shorter events, 12.1 us)
Async XLA Ops:
  0.6 14.6 %collective-permute-start.1 = (bf16[192,512]{1,0:T(8,128)(2,1)}, bf16[192,512]{1,0:T(8,128)(2,1)S(1)}, u32[]{:S(2)}, u32[]{:S(2)}) collective-permute-start(bf16[192,512]{1,0:T(8,128)(2,1)} %refs_0_.5), channel_id=1, source_target_pairs={{0,4},{1,5},{2,6},{3,7},{4,0},{5,1},{6,2},{7,3},{8,12},{9,13},{10,... | collective-permute-start | bytes 589832 | tf_op jit(solution)/shard_map/ppermute | solution.py:573
  4.3 10.9 %collective-permute-start.3 = (bf16[192,512]{1,0:T(8,128)(2,1)}, bf16[192,512]{1,0:T(8,128)(2,1)S(1)}, u32[]{:S(2)}, u32[]{:S(2)}) collective-permute-start(bf16[192,512]{1,0:T(8,128)(2,1)} %refs_0_.5), channel_id=1, source_target_pairs={{0,2},{1,3},{2,0},{3,1},{4,6},{5,7},{6,4},{7,5},{8,10},{9,11},{10,... | collective-permute-start | bytes 589832 | tf_op jit(solution)/shard_map/ppermute | solution.py:573
  4.6 10.6 %collective-permute-start.5 = (bf16[192,512]{1,0:T(8,128)(2,1)}, bf16[192,512]{1,0:T(8,128)(2,1)S(1)}, u32[]{:S(2)}, u32[]{:S(2)}) collective-permute-start(bf16[192,512]{1,0:T(8,128)(2,1)} %refs_0_.5), channel_id=1, source_target_pairs={{0,6},{1,7},{2,4},{3,5},{4,2},{5,3},{6,0},{7,1},{8,14},{9,15},{10,... | collective-permute-start | bytes 589832 | tf_op jit(solution)/shard_map/ppermute | solution.py:573
  5.2 10.8 %collective-permute-start = (bf16[192,512]{1,0:T(8,128)(2,1)}, bf16[192,512]{1,0:T(8,128)(2,1)S(1)}, u32[]{:S(2)}, u32[]{:S(2)}) collective-permute-start(bf16[192,512]{1,0:T(8,128)(2,1)} %refs_0_.5), channel_id=1, source_target_pairs={{0,1},{1,0},{2,3},{3,2},{4,5},{5,4},{6,7},{7,6},{8,9},{9,8},{10,11... | collective-permute-start | bytes 589832 | tf_op jit(solution)/shard_map/ppermute | solution.py:573
  8.1 1.0 %copy-start.1 = (bf16[192,1024]{1,0:T(8,128)(2,1)S(1)}, bf16[192,1024]{1,0:T(8,128)(2,1)}, u32[]{:S(2)}) copy-start(bf16[192,1024]{1,0:T(8,128)(2,1)} %refs_3_.1) | copy-start | bytes 1179652
  9.1 0.9 %copy-start.2 = (bf16[192,512]{1,0:T(8,128)(2,1)S(1)}, bf16[192,512]{1,0:T(8,128)(2,1)}, u32[]{:S(2)}) copy-start(bf16[192,512]{1,0:T(8,128)(2,1)} %refs_2_.1) | copy-start | bytes 589828
  11.7 5.6 %copy-start = (bf16[192,512]{1,0:T(8,128)(2,1)S(1)}, bf16[192,512]{1,0:T(8,128)(2,1)}, u32[]{:S(2)}) copy-start(bf16[192,512]{1,0:T(8,128)(2,1)} %refs_0_.5) | copy-start | bytes 589828
  11.7 5.6 %copy-start.5 = (f32[8]{0:T(128)S(1)}, f32[8]{0:T(128)}, u32[]{:S(2)}) copy-start(f32[8]{0:T(128)} %param.10) | copy-start | bytes 100
  15.3 1.5 %collective-permute-start.6 = (bf16[192,512]{1,0:T(8,128)(2,1)S(1)}, bf16[192,512]{1,0:T(8,128)(2,1)S(1)}, u32[]{:S(2)}, u32[]{:S(2)}) collective-permute-start(bf16[192,512]{1,0:T(8,128)(2,1)S(1)} %collective-permute-done.5.refs_6_), channel_id=1, source_target_pairs={{0,1},{1,0},{2,3},{3,2},{4,5},{5,4},{6,7},{7,6},{8,9},{9,8},{10,11... | collective-permute-start | bytes 589832 | tf_op jit(solution)/shard_map/ppermute | solution.py:573
  15.5 1.6 %collective-permute-start.4 = (bf16[192,512]{1,0:T(8,128)(2,1)S(1)}, bf16[192,512]{1,0:T(8,128)(2,1)S(1)}, u32[]{:S(2)}, u32[]{:S(2)}) collective-permute-start(bf16[192,512]{1,0:T(8,128)(2,1)S(1)} %collective-permute-done.3.refs_4_), channel_id=1, source_target_pairs={{0,1},{1,0},{2,3},{3,2},{4,5},{5,4},{6,7},{7,6},{8,9},{9,8},{10,11... | collective-permute-start | bytes 589832 | tf_op jit(solution)/shard_map/ppermute | solution.py:573
  15.9 1.5 %collective-permute-start.2 = (bf16[192,512]{1,0:T(8,128)(2,1)S(1)}, bf16[192,512]{1,0:T(8,128)(2,1)S(1)}, u32[]{:S(2)}, u32[]{:S(2)}) collective-permute-start(bf16[192,512]{1,0:T(8,128)(2,1)S(1)} %collective-permute-done.1.refs_2_), channel_id=1, source_target_pairs={{0,1},{1,0},{2,3},{3,2},{4,5},{5,4},{6,7},{7,6},{8,9},{9,8},{10,11... | collective-permute-start | bytes 589832 | tf_op jit(solution)/shard_map/ppermute | solution.py:573
  26.4 9.3 %collective-permute-start.7 = (f16[400,128]{1,0:T(8,128)(2,1)S(1)}, f16[400,128]{1,0:T(8,128)(2,1)S(1)}, u32[]{:S(2)}, u32[]{:S(2)}) collective-permute-start(f16[400,128]{1,0:T(8,128)(2,1)S(1)} %convert_element_type.66), channel_id=1, source_target_pairs={{0,8},{8,0},{16,24},{24,16},{32,40},{40,32},{48,56},{56,48},{64,72... | collective-permute-start | bytes 307208 | tf_op jit(solution)/shard_map/ppermute | solution.py:573
  27.1 8.6 %collective-permute-start.8 = (f16[400,128]{1,0:T(8,128)(2,1)S(1)}, f16[400,128]{1,0:T(8,128)(2,1)S(1)}, u32[]{:S(2)}, u32[]{:S(2)}) collective-permute-start(f16[400,128]{1,0:T(8,128)(2,1)S(1)} %convert_element_type.68), channel_id=1, source_target_pairs={{0,16},{8,24},{16,0},{24,8},{32,48},{40,56},{48,32},{56,40},{64,80... | collective-permute-start | bytes 307208 | tf_op jit(solution)/shard_map/ppermute | solution.py:573
  30.0 7.4 %collective-permute-start.9 = (f16[400,128]{1,0:T(8,128)(2,1)S(1)}, f16[400,128]{1,0:T(8,128)(2,1)S(1)}, u32[]{:S(2)}, u32[]{:S(2)}) collective-permute-start(f16[400,128]{1,0:T(8,128)(2,1)S(1)} %convert_element_type.70), channel_id=1, source_target_pairs={{0,24},{8,16},{16,8},{24,0},{32,56},{40,48},{48,40},{56,32},{64,88... | collective-permute-start | bytes 307208 | tf_op jit(solution)/shard_map/ppermute | solution.py:573
  38.3 4.4 %collective-permute-start.10 = (f16[400,128]{1,0:T(8,128)(2,1)S(1)}, f16[400,128]{1,0:T(8,128)(2,1)S(1)}, u32[]{:S(2)}, u32[]{:S(2)}) collective-permute-start(f16[400,128]{1,0:T(8,128)(2,1)S(1)} %convert_element_type.72), channel_id=1, source_target_pairs={{0,32},{8,40},{16,48},{24,56},{32,0},{40,8},{48,16},{56,24},{64,96... | collective-permute-start | bytes 307208 | tf_op jit(solution)/shard_map/ppermute | solution.py:573
  43.1 6.2 %collective-permute-start.11 = (f16[400,128]{1,0:T(8,128)(2,1)S(1)}, f16[400,128]{1,0:T(8,128)(2,1)S(1)}, u32[]{:S(2)}, u32[]{:S(2)}) collective-permute-start(f16[400,128]{1,0:T(8,128)(2,1)S(1)} %convert_element_type.74), channel_id=1, source_target_pairs={{0,64},{8,72},{16,80},{24,88},{32,96},{40,104},{48,112},{56,120},{... | collective-permute-start | bytes 307208 | tf_op jit(solution)/shard_map/ppermute | solution.py:573
  49.7 7.7 %collective-permute-start.12 = (f16[144,128]{1,0:T(8,128)(2,1)S(1)}, f16[144,128]{1,0:T(8,128)(2,1)S(1)}, u32[]{:S(2)}, u32[]{:S(2)}) collective-permute-start(f16[144,128]{1,0:T(8,128)(2,1)S(1)} %convert_element_type.76), channel_id=1, source_target_pairs={{0,224},{8,232},{16,240},{24,248},{32,192},{40,200},{48,208},{56,2... | collective-permute-start | bytes 110600 | tf_op jit(solution)/shard_map/ppermute | solution.py:573
  58.6 4.4 %collective-permute-start.13 = (f16[272,128]{1,0:T(8,128)(2,1)S(1)}, f16[272,128]{1,0:T(8,128)(2,1)S(1)}, u32[]{:S(2)}, u32[]{:S(2)}) collective-permute-start(f16[272,128]{1,0:T(8,128)(2,1)S(1)} %convert_element_type.78), channel_id=1, source_target_pairs={{0,8},{8,0},{16,24},{24,16},{32,40},{40,32},{48,56},{56,48},{64,72... | collective-permute-start | bytes 208904 | tf_op jit(solution)/shard_map/ppermute | solution.py:573
  58.7 4.8 %collective-permute-start.14 = (f16[272,128]{1,0:T(8,128)(2,1)S(1)}, f16[272,128]{1,0:T(8,128)(2,1)S(1)}, u32[]{:S(2)}, u32[]{:S(2)}) collective-permute-start(f16[272,128]{1,0:T(8,128)(2,1)S(1)} %convert_element_type.80), channel_id=1, source_target_pairs={{0,16},{8,24},{16,0},{24,8},{32,48},{40,56},{48,32},{56,40},{64,80... | collective-permute-start | bytes 208904 | tf_op jit(solution)/shard_map/ppermute | solution.py:573
  58.8 6.1 %collective-permute-start.15 = (f16[272,128]{1,0:T(8,128)(2,1)S(1)}, f16[272,128]{1,0:T(8,128)(2,1)S(1)}, u32[]{:S(2)}, u32[]{:S(2)}) collective-permute-start(f16[272,128]{1,0:T(8,128)(2,1)S(1)} %convert_element_type.82), channel_id=1, source_target_pairs={{0,24},{8,16},{16,8},{24,0},{32,56},{40,48},{48,40},{56,32},{64,88... | collective-permute-start | bytes 208904 | tf_op jit(solution)/shard_map/ppermute | solution.py:573
  71.6 5.9 %collective-permute-start.16 = (bf16[4,192,512]{2,1,0:T(8,128)(2,1)S(1)}, bf16[4,192,512]{2,1,0:T(8,128)(2,1)S(1)}, u32[]{:S(2)}, u32[]{:S(2)}) collective-permute-start(bf16[4,192,512]{2,1,0:T(8,128)(2,1)S(1)} %shares.3), channel_id=1, source_target_pairs={{0,1},{1,0},{2,3},{3,2},{4,5},{5,4},{6,7},{7,6},{8,9},{9,8},{10,11... | collective-permute-start | bytes 2359304 | tf_op jit(solution)/shard_map/ppermute | solution.py:573
  77.7 7.7 %collective-permute-start.17 = (bf16[192,512]{1,0:T(8,128)(2,1)S(1)}, bf16[192,512]{1,0:T(8,128)(2,1)S(1)}, u32[]{:S(2)}, u32[]{:S(2)}) collective-permute-start(bf16[192,512]{1,0:T(8,128)(2,1)S(1)} %get-tuple-element.109), channel_id=1, source_target_pairs={{0,4},{1,5},{2,6},{3,7},{4,0},{5,1},{6,2},{7,3},{8,12},{9,13},{10,... | collective-permute-start | bytes 589832 | tf_op jit(solution)/shard_map/ppermute | solution.py:573
  80.4 9.2 %collective-permute-start.18 = (bf16[192,512]{1,0:T(8,128)(2,1)S(1)}, bf16[192,512]{1,0:T(8,128)(2,1)S(1)}, u32[]{:S(2)}, u32[]{:S(2)}) collective-permute-start(bf16[192,512]{1,0:T(8,128)(2,1)S(1)} %get-tuple-element.110), channel_id=1, source_target_pairs={{0,2},{1,3},{2,0},{3,1},{4,6},{5,7},{6,4},{7,5},{8,10},{9,11},{10,... | collective-permute-start | bytes 589832 | tf_op jit(solution)/shard_map/ppermute | solution.py:573
  80.7 9.4 %collective-permute-start.19 = (bf16[192,512]{1,0:T(8,128)(2,1)S(1)}, bf16[192,512]{1,0:T(8,128)(2,1)S(1)}, u32[]{:S(2)}, u32[]{:S(2)}) collective-permute-start(bf16[192,512]{1,0:T(8,128)(2,1)S(1)} %get-tuple-element.111), channel_id=1, source_target_pairs={{0,6},{1,7},{2,4},{3,5},{4,2},{5,3},{6,0},{7,1},{8,14},{9,15},{10,... | collective-permute-start | bytes 589832 | tf_op jit(solution)/shard_map/ppermute | solution.py:573
  (2 other events, 1.8 us)

commit v5 on v4

--- a/solution.py
+++ b/solution.py
@@ -285,8 +285,9 @@
     starts = [pl.multiple_of((me ^ mask) * depth, depth) for mask in masks]
 
     total = beta_bias[...]
-    for piece, start in zip(pieces, starts):
-        total = total + product(piece[...], beta_weight[:, pl.ds(start, depth)], 1, 1)
+    if total.shape[0] == 1:
+        for piece, start in zip(pieces, starts):
+            total = total + product(piece[...], beta_weight[:, pl.ds(start, depth)], 1, 1)
     logits[...] = total
     for near, head in enumerate(heads):
         wide = pl.ds(pl.multiple_of(head * 2 * width, 2 * width), 2 * width)
@@ -450,19 +451,17 @@
         logit_cot[i * SPAN : (i + 1) * SPAN, :] = columns[i].astype(BF16)
 
 
-def shares_kernel(core, key_cot, logit_cot, key_weight, beta_weight, output):
-    depth = output.shape[2]
+def shares_kernel(core, chips, key_cot, logit_cot, key_weight, beta_weight, *refs):
+    depth = key_weight.shape[0] // lax.axis_size("head")
+    outputs = refs[-len(chips) :]
     me = lax.axis_index("head")
-    for chip in range(output.shape[0]):
+    for near, (chip, output) in enumerate(zip(chips, outputs)):
         start = pl.multiple_of((me ^ (2 * chip + core)) * depth, depth)
         total = product(key_cot[...], key_weight[pl.ds(start, depth), :], 1, 1)
         total = total + product(logit_cot[...], beta_weight[:, pl.ds(start, depth)])
-        output[chip] = total.astype(output.dtype)
-
-
-def add_kernel(own, away, *outputs):
-    for chip, output in enumerate(outputs):
-        output[...] = (own[chip] + away[chip].astype(F32)).astype(output.dtype)
+        if len(refs) > len(chips):
+            total = total + refs[near][...].astype(F32)
+        output[...] = total.astype(output.dtype)
 
 
 VMEM = pl.BlockSpec(memory_space=pltpu.VMEM)
@@ -556,16 +555,17 @@
     )
 
 
-def shares(core, chips, key_cot, logit_cot, key_weight, beta_across, dtype):
-    depth = key_weight.shape[0] // (2 * chips)
+def shares(core, chips, key_cot, logit_cot, key_weight, beta_across, dtype, *more):
+    shape = (key_cot.shape[0], key_weight.shape[0] // lax.axis_size("head"))
     return call(
-        functools.partial(shares_kernel, core),
+        functools.partial(shares_kernel, core, chips),
         "shares",
-        shape_of(chips, key_cot.shape[0], depth, dtype=dtype),
+        [shape_of(*shape, dtype=dtype)] * len(chips),
         key_cot,
         logit_cot,
         key_weight,
         beta_across,
+        *more,
     )
 
 
@@ -580,7 +580,6 @@
 def per_device(inputs, key_weight, beta_weight, beta_bias, queries, values, out_grad):
     heads = beta_bias.shape[0] // 2
     width = queries.shape[1] // heads
-    chips = lax.axis_size("head") // 2
     beta_across = jnp.swapaxes(beta_weight, 0, 1)
 
     fetched = fetch(key_weight, beta_across, queries, values, out_grad)
@@ -591,10 +590,10 @@
         masks += [2 * chip, 2 * chip + 1]
         pieces += [piece, swapped(piece, "head", 1)]
     key_weight, beta_across, queries, values, out_grad = fetched
-    local, arrived = {}, {}
+    local, arrived, logits = {}, {}, beta_bias[None]
     for slots in GROUPS:
         logits, local[slots], wholes = project(
-            masks, slots, pieces, key_weight, beta_across, beta_bias[None], queries, values, out_grad
+            masks, slots, pieces, key_weight, beta_across, logits, queries, values, out_grad
         )
         for slot, whole in zip(slots, wholes):
             arrived[slot] = swapped16(whole, "ctx", slot) if slot else whole
@@ -626,18 +625,16 @@
         logits, queries, out_grad, GROUPS, [local[slots] for slots in GROUPS], arrived
     )
 
-    operands = (chips, key_cot, logit_cot, key_weight, beta_across)
-    away = swapped(shares(1, *operands, BF16), "head", 1)
-    own = shares(0, *operands, F32)
-    total, *sent = call(
-        add_kernel,
-        "add",
-        [shape_of(*own.shape[1:])] + [shape_of(*own.shape[1:], dtype=BF16)] * (chips - 1),
-        own,
-        away,
-    )
-    for chip in (2, 1, 3):
-        total = total + swapped(sent[chip - 1], "head", 2 * chip).astype(F32)
+    operands = (key_cot, logit_cot, key_weight, beta_across)
+    away, total = {}, 0.0
+    for chips in ((2,), (1, 3), (0,)):
+        for chip, share in zip(chips, shares(1, chips, *operands, BF16)):
+            away[chip] = swapped(share, "head", 1)
+    for chips in ((2,), (1, 3), (0,)):
+        dtype = BF16 if chips[0] else F32
+        found = shares(0, chips, *operands, dtype, *[away[chip] for chip in chips])
+        for chip, share in zip(chips, found):
+            total = total + (swapped(share, "head", 2 * chip).astype(F32) if chip else share)
     return mixed, query_grad, value_grad, total.astype(BF16)
 
 

time: 91.1 us -> 87.5 us (0.960)
  waiting for transfers between devices: 21.3 us -> 17.3 us
    ppermute x20 -> x23, waiting for transfers between devices: 21.3 us -> 17.3 us  [swapped(): lax.ppermute(value, axis, [(i, i ^ mask) for i in range(lax.axis_size(axi...]
    ppermute x20 -> x23, starting transfers between devices: 35.5 us -> 35.7 us  [swapped(): lax.ppermute(value, axis, [(i, i ^ mask) for i in range(lax.axis_size(axi...]
    pallas_call x11 -> x14, Pallas kernels: 28.5 us -> 28.6 us  [call(): pl.pallas_call(kernel, in_specs=specs or [VMEM] * len(operands), out_spec...]
  transfers between devices with their start and end apart: 20 -> 23, of which waited for: 13 -> 11; matrix products, arithmetic and copies ran while one was open for 0% -> 0% of each run, Pallas kernels for 11% -> 13%
where the time goes in v5:
time: 87.5 us; the launch traced here: 87.2 us
  starting transfers between devices  35.7 us (41%)
  Pallas kernels  28.6 us (33%)
  waiting for transfers between devices  17.3 us (20%)
  local copies, waits for them, and re-layouts  3.69 us (4%)
  other arithmetic  1.03 us (1%)
  between operations  0.91 us (1%)
    ppermute x23, starting transfers between devices, swapped(): lax.ppermute(value, axis, [(i, i ^ mask) for i in range(lax.axis_size(axi...  35.7 us
    pallas_call x14, Pallas kernels, call(): pl.pallas_call(kernel, in_specs=specs or [VMEM] * len(operands), out_spec...  28.6 us
    ppermute x23, waiting for transfers between devices, swapped(): lax.ppermute(value, axis, [(i, i ^ mask) for i in range(lax.axis_size(axi...  17.3 us
    unnamed x12, local copies, waits for them, and re-layouts  3.69 us
  transfers between devices with their start and end apart: 23, of which 11 were waited for; matrix products, arithmetic and copies ran while one was open for 0% of the time, Pallas kernels for 13%

profile of v5, /device:TPU:1, one launch (start us, length us, event | category | flops | bytes accessed | tf_op | source)
XLA Modules:
  0.0 87.2 jit_solution(12190191650433988561)
XLA Ops:
  0.6 3.7 %collective-permute-start.1 = (bf16[192,512]{1,0:T(8,128)(2,1)}, bf16[192,512]{1,0:T(8,128)(2,1)S(1)}, u32[]{:S(2)}, u32[]{:S(2)}) collective-permute-start(bf16[192,512]{1,0:T(8,128)(2,1)} %refs_0_.5), channel_id=1, source_target_pairs={{0,4},{1,5},{2,6},{3,7},{4,0},{5,1},{6,2},{7,3},{8,12},{9,13},{10,... | collective-permute-start | bytes 589832 | tf_op jit(solution)/shard_map/ppermute | solution.py:573
  5.2 2.9 %collective-permute-start = (bf16[192,512]{1,0:T(8,128)(2,1)}, bf16[192,512]{1,0:T(8,128)(2,1)S(1)}, u32[]{:S(2)}, u32[]{:S(2)}) collective-permute-start(bf16[192,512]{1,0:T(8,128)(2,1)} %refs_0_.5), channel_id=1, source_target_pairs={{0,1},{1,0},{2,3},{3,2},{4,5},{5,4},{6,7},{7,6},{8,9},{9,8},{10,11... | collective-permute-start | bytes 589832 | tf_op jit(solution)/shard_map/ppermute | solution.py:573
  8.1 1.0 %copy-done.1 = bf16[192,1024]{1,0:T(8,128)(2,1)S(1)} copy-done((bf16[192,1024]{1,0:T(8,128)(2,1)S(1)}, bf16[192,1024]{1,0:T(8,128)(2,1)}, u32[]{:S(2)}) %copy-start.1) | copy-done | bytes 393240
  9.1 0.9 %copy-done.2 = bf16[192,512]{1,0:T(8,128)(2,1)S(1)} copy-done((bf16[192,512]{1,0:T(8,128)(2,1)S(1)}, bf16[192,512]{1,0:T(8,128)(2,1)}, u32[]{:S(2)}) %copy-start.2) | copy-done | bytes 196632
  10.0 0.9 %copy-done.3 = bf16[192,512]{1,0:T(8,128)(2,1)S(1)} copy-done((bf16[192,512]{1,0:T(8,128)(2,1)S(1)}, bf16[192,512]{1,0:T(8,128)(2,1)}, u32[]{:S(2)}) %copy-start.3) | copy-done | bytes 196632
  11.8 3.5 %fetch.1 = (bf16[4096,1024]{1,0:T(8,128)(2,1)S(1)}, bf16[8,4096]{1,0:T(8,128)(2,1)S(1)}, bf16[192,512]{1,0:T(8,128)(2,1)S(1)}, bf16[192,1024]{1,0:T(8,128)(2,1)S(1)}, bf16[192,512]{1,0:T(8,128)(2,1)S(1)}) custom-call(bf16[4096,1024]{1,0:T(8,128)(2,1)} %refs_0_.3, bf16[8,4096]{1,0:T(8,128)(2,1)S(1)} %bitcast.2, bf16[192,512]{1,0:T(8,128)(2,1)S(1)} %copy-done.2, ...), custom_call_target="tpu_custom_call" | custom-call | bytes 18481152 | tf_op jit(solution)/shard_map/fetch/pallas_call | solution.py:480
  17.4 8.5 %project.2 = (f32[192,768]{1,0:T(8,128)S(1)}, f32[192,8]{1,0:T(8,128)S(1)}, f32[3,3,128,256]{3,2,1,0:T(8,128)S(1)}, f32[3,3,128,256]{3,2,1,0:T(8,128)S(1)}, f32[...) custom-call(bf16[192,512]{1,0:T(8,128)(2,1)S(1)} %copy-done, ...), custom_call_target="tpu_custom_call" | custom-call | tf_op jit(solution)/shard_map/project/pallas_call | solution.py:480
  25.9 2.1 %collective-permute-start.9 = (f16[400,128]{1,0:T(8,128)(2,1)S(1)}, f16[400,128]{1,0:T(8,128)(2,1)S(1)}, u32[]{:S(2)}, u32[]{:S(2)}) collective-permute-start(f16[400,128]{1,0:T(8,128)(2,1)S(1)} %convert_element_type.70), channel_id=1, source_target_pairs={{0,24},{8,16},{16,8},{24,0},{32,56},{40,48},{48,40},{56,32},{64,88... | collective-permute-start | bytes 307208 | tf_op jit(solution)/shard_map/ppermute | solution.py:573
  29.4 5.1 %project.3 = (f32[192,256]{1,0:T(8,128)S(1)}, f32[192,8]{1,0:T(8,128)S(1)}, f32[1,3,128,256]{3,2,1,0:T(8,128)S(1)}, f32[1,3,128,256]{3,2,1,0:T(8,128)S(1)}, f32[...) custom-call(bf16[192,512]{1,0:T(8,128)(2,1)S(1)} %copy-done, bf16[192,512]{1,0:T(8,128)(2,1)S(1)} %collective-permute-done.refs_1_, ...), custom_call_target="tpu_custom_call" | custom-call | tf_op jit(solution)/shard_map/project/pallas_call | solution.py:480
  35.5 1.4 %collective-permute-start.10 = (f16[400,128]{1,0:T(8,128)(2,1)S(1)}, f16[400,128]{1,0:T(8,128)(2,1)S(1)}, u32[]{:S(2)}, u32[]{:S(2)}) collective-permute-start(f16[400,128]{1,0:T(8,128)(2,1)S(1)} %convert_element_type.72), channel_id=1, source_target_pairs={{0,32},{8,40},{16,48},{24,56},{32,0},{40,8},{48,16},{56,24},{64,96... | collective-permute-start | bytes 307208 | tf_op jit(solution)/shard_map/ppermute | solution.py:573
  36.8 2.2 %collective-permute-done.10 = f16[400,128]{1,0:T(8,128)(2,1)S(1)} collective-permute-done((f16[400,128]{1,0:T(8,128)(2,1)S(1)}, f16[400,128]{1,0:T(8,128)(2,1)S(1)}, u32[]{:S(2)}, u32[]{:S(2)}) %collective-permute-start.10) | collective-permute-done | bytes 102432 | tf_op jit(solution)/shard_map/ppermute | solution.py:573
  39.5 2.9 %collective-permute-start.11 = (f16[400,128]{1,0:T(8,128)(2,1)S(1)}, f16[400,128]{1,0:T(8,128)(2,1)S(1)}, u32[]{:S(2)}, u32[]{:S(2)}) collective-permute-start(f16[400,128]{1,0:T(8,128)(2,1)S(1)} %convert_element_type.74), channel_id=1, source_target_pairs={{0,64},{8,72},{16,80},{24,88},{32,96},{40,104},{48,112},{56,120},{... | collective-permute-start | bytes 307208 | tf_op jit(solution)/shard_map/ppermute | solution.py:573
  42.4 2.1 %collective-permute-done.11 = f16[400,128]{1,0:T(8,128)(2,1)S(1)} collective-permute-done((f16[400,128]{1,0:T(8,128)(2,1)S(1)}, f16[400,128]{1,0:T(8,128)(2,1)S(1)}, u32[]{:S(2)}, u32[]{:S(2)}) %collective-permute-start.11) | collective-permute-done | bytes 102432 | tf_op jit(solution)/shard_map/ppermute | solution.py:573
  44.8 5.9 %collective-permute-start.12 = (f16[144,128]{1,0:T(8,128)(2,1)S(1)}, f16[144,128]{1,0:T(8,128)(2,1)S(1)}, u32[]{:S(2)}, u32[]{:S(2)}) collective-permute-start(f16[144,128]{1,0:T(8,128)(2,1)S(1)} %convert_element_type.76), channel_id=1, source_target_pairs={{0,224},{8,232},{16,240},{24,248},{32,192},{40,200},{48,208},{56,2... | collective-permute-start | bytes 110600 | tf_op jit(solution)/shard_map/ppermute | solution.py:573
  50.8 1.7 %collective-permute-done.12 = f16[144,128]{1,0:T(8,128)(2,1)S(1)} collective-permute-done((f16[144,128]{1,0:T(8,128)(2,1)S(1)}, f16[144,128]{1,0:T(8,128)(2,1)S(1)}, u32[]{:S(2)}, u32[]{:S(2)}) %collective-permute-start.12) | collective-permute-done | bytes 36896 | tf_op jit(solution)/shard_map/ppermute | solution.py:573
  52.4 1.1 %scan.1 = (f32[272,128]{1,0:T(8,128)S(1)}, f32[272,128]{1,0:T(8,128)S(1)}, f32[272,128]{1,0:T(8,128)S(1)}, f32[272,128]{1,0:T(8,128)S(1)}) custom-call(f32[4,3,128,128]{3,2,1,0:T(8,128)S(1)} %get-tuple-element.92.spans, f32[400,128]{1,0:T(8,128)S(1)} %convert_element_type.73.other.near_group, f32[400,128]{1,0:T(8,128)S(1)} %convert_element_type.75.other.near_pair, ...), custom_call_target="tpu_custom_call" | custom-call | tf_op jit(solution)/shard_map/scan/pallas_call | solution.py:480
  53.6 2.2 %collective-permute-start.15 = (f16[272,128]{1,0:T(8,128)(2,1)S(1)}, f16[272,128]{1,0:T(8,128)(2,1)S(1)}, u32[]{:S(2)}, u32[]{:S(2)}) collective-permute-start(f16[272,128]{1,0:T(8,128)(2,1)S(1)} %convert_element_type.82), channel_id=1, source_target_pairs={{0,24},{8,16},{16,8},{24,0},{32,56},{40,48},{48,40},{56,32},{64,88... | collective-permute-start | bytes 208904 | tf_op jit(solution)/shard_map/ppermute | solution.py:573
  56.2 1.0 %collective-permute-start.13 = (f16[272,128]{1,0:T(8,128)(2,1)S(1)}, f16[272,128]{1,0:T(8,128)(2,1)S(1)}, u32[]{:S(2)}, u32[]{:S(2)}) collective-permute-start(f16[272,128]{1,0:T(8,128)(2,1)S(1)} %convert_element_type.78), channel_id=1, source_target_pairs={{0,8},{8,0},{16,24},{24,16},{32,40},{40,32},{48,56},{56,48},{64,72... | collective-permute-start | bytes 208904 | tf_op jit(solution)/shard_map/ppermute | solution.py:573
  58.1 2.4 %collective-permute-done.14 = f16[272,128]{1,0:T(8,128)(2,1)S(1)} collective-permute-done((f16[272,128]{1,0:T(8,128)(2,1)S(1)}, f16[272,128]{1,0:T(8,128)(2,1)S(1)}, u32[]{:S(2)}, u32[]{:S(2)}) %collective-permute-start.14) | collective-permute-done | bytes 69664 | tf_op jit(solution)/shard_map/ppermute | solution.py:573
  60.5 4.9 %outputs.1 = (bf16[192,512]{1,0:T(8,128)(2,1)}, bf16[192,512]{1,0:T(8,128)(2,1)}, bf16[192,1024]{1,0:T(8,128)(2,1)}, bf16[192,1024]{1,0:T(8,128)(2,1)S(1)}, bf16[192,8]{1,0:T(8,128)(2,1)S(1)}) custom-call(f32[192,8]{1,0:T(8,128)S(1)} %get-tuple-element.83.refs_0_, bf16[192,512]{1,0:T(8,128)(2,1)S(1)} %get-tuple-element.79.refs_11_.refs_1_, ...), custom_call_target="tpu_custom_call" | custom-call | tf_op jit(solution)/shard_map/outputs/pallas_call | solution.py:480
  66.9 5.8 %collective-permute-start.16 = (bf16[192,512]{1,0:T(8,128)(2,1)S(1)}, bf16[192,512]{1,0:T(8,128)(2,1)S(1)}, u32[]{:S(2)}, u32[]{:S(2)}) collective-permute-start(bf16[192,512]{1,0:T(8,128)(2,1)S(1)} %shares.6), channel_id=1, source_target_pairs={{0,1},{1,0},{2,3},{3,2},{4,5},{5,4},{6,7},{7,6},{8,9},{9,8},{10,11... | collective-permute-start | bytes 589832 | tf_op jit(solution)/shard_map/ppermute | solution.py:573
  74.4 2.7 %collective-permute-start.17 = (bf16[192,512]{1,0:T(8,128)(2,1)S(1)}, bf16[192,512]{1,0:T(8,128)(2,1)S(1)}, u32[]{:S(2)}, u32[]{:S(2)}) collective-permute-start(bf16[192,512]{1,0:T(8,128)(2,1)S(1)} %shares.7), channel_id=1, source_target_pairs={{0,4},{1,5},{2,6},{3,7},{4,0},{5,1},{6,2},{7,3},{8,12},{9,13},{10,... | collective-permute-start | bytes 589832 | tf_op jit(solution)/shard_map/ppermute | solution.py:573
  79.7 2.4 %collective-permute-done.17 = bf16[192,512]{1,0:T(8,128)(2,1)S(1)} collective-permute-done((bf16[192,512]{1,0:T(8,128)(2,1)S(1)}, bf16[192,512]{1,0:T(8,128)(2,1)S(1)}, u32[]{:S(2)}, u32[]{:S(2)}) %collective-permute-start.17) | collective-permute-done | bytes 196640 | tf_op jit(solution)/shard_map/ppermute | solution.py:573
  82.1 4.2 %collective-permute-done.20 = bf16[192,512]{1,0:T(8,128)(2,1)S(1)} collective-permute-done((bf16[192,512]{1,0:T(8,128)(2,1)S(1)}, bf16[192,512]{1,0:T(8,128)(2,1)S(1)}, u32[]{:S(2)}, u32[]{:S(2)}) %collective-permute-start.20) | collective-permute-done | bytes 196640 | tf_op jit(solution)/shard_map/ppermute | solution.py:573
  (67 shorter events, 14.9 us)
Async XLA Ops:
  0.6 14.6 %collective-permute-start.1 = (bf16[192,512]{1,0:T(8,128)(2,1)}, bf16[192,512]{1,0:T(8,128)(2,1)S(1)}, u32[]{:S(2)}, u32[]{:S(2)}) collective-permute-start(bf16[192,512]{1,0:T(8,128)(2,1)} %refs_0_.5), channel_id=1, source_target_pairs={{0,4},{1,5},{2,6},{3,7},{4,0},{5,1},{6,2},{7,3},{8,12},{9,13},{10,... | collective-permute-start | bytes 589832 | tf_op jit(solution)/shard_map/ppermute | solution.py:573
  4.3 10.9 %collective-permute-start.3 = (bf16[192,512]{1,0:T(8,128)(2,1)}, bf16[192,512]{1,0:T(8,128)(2,1)S(1)}, u32[]{:S(2)}, u32[]{:S(2)}) collective-permute-start(bf16[192,512]{1,0:T(8,128)(2,1)} %refs_0_.5), channel_id=1, source_target_pairs={{0,2},{1,3},{2,0},{3,1},{4,6},{5,7},{6,4},{7,5},{8,10},{9,11},{10,... | collective-permute-start | bytes 589832 | tf_op jit(solution)/shard_map/ppermute | solution.py:573
  4.6 10.6 %collective-permute-start.5 = (bf16[192,512]{1,0:T(8,128)(2,1)}, bf16[192,512]{1,0:T(8,128)(2,1)S(1)}, u32[]{:S(2)}, u32[]{:S(2)}) collective-permute-start(bf16[192,512]{1,0:T(8,128)(2,1)} %refs_0_.5), channel_id=1, source_target_pairs={{0,6},{1,7},{2,4},{3,5},{4,2},{5,3},{6,0},{7,1},{8,14},{9,15},{10,... | collective-permute-start | bytes 589832 | tf_op jit(solution)/shard_map/ppermute | solution.py:573
  5.2 10.8 %collective-permute-start = (bf16[192,512]{1,0:T(8,128)(2,1)}, bf16[192,512]{1,0:T(8,128)(2,1)S(1)}, u32[]{:S(2)}, u32[]{:S(2)}) collective-permute-start(bf16[192,512]{1,0:T(8,128)(2,1)} %refs_0_.5), channel_id=1, source_target_pairs={{0,1},{1,0},{2,3},{3,2},{4,5},{5,4},{6,7},{7,6},{8,9},{9,8},{10,11... | collective-permute-start | bytes 589832 | tf_op jit(solution)/shard_map/ppermute | solution.py:573
  11.7 5.6 %copy-start.5 = (f32[8]{0:T(128)S(1)}, f32[8]{0:T(128)}, u32[]{:S(2)}) copy-start(f32[8]{0:T(128)} %param.10) | copy-start | bytes 100
  15.3 1.5 %collective-permute-start.6 = (bf16[192,512]{1,0:T(8,128)(2,1)S(1)}, bf16[192,512]{1,0:T(8,128)(2,1)S(1)}, u32[]{:S(2)}, u32[]{:S(2)}) collective-permute-start(bf16[192,512]{1,0:T(8,128)(2,1)S(1)} %collective-permute-done.5.refs_6_), channel_id=1, source_target_pairs={{0,1},{1,0},{2,3},{3,2},{4,5},{5,4},{6,7},{7,6},{8,9},{9,8},{10,11... | collective-permute-start | bytes 589832 | tf_op jit(solution)/shard_map/ppermute | solution.py:573
  15.5 1.6 %collective-permute-start.4 = (bf16[192,512]{1,0:T(8,128)(2,1)S(1)}, bf16[192,512]{1,0:T(8,128)(2,1)S(1)}, u32[]{:S(2)}, u32[]{:S(2)}) collective-permute-start(bf16[192,512]{1,0:T(8,128)(2,1)S(1)} %collective-permute-done.3.refs_4_), channel_id=1, source_target_pairs={{0,1},{1,0},{2,3},{3,2},{4,5},{5,4},{6,7},{7,6},{8,9},{9,8},{10,11... | collective-permute-start | bytes 589832 | tf_op jit(solution)/shard_map/ppermute | solution.py:573
  15.9 1.5 %collective-permute-start.2 = (bf16[192,512]{1,0:T(8,128)(2,1)S(1)}, bf16[192,512]{1,0:T(8,128)(2,1)S(1)}, u32[]{:S(2)}, u32[]{:S(2)}) collective-permute-start(bf16[192,512]{1,0:T(8,128)(2,1)S(1)} %collective-permute-done.1.refs_2_), channel_id=1, source_target_pairs={{0,1},{1,0},{2,3},{3,2},{4,5},{5,4},{6,7},{7,6},{8,9},{9,8},{10,11... | collective-permute-start | bytes 589832 | tf_op jit(solution)/shard_map/ppermute | solution.py:573
  25.9 8.6 %collective-permute-start.9 = (f16[400,128]{1,0:T(8,128)(2,1)S(1)}, f16[400,128]{1,0:T(8,128)(2,1)S(1)}, u32[]{:S(2)}, u32[]{:S(2)}) collective-permute-start(f16[400,128]{1,0:T(8,128)(2,1)S(1)} %convert_element_type.70), channel_id=1, source_target_pairs={{0,24},{8,16},{16,8},{24,0},{32,56},{40,48},{48,40},{56,32},{64,88... | collective-permute-start | bytes 307208 | tf_op jit(solution)/shard_map/ppermute | solution.py:573
  28.1 6.5 %collective-permute-start.8 = (f16[400,128]{1,0:T(8,128)(2,1)S(1)}, f16[400,128]{1,0:T(8,128)(2,1)S(1)}, u32[]{:S(2)}, u32[]{:S(2)}) collective-permute-start(f16[400,128]{1,0:T(8,128)(2,1)S(1)} %convert_element_type.68), channel_id=1, source_target_pairs={{0,16},{8,24},{16,0},{24,8},{32,48},{40,56},{48,32},{56,40},{64,80... | collective-permute-start | bytes 307208 | tf_op jit(solution)/shard_map/ppermute | solution.py:573
  28.5 6.1 %collective-permute-start.7 = (f16[400,128]{1,0:T(8,128)(2,1)S(1)}, f16[400,128]{1,0:T(8,128)(2,1)S(1)}, u32[]{:S(2)}, u32[]{:S(2)}) collective-permute-start(f16[400,128]{1,0:T(8,128)(2,1)S(1)} %convert_element_type.66), channel_id=1, source_target_pairs={{0,8},{8,0},{16,24},{24,16},{32,40},{40,32},{48,56},{56,48},{64,72... | collective-permute-start | bytes 307208 | tf_op jit(solution)/shard_map/ppermute | solution.py:573
  35.5 3.6 %collective-permute-start.10 = (f16[400,128]{1,0:T(8,128)(2,1)S(1)}, f16[400,128]{1,0:T(8,128)(2,1)S(1)}, u32[]{:S(2)}, u32[]{:S(2)}) collective-permute-start(f16[400,128]{1,0:T(8,128)(2,1)S(1)} %convert_element_type.72), channel_id=1, source_target_pairs={{0,32},{8,40},{16,48},{24,56},{32,0},{40,8},{48,16},{56,24},{64,96... | collective-permute-start | bytes 307208 | tf_op jit(solution)/shard_map/ppermute | solution.py:573
  39.5 4.9 %collective-permute-start.11 = (f16[400,128]{1,0:T(8,128)(2,1)S(1)}, f16[400,128]{1,0:T(8,128)(2,1)S(1)}, u32[]{:S(2)}, u32[]{:S(2)}) collective-permute-start(f16[400,128]{1,0:T(8,128)(2,1)S(1)} %convert_element_type.74), channel_id=1, source_target_pairs={{0,64},{8,72},{16,80},{24,88},{32,96},{40,104},{48,112},{56,120},{... | collective-permute-start | bytes 307208 | tf_op jit(solution)/shard_map/ppermute | solution.py:573
  44.8 7.6 %collective-permute-start.12 = (f16[144,128]{1,0:T(8,128)(2,1)S(1)}, f16[144,128]{1,0:T(8,128)(2,1)S(1)}, u32[]{:S(2)}, u32[]{:S(2)}) collective-permute-start(f16[144,128]{1,0:T(8,128)(2,1)S(1)} %convert_element_type.76), channel_id=1, source_target_pairs={{0,224},{8,232},{16,240},{24,248},{32,192},{40,200},{48,208},{56,2... | collective-permute-start | bytes 110600 | tf_op jit(solution)/shard_map/ppermute | solution.py:573
  53.6 4.5 %collective-permute-start.15 = (f16[272,128]{1,0:T(8,128)(2,1)S(1)}, f16[272,128]{1,0:T(8,128)(2,1)S(1)}, u32[]{:S(2)}, u32[]{:S(2)}) collective-permute-start(f16[272,128]{1,0:T(8,128)(2,1)S(1)} %convert_element_type.82), channel_id=1, source_target_pairs={{0,24},{8,16},{16,8},{24,0},{32,56},{40,48},{48,40},{56,32},{64,88... | collective-permute-start | bytes 208904 | tf_op jit(solution)/shard_map/ppermute | solution.py:573
  55.8 4.7 %collective-permute-start.14 = (f16[272,128]{1,0:T(8,128)(2,1)S(1)}, f16[272,128]{1,0:T(8,128)(2,1)S(1)}, u32[]{:S(2)}, u32[]{:S(2)}) collective-permute-start(f16[272,128]{1,0:T(8,128)(2,1)S(1)} %convert_element_type.80), channel_id=1, source_target_pairs={{0,16},{8,24},{16,0},{24,8},{32,48},{40,56},{48,32},{56,40},{64,80... | collective-permute-start | bytes 208904 | tf_op jit(solution)/shard_map/ppermute | solution.py:573
  56.2 4.2 %collective-permute-start.13 = (f16[272,128]{1,0:T(8,128)(2,1)S(1)}, f16[272,128]{1,0:T(8,128)(2,1)S(1)}, u32[]{:S(2)}, u32[]{:S(2)}) collective-permute-start(f16[272,128]{1,0:T(8,128)(2,1)S(1)} %convert_element_type.78), channel_id=1, source_target_pairs={{0,8},{8,0},{16,24},{24,16},{32,40},{40,32},{48,56},{56,48},{64,72... | collective-permute-start | bytes 208904 | tf_op jit(solution)/shard_map/ppermute | solution.py:573
  66.9 7.0 %collective-permute-start.16 = (bf16[192,512]{1,0:T(8,128)(2,1)S(1)}, bf16[192,512]{1,0:T(8,128)(2,1)S(1)}, u32[]{:S(2)}, u32[]{:S(2)}) collective-permute-start(bf16[192,512]{1,0:T(8,128)(2,1)S(1)} %shares.6), channel_id=1, source_target_pairs={{0,1},{1,0},{2,3},{3,2},{4,5},{5,4},{6,7},{7,6},{8,9},{9,8},{10,11... | collective-permute-start | bytes 589832 | tf_op jit(solution)/shard_map/ppermute | solution.py:573
  72.7 4.4 %collective-permute-start.18 = (bf16[192,512]{1,0:T(8,128)(2,1)S(1)}, bf16[192,512]{1,0:T(8,128)(2,1)S(1)}, u32[]{:S(2)}, u32[]{:S(2)}) collective-permute-start(bf16[192,512]{1,0:T(8,128)(2,1)S(1)} %get-tuple-element.110), channel_id=1, source_target_pairs={{0,1},{1,0},{2,3},{3,2},{4,5},{5,4},{6,7},{7,6},{8,9},{9,8},{10,11... | collective-permute-start | bytes 589832 | tf_op jit(solution)/shard_map/ppermute | solution.py:573
  72.8 4.3 %collective-permute-start.19 = (bf16[192,512]{1,0:T(8,128)(2,1)S(1)}, bf16[192,512]{1,0:T(8,128)(2,1)S(1)}, u32[]{:S(2)}, u32[]{:S(2)}) collective-permute-start(bf16[192,512]{1,0:T(8,128)(2,1)S(1)} %get-tuple-element.111), channel_id=1, source_target_pairs={{0,1},{1,0},{2,3},{3,2},{4,5},{5,4},{6,7},{7,6},{8,9},{9,8},{10,11... | collective-permute-start | bytes 589832 | tf_op jit(solution)/shard_map/ppermute | solution.py:573
  73.7 5.4 %collective-permute-start.22 = (bf16[192,512]{1,0:T(8,128)(2,1)S(1)}, bf16[192,512]{1,0:T(8,128)(2,1)S(1)}, u32[]{:S(2)}, u32[]{:S(2)}) collective-permute-start(bf16[192,512]{1,0:T(8,128)(2,1)S(1)} %shares.10), channel_id=1, source_target_pairs={{0,1},{1,0},{2,3},{3,2},{4,5},{5,4},{6,7},{7,6},{8,9},{9,8},{10,11... | collective-permute-start | bytes 589832 | tf_op jit(solution)/shard_map/ppermute | solution.py:573
  74.4 7.7 %collective-permute-start.17 = (bf16[192,512]{1,0:T(8,128)(2,1)S(1)}, bf16[192,512]{1,0:T(8,128)(2,1)S(1)}, u32[]{:S(2)}, u32[]{:S(2)}) collective-permute-start(bf16[192,512]{1,0:T(8,128)(2,1)S(1)} %shares.7), channel_id=1, source_target_pairs={{0,4},{1,5},{2,6},{3,7},{4,0},{5,1},{6,2},{7,3},{8,12},{9,13},{10,... | collective-permute-start | bytes 589832 | tf_op jit(solution)/shard_map/ppermute | solution.py:573
  78.0 8.2 %collective-permute-start.20 = (bf16[192,512]{1,0:T(8,128)(2,1)S(1)}, bf16[192,512]{1,0:T(8,128)(2,1)S(1)}, u32[]{:S(2)}, u32[]{:S(2)}) collective-permute-start(bf16[192,512]{1,0:T(8,128)(2,1)S(1)} %get-tuple-element.112), channel_id=1, source_target_pairs={{0,2},{1,3},{2,0},{3,1},{4,6},{5,7},{6,4},{7,5},{8,10},{9,11},{10,... | collective-permute-start | bytes 589832 | tf_op jit(solution)/shard_map/ppermute | solution.py:573
  78.4 8.1 %collective-permute-start.21 = (bf16[192,512]{1,0:T(8,128)(2,1)S(1)}, bf16[192,512]{1,0:T(8,128)(2,1)S(1)}, u32[]{:S(2)}, u32[]{:S(2)}) collective-permute-start(bf16[192,512]{1,0:T(8,128)(2,1)S(1)} %get-tuple-element.113), channel_id=1, source_target_pairs={{0,6},{1,7},{2,4},{3,5},{4,2},{5,3},{6,0},{7,1},{8,14},{9,15},{10,... | collective-permute-start | bytes 589832 | tf_op jit(solution)/shard_map/ppermute | solution.py:573
  (5 other events, 9.3 us)

commit v6 on v5

--- a/solution.py
+++ b/solution.py
@@ -78,15 +78,25 @@
     return block_times(0, shape), block_times(1, shape)
 
 
+def within(later, earlier, level):
+    later_half, earlier_half = later >> level, earlier >> level
+    return ((later_half >> 1) == (earlier_half >> 1)) & (later_half > earlier_half)
+
+
 def solver_levels():
-    later, earlier = key_order()
-    levels = []
-    for level in range((2 * SPAN).bit_length() - 1):
-        later_half, earlier_half = later >> level, earlier >> level
-        levels.append(
-            ((later_half >> 1) == (earlier_half >> 1)) & (later_half > earlier_half)
-        )
-    return levels
+    return [within(*key_order(), level) for level in range((2 * SPAN).bit_length() - 1)]
+
+
+def odd_rows(value, chunk):
+    starts = range(chunk, value.shape[0], 2 * chunk)
+    return jnp.concatenate([value[start : start + chunk] for start in starts], axis=0)
+
+
+def set_odd_rows(value, chunk, rows):
+    pieces = []
+    for start in range(0, rows.shape[0], chunk):
+        pieces += [value[2 * start : 2 * start + chunk], rows[start : start + chunk]]
+    return jnp.concatenate(pieces, axis=0)
 
 
 def seen(axis):
@@ -113,10 +123,32 @@
     lower = [halves(crossings[i]) for i in each]
     one = jnp.where(later == earlier, 1.0, 0.0)
     solver = [one - jnp.where(levels[0], crossings[i], 0.0) for i in each]
-    for level in levels[1:]:
+    for size, level in enumerate(levels[1:], 1):
         parts = [halves(solver[i]) for i in each]
-        step = [fine(lower[i], parts[i]) for i in each]
-        solver = [solver[i] - jnp.where(level, fine(parts[i], step[i]), 0.0) for i in each]
+        chunk = 2**size // 2
+        if chunk < 16:
+            step = [fine(lower[i], parts[i]) for i in each]
+            solver = [solver[i] - jnp.where(level, fine(parts[i], step[i]), 0.0) for i in each]
+            continue
+        changes = within(odd_rows(later, chunk), odd_rows(earlier, chunk), size)
+        step = [
+            halves(fine(tuple(odd_rows(part, chunk) for part in lower[i]), parts[i])) for i in each
+        ]
+        step = [
+            tuple(set_odd_rows(jnp.zeros_like(part), chunk, rows) for part, rows in zip(parts[i], step[i]))
+            for i in each
+        ]
+        change = [
+            fine(tuple(odd_rows(part, chunk) for part in parts[i]), step[i]) for i in each
+        ]
+        solver = [
+            set_odd_rows(
+                solver[i],
+                chunk,
+                odd_rows(solver[i], chunk) - jnp.where(changes, change[i], 0.0),
+            )
+            for i in each
+        ]
     turned = [halves(jnp.swapaxes(solver[i], 0, 1)) for i in each]
     targets = [
         jnp.concatenate([rates[i] * keys[i], rates[i] * values[i].astype(F32)], axis=1)
@@ -347,7 +379,11 @@
     for mask, ref in enumerate(arrived):
         for part, matrix in enumerate(unpack(ref, 1, 3)):
             spans[place ^ mask, part] = matrix
-    found = chained(*[[spans[i, part] for i in range(len(arrived))] for part in range(3)])
+    pairs = [
+        chained(*[[spans[i, part], spans[i + 1, part]] for part in range(3)])
+        for i in range(0, len(arrived), 2)
+    ]
+    found = chained(*[list(both) for both in zip(*pairs)])
     for part in range(3):
         total[part] = found[part]
     pack(packed, 1, found)
@@ -475,12 +511,14 @@
     return shape_of(count * width + TAIL, width)
 
 
-def call(kernel, name, out_shape, *operands, scratch=(), specs=None, limit=VMEM_BYTES, cost=None):
+def call(
+    kernel, name, out_shape, *operands, scratch=(), specs=None, outs=VMEM, limit=VMEM_BYTES, cost=None
+):
     single = isinstance(out_shape, jax.ShapeDtypeStruct)
     return pl.pallas_call(
         kernel,
         in_specs=specs or [VMEM] * len(operands),
-        out_specs=VMEM if single else [VMEM] * len(out_shape),
+        out_specs=outs if single else [outs] * len(out_shape),
         out_shape=out_shape,
         scratch_shapes=list(scratch),
         compiler_params=pltpu.CompilerParams(vmem_limit_bytes=limit),
@@ -501,6 +539,17 @@
         cost=pl.CostEstimate(
             flops=0, bytes_accessed=2 * sum(array.nbytes for array in arrays), transcendentals=0
         ),
+    )
+
+
+def store(*arrays):
+    return call(
+        fetch_kernel,
+        "store",
+        [shape_of(*array.shape, dtype=array.dtype) for array in arrays],
+        *arrays,
+        scratch=[pltpu.SemaphoreType.DMA((len(arrays),))],
+        outs=pl.BlockSpec(memory_space=pltpu.HBM),
     )
 
 
@@ -632,10 +681,14 @@
             away[chip] = swapped(share, "head", 1)
     for chips in ((2,), (1, 3), (0,)):
         dtype = BF16 if chips[0] else F32
+        if not chips[0]:
+            stored, operands = lax.optimization_barrier(
+                (store(mixed, query_grad, value_grad), operands)
+            )
         found = shares(0, chips, *operands, dtype, *[away[chip] for chip in chips])
         for chip, share in zip(chips, found):
             total = total + (swapped(share, "head", 2 * chip).astype(F32) if chip else share)
-    return mixed, query_grad, value_grad, total.astype(BF16)
+    return *stored, total.astype(BF16)
 
 
 def solution(mesh):

time: 87.5 us -> 87.2 us (level)
    ppermute x23, waiting for transfers between devices: 17.3 us -> 16.5 us  [swapped(): lax.ppermute(value, axis, [(i, i ^ mask) for i in range(lax.axis_size(axi...]
    pallas_call x14 -> x15, Pallas kernels: 28.6 us -> 29.2 us  [call(): pl.pallas_call(kernel, in_specs=specs or [VMEM] * len(operands), out_spec...]
  transfers between devices with their start and end apart: 23 -> 23, of which waited for: 11 -> 11; matrix products, arithmetic and copies ran while one was open for 0% -> 0% of each run, Pallas kernels for 13% -> 14%
where the time goes in v6:
time: 87.2 us; the launch traced here: 87 us
  starting transfers between devices  35.6 us (41%)
  Pallas kernels  29.2 us (33%)
  waiting for transfers between devices  16.5 us (19%)
  local copies, waits for them, and re-layouts  3.69 us (4%)
  other arithmetic  1.03 us (1%)
  between operations  0.93 us (1%)
    ppermute x23, starting transfers between devices, swapped(): lax.ppermute(value, axis, [(i, i ^ mask) for i in range(lax.axis_size(axi...  35.6 us
    pallas_call x15, Pallas kernels, call(): pl.pallas_call(kernel, in_specs=specs or [VMEM] * len(operands), out_spec...  29.2 us
    ppermute x23, waiting for transfers between devices, swapped(): lax.ppermute(value, axis, [(i, i ^ mask) for i in range(lax.axis_size(axi...  16.5 us
    unnamed x12, local copies, waits for them, and re-layouts  3.69 us
  transfers between devices with their start and end apart: 23, of which 11 were waited for; matrix products, arithmetic and copies ran while one was open for 0% of the time, Pallas kernels for 14%

profile of v6, /device:TPU:1, one launch (start us, length us, event | category | flops | bytes accessed | tf_op | source)
XLA Modules:
  0.0 87.0 jit_solution(2665003350144293011)
XLA Ops:
  0.6 3.7 %collective-permute-start.1 = (bf16[192,512]{1,0:T(8,128)(2,1)}, bf16[192,512]{1,0:T(8,128)(2,1)S(1)}, u32[]{:S(2)}, u32[]{:S(2)}) collective-permute-start(bf16[192,512]{1,0:T(8,128)(2,1)} %refs_0_.5), channel_id=1, source_target_pairs={{0,4},{1,5},{2,6},{3,7},{4,0},{5,1},{6,2},{7,3},{8,12},{9,13},{10,... | collective-permute-start | bytes 589832 | tf_op jit(solution)/shard_map/ppermute | solution.py:622
  5.2 2.9 %collective-permute-start = (bf16[192,512]{1,0:T(8,128)(2,1)}, bf16[192,512]{1,0:T(8,128)(2,1)S(1)}, u32[]{:S(2)}, u32[]{:S(2)}) collective-permute-start(bf16[192,512]{1,0:T(8,128)(2,1)} %refs_0_.5), channel_id=1, source_target_pairs={{0,1},{1,0},{2,3},{3,2},{4,5},{5,4},{6,7},{7,6},{8,9},{9,8},{10,11... | collective-permute-start | bytes 589832 | tf_op jit(solution)/shard_map/ppermute | solution.py:622
  8.1 1.0 %copy-done.1 = bf16[192,1024]{1,0:T(8,128)(2,1)S(1)} copy-done((bf16[192,1024]{1,0:T(8,128)(2,1)S(1)}, bf16[192,1024]{1,0:T(8,128)(2,1)}, u32[]{:S(2)}) %copy-start.1) | copy-done | bytes 393240
  9.1 0.9 %copy-done.2 = bf16[192,512]{1,0:T(8,128)(2,1)S(1)} copy-done((bf16[192,512]{1,0:T(8,128)(2,1)S(1)}, bf16[192,512]{1,0:T(8,128)(2,1)}, u32[]{:S(2)}) %copy-start.2) | copy-done | bytes 196632
  10.0 0.9 %copy-done.3 = bf16[192,512]{1,0:T(8,128)(2,1)S(1)} copy-done((bf16[192,512]{1,0:T(8,128)(2,1)S(1)}, bf16[192,512]{1,0:T(8,128)(2,1)}, u32[]{:S(2)}) %copy-start.3) | copy-done | bytes 196632
  11.8 3.5 %fetch.1 = (bf16[4096,1024]{1,0:T(8,128)(2,1)S(1)}, bf16[8,4096]{1,0:T(8,128)(2,1)S(1)}, bf16[192,512]{1,0:T(8,128)(2,1)S(1)}, bf16[192,1024]{1,0:T(8,128)(2,1)S(1)}, bf16[192,512]{1,0:T(8,128)(2,1)S(1)}) custom-call(bf16[4096,1024]{1,0:T(8,128)(2,1)} %refs_0_.3, bf16[8,4096]{1,0:T(8,128)(2,1)S(1)} %bitcast.2, bf16[192,512]{1,0:T(8,128)(2,1)S(1)} %copy-done.2, ...), custom_call_target="tpu_custom_call" | custom-call | bytes 18481152 | tf_op jit(solution)/shard_map/fetch/pallas_call | solution.py:518
  17.4 8.5 %project.2 = (f32[192,768]{1,0:T(8,128)S(1)}, f32[192,8]{1,0:T(8,128)S(1)}, f32[3,3,128,256]{3,2,1,0:T(8,128)S(1)}, f32[3,3,128,256]{3,2,1,0:T(8,128)S(1)}, f32[...) custom-call(bf16[192,512]{1,0:T(8,128)(2,1)S(1)} %copy-done, ...), custom_call_target="tpu_custom_call" | custom-call | tf_op jit(solution)/shard_map/project/pallas_call | solution.py:518
  25.9 2.1 %collective-permute-start.9 = (f16[400,128]{1,0:T(8,128)(2,1)S(1)}, f16[400,128]{1,0:T(8,128)(2,1)S(1)}, u32[]{:S(2)}, u32[]{:S(2)}) collective-permute-start(f16[400,128]{1,0:T(8,128)(2,1)S(1)} %convert_element_type.70), channel_id=1, source_target_pairs={{0,24},{8,16},{16,8},{24,0},{32,56},{40,48},{48,40},{56,32},{64,88... | collective-permute-start | bytes 307208 | tf_op jit(solution)/shard_map/ppermute | solution.py:622
  29.4 5.0 %project.3 = (f32[192,256]{1,0:T(8,128)S(1)}, f32[192,8]{1,0:T(8,128)S(1)}, f32[1,3,128,256]{3,2,1,0:T(8,128)S(1)}, f32[1,3,128,256]{3,2,1,0:T(8,128)S(1)}, f32[...) custom-call(bf16[192,512]{1,0:T(8,128)(2,1)S(1)} %copy-done, bf16[192,512]{1,0:T(8,128)(2,1)S(1)} %collective-permute-done.refs_1_, ...), custom_call_target="tpu_custom_call" | custom-call | tf_op jit(solution)/shard_map/project/pallas_call | solution.py:518
  35.2 1.3 %collective-permute-start.10 = (f16[400,128]{1,0:T(8,128)(2,1)S(1)}, f16[400,128]{1,0:T(8,128)(2,1)S(1)}, u32[]{:S(2)}, u32[]{:S(2)}) collective-permute-start(f16[400,128]{1,0:T(8,128)(2,1)S(1)} %convert_element_type.72), channel_id=1, source_target_pairs={{0,32},{8,40},{16,48},{24,56},{32,0},{40,8},{48,16},{56,24},{64,96... | collective-permute-start | bytes 307208 | tf_op jit(solution)/shard_map/ppermute | solution.py:622
  36.5 2.3 %collective-permute-done.10 = f16[400,128]{1,0:T(8,128)(2,1)S(1)} collective-permute-done((f16[400,128]{1,0:T(8,128)(2,1)S(1)}, f16[400,128]{1,0:T(8,128)(2,1)S(1)}, u32[]{:S(2)}, u32[]{:S(2)}) %collective-permute-start.10) | collective-permute-done | bytes 102432 | tf_op jit(solution)/shard_map/ppermute | solution.py:622
  39.2 2.8 %collective-permute-start.11 = (f16[400,128]{1,0:T(8,128)(2,1)S(1)}, f16[400,128]{1,0:T(8,128)(2,1)S(1)}, u32[]{:S(2)}, u32[]{:S(2)}) collective-permute-start(f16[400,128]{1,0:T(8,128)(2,1)S(1)} %convert_element_type.74), channel_id=1, source_target_pairs={{0,64},{8,72},{16,80},{24,88},{32,96},{40,104},{48,112},{56,120},{... | collective-permute-start | bytes 307208 | tf_op jit(solution)/shard_map/ppermute | solution.py:622
  42.0 2.1 %collective-permute-done.11 = f16[400,128]{1,0:T(8,128)(2,1)S(1)} collective-permute-done((f16[400,128]{1,0:T(8,128)(2,1)S(1)}, f16[400,128]{1,0:T(8,128)(2,1)S(1)}, u32[]{:S(2)}, u32[]{:S(2)}) %collective-permute-start.11) | collective-permute-done | bytes 102432 | tf_op jit(solution)/shard_map/ppermute | solution.py:622
  44.4 6.0 %collective-permute-start.12 = (f16[144,128]{1,0:T(8,128)(2,1)S(1)}, f16[144,128]{1,0:T(8,128)(2,1)S(1)}, u32[]{:S(2)}, u32[]{:S(2)}) collective-permute-start(f16[144,128]{1,0:T(8,128)(2,1)S(1)} %convert_element_type.76), channel_id=1, source_target_pairs={{0,224},{8,232},{16,240},{24,248},{32,192},{40,200},{48,208},{56,2... | collective-permute-start | bytes 110600 | tf_op jit(solution)/shard_map/ppermute | solution.py:622
  50.4 1.6 %collective-permute-done.12 = f16[144,128]{1,0:T(8,128)(2,1)S(1)} collective-permute-done((f16[144,128]{1,0:T(8,128)(2,1)S(1)}, f16[144,128]{1,0:T(8,128)(2,1)S(1)}, u32[]{:S(2)}, u32[]{:S(2)}) %collective-permute-start.12) | collective-permute-done | bytes 36896 | tf_op jit(solution)/shard_map/ppermute | solution.py:622
  52.0 1.1 %scan.1 = (f32[272,128]{1,0:T(8,128)S(1)}, f32[272,128]{1,0:T(8,128)S(1)}, f32[272,128]{1,0:T(8,128)S(1)}, f32[272,128]{1,0:T(8,128)S(1)}) custom-call(f32[4,3,128,128]{3,2,1,0:T(8,128)S(1)} %get-tuple-element.102.spans, f32[400,128]{1,0:T(8,128)S(1)} %convert_element_type.73.other.near_group, f32[400,128]{1,0:T(8,128)S(1)} %convert_element_type.75.other.near_pair, ...), custom_call_target="tpu_custom_call" | custom-call | tf_op jit(solution)/shard_map/scan/pallas_call | solution.py:518
  53.2 2.2 %collective-permute-start.15 = (f16[272,128]{1,0:T(8,128)(2,1)S(1)}, f16[272,128]{1,0:T(8,128)(2,1)S(1)}, u32[]{:S(2)}, u32[]{:S(2)}) collective-permute-start(f16[272,128]{1,0:T(8,128)(2,1)S(1)} %convert_element_type.82), channel_id=1, source_target_pairs={{0,24},{8,16},{16,8},{24,0},{32,56},{40,48},{48,40},{56,32},{64,88... | collective-permute-start | bytes 208904 | tf_op jit(solution)/shard_map/ppermute | solution.py:622
  55.9 0.9 %collective-permute-start.13 = (f16[272,128]{1,0:T(8,128)(2,1)S(1)}, f16[272,128]{1,0:T(8,128)(2,1)S(1)}, u32[]{:S(2)}, u32[]{:S(2)}) collective-permute-start(f16[272,128]{1,0:T(8,128)(2,1)S(1)} %convert_element_type.78), channel_id=1, source_target_pairs={{0,8},{8,0},{16,24},{24,16},{32,40},{40,32},{48,56},{56,48},{64,72... | collective-permute-start | bytes 208904 | tf_op jit(solution)/shard_map/ppermute | solution.py:622
  57.6 2.4 %collective-permute-done.14 = f16[272,128]{1,0:T(8,128)(2,1)S(1)} collective-permute-done((f16[272,128]{1,0:T(8,128)(2,1)S(1)}, f16[272,128]{1,0:T(8,128)(2,1)S(1)}, u32[]{:S(2)}, u32[]{:S(2)}) %collective-permute-start.14) | collective-permute-done | bytes 69664 | tf_op jit(solution)/shard_map/ppermute | solution.py:622
  60.1 5.0 %outputs.1 = (bf16[192,512]{1,0:T(8,128)(2,1)S(1)}, bf16[192,512]{1,0:T(8,128)(2,1)S(1)}, bf16[192,1024]{1,0:T(8,128)(2,1)S(1)}, bf16[192,1024]{1,0:T(8,128)(2,1)S(1)}, bf16[192,8]{1,0:T(8,128)(2,1)S(1)}) custom-call(f32[192,8]{1,0:T(8,128)S(1)} %get-tuple-element.93.refs_0_, bf16[192,512]{1,0:T(8,128)(2,1)S(1)} %get-tuple-element.89.refs_11_.refs_1_, ...), custom_call_target="tpu_custom_call" | custom-call | tf_op jit(solution)/shard_map/outputs/pallas_call | solution.py:518
  66.6 5.8 %collective-permute-start.16 = (bf16[192,512]{1,0:T(8,128)(2,1)S(1)}, bf16[192,512]{1,0:T(8,128)(2,1)S(1)}, u32[]{:S(2)}, u32[]{:S(2)}) collective-permute-start(bf16[192,512]{1,0:T(8,128)(2,1)S(1)} %shares.6), channel_id=1, source_target_pairs={{0,1},{1,0},{2,3},{3,2},{4,5},{5,4},{6,7},{7,6},{8,9},{9,8},{10,11... | collective-permute-start | bytes 589832 | tf_op jit(solution)/shard_map/ppermute | solution.py:622
  74.1 2.7 %collective-permute-start.17 = (bf16[192,512]{1,0:T(8,128)(2,1)S(1)}, bf16[192,512]{1,0:T(8,128)(2,1)S(1)}, u32[]{:S(2)}, u32[]{:S(2)}) collective-permute-start(bf16[192,512]{1,0:T(8,128)(2,1)S(1)} %shares.7), channel_id=1, source_target_pairs={{0,4},{1,5},{2,6},{3,7},{4,0},{5,1},{6,2},{7,3},{8,12},{9,13},{10,... | collective-permute-start | bytes 589832 | tf_op jit(solution)/shard_map/ppermute | solution.py:622
  80.3 1.5 %collective-permute-done.17 = bf16[192,512]{1,0:T(8,128)(2,1)S(1)} collective-permute-done((bf16[192,512]{1,0:T(8,128)(2,1)S(1)}, bf16[192,512]{1,0:T(8,128)(2,1)S(1)}, u32[]{:S(2)}, u32[]{:S(2)}) %collective-permute-start.17) | collective-permute-done | bytes 196640 | tf_op jit(solution)/shard_map/ppermute | solution.py:622
  81.8 4.2 %collective-permute-done.20 = bf16[192,512]{1,0:T(8,128)(2,1)S(1)} collective-permute-done((bf16[192,512]{1,0:T(8,128)(2,1)S(1)}, bf16[192,512]{1,0:T(8,128)(2,1)S(1)}, u32[]{:S(2)}, u32[]{:S(2)}) %collective-permute-start.20) | collective-permute-done | bytes 196640 | tf_op jit(solution)/shard_map/ppermute | solution.py:622
  (68 shorter events, 15.7 us)
Async XLA Ops:
  0.6 14.6 %collective-permute-start.1 = (bf16[192,512]{1,0:T(8,128)(2,1)}, bf16[192,512]{1,0:T(8,128)(2,1)S(1)}, u32[]{:S(2)}, u32[]{:S(2)}) collective-permute-start(bf16[192,512]{1,0:T(8,128)(2,1)} %refs_0_.5), channel_id=1, source_target_pairs={{0,4},{1,5},{2,6},{3,7},{4,0},{5,1},{6,2},{7,3},{8,12},{9,13},{10,... | collective-permute-start | bytes 589832 | tf_op jit(solution)/shard_map/ppermute | solution.py:622
  4.3 10.9 %collective-permute-start.3 = (bf16[192,512]{1,0:T(8,128)(2,1)}, bf16[192,512]{1,0:T(8,128)(2,1)S(1)}, u32[]{:S(2)}, u32[]{:S(2)}) collective-permute-start(bf16[192,512]{1,0:T(8,128)(2,1)} %refs_0_.5), channel_id=1, source_target_pairs={{0,2},{1,3},{2,0},{3,1},{4,6},{5,7},{6,4},{7,5},{8,10},{9,11},{10,... | collective-permute-start | bytes 589832 | tf_op jit(solution)/shard_map/ppermute | solution.py:622
  4.6 10.6 %collective-permute-start.5 = (bf16[192,512]{1,0:T(8,128)(2,1)}, bf16[192,512]{1,0:T(8,128)(2,1)S(1)}, u32[]{:S(2)}, u32[]{:S(2)}) collective-permute-start(bf16[192,512]{1,0:T(8,128)(2,1)} %refs_0_.5), channel_id=1, source_target_pairs={{0,6},{1,7},{2,4},{3,5},{4,2},{5,3},{6,0},{7,1},{8,14},{9,15},{10,... | collective-permute-start | bytes 589832 | tf_op jit(solution)/shard_map/ppermute | solution.py:622
  5.2 10.8 %collective-permute-start = (bf16[192,512]{1,0:T(8,128)(2,1)}, bf16[192,512]{1,0:T(8,128)(2,1)S(1)}, u32[]{:S(2)}, u32[]{:S(2)}) collective-permute-start(bf16[192,512]{1,0:T(8,128)(2,1)} %refs_0_.5), channel_id=1, source_target_pairs={{0,1},{1,0},{2,3},{3,2},{4,5},{5,4},{6,7},{7,6},{8,9},{9,8},{10,11... | collective-permute-start | bytes 589832 | tf_op jit(solution)/shard_map/ppermute | solution.py:622
  11.7 5.6 %copy-start.5 = (f32[8]{0:T(128)S(1)}, f32[8]{0:T(128)}, u32[]{:S(2)}) copy-start(f32[8]{0:T(128)} %param.10) | copy-start | bytes 100
  15.3 1.5 %collective-permute-start.6 = (bf16[192,512]{1,0:T(8,128)(2,1)S(1)}, bf16[192,512]{1,0:T(8,128)(2,1)S(1)}, u32[]{:S(2)}, u32[]{:S(2)}) collective-permute-start(bf16[192,512]{1,0:T(8,128)(2,1)S(1)} %collective-permute-done.5.refs_6_), channel_id=1, source_target_pairs={{0,1},{1,0},{2,3},{3,2},{4,5},{5,4},{6,7},{7,6},{8,9},{9,8},{10,11... | collective-permute-start | bytes 589832 | tf_op jit(solution)/shard_map/ppermute | solution.py:622
  15.5 1.6 %collective-permute-start.4 = (bf16[192,512]{1,0:T(8,128)(2,1)S(1)}, bf16[192,512]{1,0:T(8,128)(2,1)S(1)}, u32[]{:S(2)}, u32[]{:S(2)}) collective-permute-start(bf16[192,512]{1,0:T(8,128)(2,1)S(1)} %collective-permute-done.3.refs_4_), channel_id=1, source_target_pairs={{0,1},{1,0},{2,3},{3,2},{4,5},{5,4},{6,7},{7,6},{8,9},{9,8},{10,11... | collective-permute-start | bytes 589832 | tf_op jit(solution)/shard_map/ppermute | solution.py:622
  15.9 1.5 %collective-permute-start.2 = (bf16[192,512]{1,0:T(8,128)(2,1)S(1)}, bf16[192,512]{1,0:T(8,128)(2,1)S(1)}, u32[]{:S(2)}, u32[]{:S(2)}) collective-permute-start(bf16[192,512]{1,0:T(8,128)(2,1)S(1)} %collective-permute-done.1.refs_2_), channel_id=1, source_target_pairs={{0,1},{1,0},{2,3},{3,2},{4,5},{5,4},{6,7},{7,6},{8,9},{9,8},{10,11... | collective-permute-start | bytes 589832 | tf_op jit(solution)/shard_map/ppermute | solution.py:622
  25.9 8.5 %collective-permute-start.9 = (f16[400,128]{1,0:T(8,128)(2,1)S(1)}, f16[400,128]{1,0:T(8,128)(2,1)S(1)}, u32[]{:S(2)}, u32[]{:S(2)}) collective-permute-start(f16[400,128]{1,0:T(8,128)(2,1)S(1)} %convert_element_type.70), channel_id=1, source_target_pairs={{0,24},{8,16},{16,8},{24,0},{32,56},{40,48},{48,40},{56,32},{64,88... | collective-permute-start | bytes 307208 | tf_op jit(solution)/shard_map/ppermute | solution.py:622
  28.0 6.5 %collective-permute-start.8 = (f16[400,128]{1,0:T(8,128)(2,1)S(1)}, f16[400,128]{1,0:T(8,128)(2,1)S(1)}, u32[]{:S(2)}, u32[]{:S(2)}) collective-permute-start(f16[400,128]{1,0:T(8,128)(2,1)S(1)} %convert_element_type.68), channel_id=1, source_target_pairs={{0,16},{8,24},{16,0},{24,8},{32,48},{40,56},{48,32},{56,40},{64,80... | collective-permute-start | bytes 307208 | tf_op jit(solution)/shard_map/ppermute | solution.py:622
  28.5 6.0 %collective-permute-start.7 = (f16[400,128]{1,0:T(8,128)(2,1)S(1)}, f16[400,128]{1,0:T(8,128)(2,1)S(1)}, u32[]{:S(2)}, u32[]{:S(2)}) collective-permute-start(f16[400,128]{1,0:T(8,128)(2,1)S(1)} %convert_element_type.66), channel_id=1, source_target_pairs={{0,8},{8,0},{16,24},{24,16},{32,40},{40,32},{48,56},{56,48},{64,72... | collective-permute-start | bytes 307208 | tf_op jit(solution)/shard_map/ppermute | solution.py:622
  35.2 3.6 %collective-permute-start.10 = (f16[400,128]{1,0:T(8,128)(2,1)S(1)}, f16[400,128]{1,0:T(8,128)(2,1)S(1)}, u32[]{:S(2)}, u32[]{:S(2)}) collective-permute-start(f16[400,128]{1,0:T(8,128)(2,1)S(1)} %convert_element_type.72), channel_id=1, source_target_pairs={{0,32},{8,40},{16,48},{24,56},{32,0},{40,8},{48,16},{56,24},{64,96... | collective-permute-start | bytes 307208 | tf_op jit(solution)/shard_map/ppermute | solution.py:622
  39.2 4.9 %collective-permute-start.11 = (f16[400,128]{1,0:T(8,128)(2,1)S(1)}, f16[400,128]{1,0:T(8,128)(2,1)S(1)}, u32[]{:S(2)}, u32[]{:S(2)}) collective-permute-start(f16[400,128]{1,0:T(8,128)(2,1)S(1)} %convert_element_type.74), channel_id=1, source_target_pairs={{0,64},{8,72},{16,80},{24,88},{32,96},{40,104},{48,112},{56,120},{... | collective-permute-start | bytes 307208 | tf_op jit(solution)/shard_map/ppermute | solution.py:622
  44.4 7.6 %collective-permute-start.12 = (f16[144,128]{1,0:T(8,128)(2,1)S(1)}, f16[144,128]{1,0:T(8,128)(2,1)S(1)}, u32[]{:S(2)}, u32[]{:S(2)}) collective-permute-start(f16[144,128]{1,0:T(8,128)(2,1)S(1)} %convert_element_type.76), channel_id=1, source_target_pairs={{0,224},{8,232},{16,240},{24,248},{32,192},{40,200},{48,208},{56,2... | collective-permute-start | bytes 110600 | tf_op jit(solution)/shard_map/ppermute | solution.py:622
  53.2 4.5 %collective-permute-start.15 = (f16[272,128]{1,0:T(8,128)(2,1)S(1)}, f16[272,128]{1,0:T(8,128)(2,1)S(1)}, u32[]{:S(2)}, u32[]{:S(2)}) collective-permute-start(f16[272,128]{1,0:T(8,128)(2,1)S(1)} %convert_element_type.82), channel_id=1, source_target_pairs={{0,24},{8,16},{16,8},{24,0},{32,56},{40,48},{48,40},{56,32},{64,88... | collective-permute-start | bytes 208904 | tf_op jit(solution)/shard_map/ppermute | solution.py:622
  55.4 4.7 %collective-permute-start.14 = (f16[272,128]{1,0:T(8,128)(2,1)S(1)}, f16[272,128]{1,0:T(8,128)(2,1)S(1)}, u32[]{:S(2)}, u32[]{:S(2)}) collective-permute-start(f16[272,128]{1,0:T(8,128)(2,1)S(1)} %convert_element_type.80), channel_id=1, source_target_pairs={{0,16},{8,24},{16,0},{24,8},{32,48},{40,56},{48,32},{56,40},{64,80... | collective-permute-start | bytes 208904 | tf_op jit(solution)/shard_map/ppermute | solution.py:622
  55.9 4.2 %collective-permute-start.13 = (f16[272,128]{1,0:T(8,128)(2,1)S(1)}, f16[272,128]{1,0:T(8,128)(2,1)S(1)}, u32[]{:S(2)}, u32[]{:S(2)}) collective-permute-start(f16[272,128]{1,0:T(8,128)(2,1)S(1)} %convert_element_type.78), channel_id=1, source_target_pairs={{0,8},{8,0},{16,24},{24,16},{32,40},{40,32},{48,56},{56,48},{64,72... | collective-permute-start | bytes 208904 | tf_op jit(solution)/shard_map/ppermute | solution.py:622
  66.6 7.0 %collective-permute-start.16 = (bf16[192,512]{1,0:T(8,128)(2,1)S(1)}, bf16[192,512]{1,0:T(8,128)(2,1)S(1)}, u32[]{:S(2)}, u32[]{:S(2)}) collective-permute-start(bf16[192,512]{1,0:T(8,128)(2,1)S(1)} %shares.6), channel_id=1, source_target_pairs={{0,1},{1,0},{2,3},{3,2},{4,5},{5,4},{6,7},{7,6},{8,9},{9,8},{10,11... | collective-permute-start | bytes 589832 | tf_op jit(solution)/shard_map/ppermute | solution.py:622
  72.4 4.4 %collective-permute-start.18 = (bf16[192,512]{1,0:T(8,128)(2,1)S(1)}, bf16[192,512]{1,0:T(8,128)(2,1)S(1)}, u32[]{:S(2)}, u32[]{:S(2)}) collective-permute-start(bf16[192,512]{1,0:T(8,128)(2,1)S(1)} %get-tuple-element.126), channel_id=1, source_target_pairs={{0,1},{1,0},{2,3},{3,2},{4,5},{5,4},{6,7},{7,6},{8,9},{9,8},{10,11... | collective-permute-start | bytes 589832 | tf_op jit(solution)/shard_map/ppermute | solution.py:622
  72.5 4.3 %collective-permute-start.19 = (bf16[192,512]{1,0:T(8,128)(2,1)S(1)}, bf16[192,512]{1,0:T(8,128)(2,1)S(1)}, u32[]{:S(2)}, u32[]{:S(2)}) collective-permute-start(bf16[192,512]{1,0:T(8,128)(2,1)S(1)} %get-tuple-element.127), channel_id=1, source_target_pairs={{0,1},{1,0},{2,3},{3,2},{4,5},{5,4},{6,7},{7,6},{8,9},{9,8},{10,11... | collective-permute-start | bytes 589832 | tf_op jit(solution)/shard_map/ppermute | solution.py:622
  73.4 6.4 %collective-permute-start.22 = (bf16[192,512]{1,0:T(8,128)(2,1)S(1)}, bf16[192,512]{1,0:T(8,128)(2,1)S(1)}, u32[]{:S(2)}, u32[]{:S(2)}) collective-permute-start(bf16[192,512]{1,0:T(8,128)(2,1)S(1)} %shares.10), channel_id=1, source_target_pairs={{0,1},{1,0},{2,3},{3,2},{4,5},{5,4},{6,7},{7,6},{8,9},{9,8},{10,11... | collective-permute-start | bytes 589832 | tf_op jit(solution)/shard_map/ppermute | solution.py:622
  74.1 7.7 %collective-permute-start.17 = (bf16[192,512]{1,0:T(8,128)(2,1)S(1)}, bf16[192,512]{1,0:T(8,128)(2,1)S(1)}, u32[]{:S(2)}, u32[]{:S(2)}) collective-permute-start(bf16[192,512]{1,0:T(8,128)(2,1)S(1)} %shares.7), channel_id=1, source_target_pairs={{0,4},{1,5},{2,6},{3,7},{4,0},{5,1},{6,2},{7,3},{8,12},{9,13},{10,... | collective-permute-start | bytes 589832 | tf_op jit(solution)/shard_map/ppermute | solution.py:622
  77.7 8.2 %collective-permute-start.20 = (bf16[192,512]{1,0:T(8,128)(2,1)S(1)}, bf16[192,512]{1,0:T(8,128)(2,1)S(1)}, u32[]{:S(2)}, u32[]{:S(2)}) collective-permute-start(bf16[192,512]{1,0:T(8,128)(2,1)S(1)} %get-tuple-element.128), channel_id=1, source_target_pairs={{0,2},{1,3},{2,0},{3,1},{4,6},{5,7},{6,4},{7,5},{8,10},{9,11},{10,... | collective-permute-start | bytes 589832 | tf_op jit(solution)/shard_map/ppermute | solution.py:622
  78.1 8.1 %collective-permute-start.21 = (bf16[192,512]{1,0:T(8,128)(2,1)S(1)}, bf16[192,512]{1,0:T(8,128)(2,1)S(1)}, u32[]{:S(2)}, u32[]{:S(2)}) collective-permute-start(bf16[192,512]{1,0:T(8,128)(2,1)S(1)} %get-tuple-element.129), channel_id=1, source_target_pairs={{0,6},{1,7},{2,4},{3,5},{4,2},{5,3},{6,0},{7,1},{8,14},{9,15},{10,... | collective-permute-start | bytes 589832 | tf_op jit(solution)/shard_map/ppermute | solution.py:622
  (5 other events, 9.3 us)
